TPU v7x, 32 devices: a whole 2x2x4 slice. The times are simulated.
32 devices in a mesh: dp: 4 (over y, x), fsdp: 8 (over z, core).
Axes of the slice: x: 2, y: 2, z: 4, core: 2. Of those that a mesh axis runs over, the one named last changes fastest.
Arguments:
- source: bfloat16 [4096, 1024], P(('dp', 'fsdp')), may hold values from -6 to 6
- dec_in: bfloat16 [4096, 3, 1024], P(('dp', 'fsdp')), may hold values from -6 to 6
- src_lengths: int32 [32], P(('dp', 'fsdp')), may hold values from 65 to 128, as said below
- tgt_lengths: int32 [32], P(('dp', 'fsdp')), may hold values from 65 to 128, as said below
- enc_in_proj: bfloat16 [1024, 3072], P(('dp', 'fsdp')), may hold values from -0.1875 to 0.1875
- enc_out_proj: bfloat16 [1024, 1024], P(('dp', 'fsdp')), may hold values from -1.5 to 1.5
- enc_ffn_in: bfloat16 [1024, 4096], P(('dp', 'fsdp')), may hold values from -0.1875 to 0.1875
- enc_ffn_out: bfloat16 [4096, 1024], P(('dp', 'fsdp')), may hold values from -0.1875 to 0.1875
- enc_gains: bfloat16 [2048], P(('dp', 'fsdp')), may hold values from 0.5 to 1.5
- enc_biases: bfloat16 [10240], P(('dp', 'fsdp')), may hold values from -1.1953125 to 1.1953125
- dec_in_proj: bfloat16 [1024, 3072], P(('dp', 'fsdp')), may hold values from -0.1875 to 0.1875
- dec_rel_proj: bfloat16 [1024, 512], P(('dp', 'fsdp')), may hold values from -0.1875 to 0.1875
- dec_out_proj: bfloat16 [1024, 1024], P(('dp', 'fsdp')), may hold values from -1.5 to 1.5
- cross_query: bfloat16 [1024, 1024], P(('dp', 'fsdp')), may hold values from -0.1875 to 0.1875
- cross_kv: bfloat16 [1024, 2048], P(('dp', 'fsdp')), may hold values from -0.1875 to 0.1875
- cross_out: bfloat16 [1024, 1024], P(('dp', 'fsdp')), may hold values from -1.5 to 1.5
- dec_ffn_in: bfloat16 [1024, 4096], P(('dp', 'fsdp')), may hold values from -0.1875 to 0.1875
- dec_ffn_out: bfloat16 [4096, 1024], P(('dp', 'fsdp')), may hold values from -0.1875 to 0.1875
- dec_gains: bfloat16 [3072], P(('dp', 'fsdp')), may hold values from 0.5 to 1.5
- dec_biases: bfloat16 [14848], P(('dp', 'fsdp')), may hold values from -1.1953125 to 1.1953125
- enc_cot: bfloat16 [4096, 1024], P(('dp', 'fsdp')), may hold values from -6 to 6
- dec_cot: bfloat16 [4096, 3, 1024], P(('dp', 'fsdp')), may hold values from -6 to 6
Outputs:
- enc_out: bfloat16 [4096, 1024], P(('dp', 'fsdp'))
- dec_out: bfloat16 [4096, 3, 1024], P(('dp', 'fsdp'))
- source_grad: float32 [4096, 1024], P(('dp', 'fsdp'))
- dec_in_grad: float32 [4096, 3, 1024], P(('dp', 'fsdp'))
- grad_enc_in_proj: float32 [1024, 3072], P(('dp', 'fsdp'))
- grad_enc_out_proj: float32 [1024, 1024], P(('dp', 'fsdp'))
- grad_enc_ffn_in: float32 [1024, 4096], P(('dp', 'fsdp'))
- grad_enc_ffn_out: float32 [4096, 1024], P(('dp', 'fsdp'))
- grad_enc_gains: float32 [2048], P(('dp', 'fsdp'))
- grad_enc_biases: float32 [10240], P(('dp', 'fsdp'))
- grad_dec_in_proj: float32 [1024, 3072], P(('dp', 'fsdp'))
- grad_dec_rel_proj: float32 [1024, 512], P(('dp', 'fsdp'))
- grad_dec_out_proj: float32 [1024, 1024], P(('dp', 'fsdp'))
- grad_cross_query: float32 [1024, 1024], P(('dp', 'fsdp'))
- grad_cross_kv: float32 [1024, 2048], P(('dp', 'fsdp'))
- grad_cross_out: float32 [1024, 1024], P(('dp', 'fsdp'))
- grad_dec_ffn_in: float32 [1024, 4096], P(('dp', 'fsdp'))
- grad_dec_ffn_out: float32 [4096, 1024], P(('dp', 'fsdp'))
- grad_dec_gains: float32 [3072], P(('dp', 'fsdp'))
- grad_dec_biases: float32 [14848], P(('dp', 'fsdp'))
Inputs may be any that keep to these rules, and one draw needn't show every extreme that they name: `src_lengths`: every draw has a source sequence of exactly 128 tokens. `tgt_lengths`: every draw has a target sequence of exactly 128 tokens.
All inputs are finite; a program needn't handle non-finite values.
Results may differ from a plain program's by a relative error of at most 0.025.
Values may be sent and summed in bfloat16 or wider, within the bound.
No kernel may reach another device: no remote copies, remote signals or barrier semaphores. Data moves between devices by JAX's collectives and lax.ppermute only.
A program may use at most 320 MiB of HBM per device.

v0:
```python
import math

import jax
import jax.numpy as jnp
from jax import lax
from jax.sharding import PartitionSpec as P

D = 1024
HEADS = 16
HEAD = 64
FF = 4096
NGRAM = 2
BUCKETS = 32
LEN = 128


norm_epsilon = 1e-05
masked_score = -1000000000.0


def bucket_value(distance, bucket_count):
    exact_count = bucket_count // 2
    if distance < exact_count:
        return distance
    return min(
        bucket_count - 1,
        exact_count
        + int(
            math.log(distance / exact_count)
            / math.log(128 / exact_count)
            * (bucket_count - exact_count)
        ),
    )


def bucket_table(length, bucket_count):
    positions = jnp.arange(length, dtype=jnp.int32)
    distance = positions[:, None] - positions[None, :]
    bucket = jnp.zeros((length, length), jnp.int32)
    for target in range(1, bucket_count):
        distance_at = 1
        while bucket_value(distance_at, bucket_count) < target:
            distance_at += 1
        bucket = bucket + (distance >= distance_at).astype(jnp.int32)
    return (bucket[:, :, None] == jnp.arange(bucket_count, dtype=jnp.int32)).astype(jnp.float32)


def slices_of(vector, widths):
    starts = 0
    result = []
    for amount in widths:
        result.append(vector[starts : starts + amount])
        starts += amount
    return result


def layer_norm(values, gain_vector, shift_vector):
    average = jnp.mean(values, axis=-1, keepdims=True)
    centered = values - average
    variance = jnp.mean(centered * centered, axis=-1, keepdims=True)
    return centered * lax.rsqrt(variance + norm_epsilon) * gain_vector + shift_vector


def norm_back(values, gain_vector, shift_vector, gradients):
    outputs, pullback = jax.vjp(layer_norm, values, gain_vector, shift_vector)
    return pullback(gradients)


def gelu_exact(inputs):
    return jax.nn.gelu(inputs, approximate=False)


def gelu_back(inputs, gradients):
    outputs, pullback = jax.vjp(gelu_exact, inputs)
    return pullback(gradients)[0]


def score_scale():
    return 1.0 / math.sqrt(HEAD)


def project(inputs, matrix):
    return jnp.einsum("...d,de->...e", inputs, matrix, preferred_element_type=jnp.float32)


def project_back(gradients, matrix):
    return jnp.einsum("...e,de->...d", gradients, matrix, preferred_element_type=jnp.float32)


def weight_grad(inputs, gradients):
    return jnp.einsum(
        "rd,re->de",
        inputs.reshape(-1, inputs.shape[-1]),
        gradients.reshape(-1, gradients.shape[-1]),
        preferred_element_type=jnp.float32,
    )


def row_sum(gradients):
    return jnp.sum(gradients.reshape(-1, gradients.shape[-1]).astype(jnp.float32), axis=0)


def score_of(queries, key_part):
    return (
        jnp.einsum("ihe,jhe->hij", queries, key_part, preferred_element_type=jnp.float32)
        * score_scale()
    )


def stream_bias(relative, onehot):
    return jnp.einsum("ihk,ijk->hij", relative, onehot, precision=lax.Precision.HIGHEST)


def bucket_grad(score_grads, onehot_low):
    return jnp.einsum("hij,ijk->ihk", score_grads, onehot_low, preferred_element_type=jnp.float32)


def attention_forward(queries, key_part, value_part, score_bias, allowed):
    scores = jnp.where(allowed, score_of(queries, key_part) + score_bias, masked_score)
    logsum = jax.nn.logsumexp(scores, axis=-1, keepdims=True)
    probabilities = jnp.exp(scores - logsum).astype(jnp.bfloat16)
    return (
        jnp.einsum("hij,jhe->ihe", probabilities, value_part, preferred_element_type=jnp.float32),
        logsum,
    )


def attention_back(queries, key_part, value_part, score_bias, allowed, logsum, grad_out):
    scores = jnp.where(allowed, score_of(queries, key_part) + score_bias, masked_score)
    exact_probs = jnp.exp(scores - logsum)
    probabilities = exact_probs.astype(jnp.bfloat16)
    grad_probs = jnp.einsum(
        "ihe,jhe->hij", grad_out, value_part, preferred_element_type=jnp.float32
    )
    grad_values = jnp.einsum(
        "hij,ihe->jhe", probabilities, grad_out, preferred_element_type=jnp.float32
    )
    grad_scores = (
        exact_probs * (grad_probs - jnp.sum(exact_probs * grad_probs, axis=-1, keepdims=True))
    ).astype(jnp.bfloat16)
    grad_queries = (
        jnp.einsum("hij,jhe->ihe", grad_scores, key_part, preferred_element_type=jnp.float32)
        * score_scale()
    )
    grad_keys = (
        jnp.einsum("hij,ihe->jhe", grad_scores, queries, preferred_element_type=jnp.float32)
        * score_scale()
    )
    return (grad_queries, grad_keys, grad_values, grad_scores)


def predict_scores(projected, relative, onehot, pred_valid, stream):
    queries = projected[:, stream, 0]
    main_part = jnp.where(
        pred_valid,
        score_of(queries, projected[:, 0, 1]) + stream_bias(relative[:, stream], onehot),
        masked_score,
    )
    own_part = jnp.einsum(
        "ihe,ihe->hi", queries, projected[:, stream, 1], preferred_element_type=jnp.float32
    ) * score_scale() + jnp.transpose(relative[:, stream, :, 0])
    return jnp.concatenate([main_part, own_part[:, :, None]], axis=-1)


def predict_values(probabilities, value_main, value_own):
    main_values = jnp.einsum(
        "hij,jhe->ihe", probabilities[:, :, :LEN], value_main, preferred_element_type=jnp.float32
    )
    return main_values + jnp.transpose(probabilities[:, :, LEN]).astype(jnp.float32)[
        :, :, None
    ] * value_own.astype(jnp.float32)


def predict_back(projected, relative, onehot, pred_valid, stream, logsum, grad_out):
    queries = projected[:, stream, 0]
    key_main = projected[:, 0, 1]
    value_main = projected[:, 0, 2]
    key_own = projected[:, stream, 1]
    value_own = projected[:, stream, 2]
    scores = predict_scores(projected, relative, onehot, pred_valid, stream)
    exact_probs = jnp.exp(scores - logsum)
    probabilities = exact_probs.astype(jnp.bfloat16)
    grad_main = jnp.einsum("ihe,jhe->hij", grad_out, value_main, preferred_element_type=jnp.float32)
    grad_own = jnp.einsum("ihe,ihe->hi", grad_out, value_own, preferred_element_type=jnp.float32)
    grad_probs = jnp.concatenate([grad_main, grad_own[:, :, None]], axis=-1)
    grad_scores = (
        exact_probs * (grad_probs - jnp.sum(exact_probs * grad_probs, axis=-1, keepdims=True))
    ).astype(jnp.bfloat16)
    main_grad = grad_scores[:, :, :LEN]
    own_grad = grad_scores[:, :, LEN]
    own_rows = jnp.transpose(own_grad).astype(jnp.float32)[:, :, None]
    grad_queries = (
        jnp.einsum("hij,jhe->ihe", main_grad, key_main, preferred_element_type=jnp.float32)
        + own_rows * key_own.astype(jnp.float32)
    ) * score_scale()
    grad_key_main = (
        jnp.einsum("hij,ihe->jhe", main_grad, queries, preferred_element_type=jnp.float32)
        * score_scale()
    )
    grad_key_own = own_rows * queries.astype(jnp.float32) * score_scale()
    grad_value_main = jnp.einsum(
        "hij,ihe->jhe", probabilities[:, :, :LEN], grad_out, preferred_element_type=jnp.float32
    )
    grad_value_own = jnp.transpose(probabilities[:, :, LEN]).astype(jnp.float32)[
        :, :, None
    ] * grad_out.astype(jnp.float32)
    return (
        grad_queries,
        grad_key_main,
        grad_value_main,
        grad_key_own,
        grad_value_own,
        main_grad,
        own_grad,
    )


def encoder_vectors(biases, gains):
    return (
        slices_of(biases.astype(jnp.float32), (D, D, D, FF, D, D, D)),
        slices_of(gains.astype(jnp.float32), (D, D)),
    )


def decoder_vectors(biases, gains):
    return (
        slices_of(biases.astype(jnp.float32), (D, D, HEADS * BUCKETS, D, D, D, D, FF, D, D, D, D)),
        slices_of(gains.astype(jnp.float32), (D, D, D)),
    )


def encoder_forward(source, src_valid, weights):
    vectors, gain_set = encoder_vectors(weights[5], weights[4])
    qkv_bias = jnp.concatenate([vectors[0], jnp.zeros((D,), jnp.float32), vectors[1]])
    projected = (
        (project(source, weights[0]) + qkv_bias).astype(jnp.bfloat16).reshape(LEN, 3, HEADS, HEAD)
    )
    attention_out, logsum = attention_forward(
        projected[:, 0], projected[:, 1], projected[:, 2], 0.0, src_valid
    )
    attended = attention_out.astype(jnp.bfloat16).reshape(LEN, D)
    first_sum = source.astype(jnp.float32) + project(attended, weights[1]) + vectors[2]
    first_norm = layer_norm(first_sum, gain_set[0], vectors[5])
    first_low = first_norm.astype(jnp.bfloat16)
    hidden = project(first_low, weights[2]) + vectors[3]
    activated = gelu_exact(hidden).astype(jnp.bfloat16)
    second_sum = first_norm + project(activated, weights[3]) + vectors[4]
    encoded = layer_norm(second_sum, gain_set[1], vectors[6])
    return (
        (projected, logsum, attended, first_sum, first_low, hidden, activated, second_sum),
        encoded,
    )


def encoder_back(source, saved, weights, src_valid, grad_encoded):
    projected, logsum, attended, first_sum, first_low, hidden, activated, second_sum = saved
    vectors, gain_set = encoder_vectors(weights[5], weights[4])
    grad_second, grad_gain_two, grad_norm_two = norm_back(
        second_sum, gain_set[1], vectors[6], grad_encoded
    )
    grad_ffn = grad_second.astype(jnp.bfloat16)
    grad_ffn_out = weight_grad(activated, grad_ffn)
    grad_hidden = gelu_back(hidden, project_back(grad_ffn, weights[3])).astype(jnp.bfloat16)
    grad_ffn_in = weight_grad(first_low, grad_hidden)
    grad_first, grad_gain_one, grad_norm_one = norm_back(
        first_sum, gain_set[0], vectors[5], grad_second + project_back(grad_hidden, weights[2])
    )
    grad_branch = grad_first.astype(jnp.bfloat16)
    grad_out_proj = weight_grad(attended, grad_branch)
    grad_attended = (
        project_back(grad_branch, weights[1]).astype(jnp.bfloat16).reshape(LEN, HEADS, HEAD)
    )
    grad_queries, grad_keys, grad_values, unused = attention_back(
        projected[:, 0], projected[:, 1], projected[:, 2], 0.0, src_valid, logsum, grad_attended
    )
    grad_projected = (
        jnp.stack([grad_queries, grad_keys, grad_values], axis=1)
        .astype(jnp.bfloat16)
        .reshape(LEN, 3 * D)
    )
    grad_in_proj = weight_grad(source, grad_projected)
    grad_source = grad_first + project_back(grad_projected, weights[0])
    column_sums = row_sum(grad_projected)
    grad_biases = jnp.concatenate(
        [
            column_sums[:D],
            column_sums[2 * D :],
            row_sum(grad_branch),
            row_sum(grad_hidden),
            row_sum(grad_ffn),
            grad_norm_one,
            grad_norm_two,
        ]
    )
    grad_gains = jnp.concatenate([grad_gain_one, grad_gain_two])
    return (
        (grad_in_proj, grad_out_proj, grad_ffn_in, grad_ffn_out, grad_gains, grad_biases),
        grad_source,
    )


def self_attention(streams, weights, mask_set):
    src_valid, main_valid, pred_valid, onehot = mask_set
    vectors, gain_set = decoder_vectors(weights[9], weights[8])
    qkv_bias = jnp.concatenate([vectors[0], jnp.zeros((D,), jnp.float32), vectors[1]])
    projected = (
        (project(streams, weights[0]) + qkv_bias)
        .astype(jnp.bfloat16)
        .reshape(LEN, NGRAM + 1, 3, HEADS, HEAD)
    )
    relative = (project(streams, weights[1]) + vectors[2]).reshape(LEN, NGRAM + 1, HEADS, BUCKETS)
    value_main = projected[:, 0, 2]
    main_out, main_logsum = attention_forward(
        projected[:, 0, 0],
        projected[:, 0, 1],
        value_main,
        stream_bias(relative[:, 0], onehot),
        main_valid,
    )
    outputs = [main_out]
    logsums = [main_logsum]
    for stream in range(1, NGRAM + 1):
        scores = predict_scores(projected, relative, onehot, pred_valid, stream)
        logsum = jax.nn.logsumexp(scores, axis=-1, keepdims=True)
        probabilities = jnp.exp(scores - logsum).astype(jnp.bfloat16)
        outputs.append(predict_values(probabilities, value_main, projected[:, stream, 2]))
        logsums.append(logsum)
    attended = jnp.stack(outputs, axis=1).astype(jnp.bfloat16).reshape(LEN, NGRAM + 1, D)
    return (projected, relative, logsums, attended)


def decoder_rest(streams, memory_low, attended, weights, src_valid):
    vectors, gain_set = decoder_vectors(weights[9], weights[8])
    first_sum = streams.astype(jnp.float32) + project(attended, weights[2]) + vectors[3]
    first_norm = layer_norm(first_sum, gain_set[0], vectors[9])
    first_low = first_norm.astype(jnp.bfloat16)
    cross_queries = (
        (project(first_low, weights[3]) + vectors[4])
        .astype(jnp.bfloat16)
        .reshape(LEN * (NGRAM + 1), HEADS, HEAD)
    )
    pair_bias = jnp.concatenate([jnp.zeros((D,), jnp.float32), vectors[5]])
    memory_pairs = (
        (project(memory_low, weights[4]) + pair_bias)
        .astype(jnp.bfloat16)
        .reshape(LEN, 2, HEADS, HEAD)
    )
    cross_values, cross_logsum = attention_forward(
        cross_queries, memory_pairs[:, 0], memory_pairs[:, 1], 0.0, src_valid
    )
    cross_attended = cross_values.astype(jnp.bfloat16).reshape(LEN, NGRAM + 1, D)
    second_sum = first_norm + project(cross_attended, weights[5]) + vectors[6]
    second_norm = layer_norm(second_sum, gain_set[1], vectors[10])
    second_low = second_norm.astype(jnp.bfloat16)
    hidden = project(second_low, weights[6]) + vectors[7]
    activated = gelu_exact(hidden).astype(jnp.bfloat16)
    third_sum = second_norm + project(activated, weights[7]) + vectors[8]
    decoded = layer_norm(third_sum, gain_set[2], vectors[11])
    return (
        (
            first_sum,
            first_low,
            cross_queries,
            memory_pairs,
            cross_logsum,
            cross_attended,
            second_sum,
            second_low,
            hidden,
            activated,
            third_sum,
        ),
        decoded,
    )


def decoder_back(streams, memory_low, self_saved, rest_saved, weights, mask_set, grad_decoded):
    projected, relative, logsums, attended = self_saved
    (
        first_sum,
        first_low,
        cross_queries,
        memory_pairs,
        cross_logsum,
        cross_attended,
        second_sum,
        second_low,
        hidden,
        activated,
        third_sum,
    ) = rest_saved
    src_valid, main_valid, pred_valid, onehot = mask_set
    vectors, gain_set = decoder_vectors(weights[9], weights[8])
    grad_third, grad_gain_three, grad_norm_three = norm_back(
        third_sum, gain_set[2], vectors[11], grad_decoded
    )
    grad_ffn = grad_third.astype(jnp.bfloat16)
    grad_ffn_out = weight_grad(activated, grad_ffn)
    grad_hidden = gelu_back(hidden, project_back(grad_ffn, weights[7])).astype(jnp.bfloat16)
    grad_ffn_in = weight_grad(second_low, grad_hidden)
    grad_second, grad_gain_two, grad_norm_two = norm_back(
        second_sum, gain_set[1], vectors[10], grad_third + project_back(grad_hidden, weights[6])
    )
    grad_cross_branch = grad_second.astype(jnp.bfloat16)
    grad_cross_out = weight_grad(cross_attended, grad_cross_branch)
    grad_cross_att = (
        project_back(grad_cross_branch, weights[5])
        .astype(jnp.bfloat16)
        .reshape(LEN * (NGRAM + 1), HEADS, HEAD)
    )
    grad_cross_q, grad_memory_key, grad_memory_value, unused = attention_back(
        cross_queries,
        memory_pairs[:, 0],
        memory_pairs[:, 1],
        0.0,
        src_valid,
        cross_logsum,
        grad_cross_att,
    )
    grad_cross_q = grad_cross_q.astype(jnp.bfloat16).reshape(LEN, NGRAM + 1, D)
    grad_cross_query = weight_grad(first_low, grad_cross_q)
    grad_pairs = (
        jnp.stack([grad_memory_key, grad_memory_value], axis=1)
        .astype(jnp.bfloat16)
        .reshape(LEN, 2 * D)
    )
    grad_cross_kv = weight_grad(memory_low, grad_pairs)
    grad_memory = project_back(grad_pairs, weights[4])
    grad_first, grad_gain_one, grad_norm_one = norm_back(
        first_sum, gain_set[0], vectors[9], grad_second + project_back(grad_cross_q, weights[3])
    )
    grad_branch = grad_first.astype(jnp.bfloat16)
    grad_out_proj = weight_grad(attended, grad_branch)
    grad_attended = (
        project_back(grad_branch, weights[2])
        .astype(jnp.bfloat16)
        .reshape(LEN, NGRAM + 1, HEADS, HEAD)
    )
    onehot_low = onehot.astype(jnp.bfloat16)
    first_bucket = (jnp.arange(BUCKETS) == 0).astype(jnp.float32)
    grad_query_main, grad_key_main, grad_value_main, grad_scores = attention_back(
        projected[:, 0, 0],
        projected[:, 0, 1],
        projected[:, 0, 2],
        stream_bias(relative[:, 0], onehot),
        main_valid,
        logsums[0],
        grad_attended[:, 0],
    )
    rel_grads = [bucket_grad(grad_scores, onehot_low)]
    query_grads = [grad_query_main]
    own_keys = []
    own_values = []
    for stream in range(1, NGRAM + 1):
        (
            grad_queries,
            grad_key_part,
            grad_value_part,
            grad_key_own,
            grad_value_own,
            main_grad,
            own_grad,
        ) = predict_back(
            projected,
            relative,
            onehot,
            pred_valid,
            stream,
            logsums[stream],
            grad_attended[:, stream],
        )
        grad_key_main = grad_key_main + grad_key_part
        grad_value_main = grad_value_main + grad_value_part
        query_grads.append(grad_queries)
        own_keys.append(grad_key_own)
        own_values.append(grad_value_own)
        rel_grads.append(
            bucket_grad(main_grad, onehot_low)
            + jnp.transpose(own_grad).astype(jnp.float32)[:, :, None] * first_bucket
        )
    key_grads = [grad_key_main] + own_keys
    value_grads = [grad_value_main] + own_values
    grad_projected = (
        jnp.stack(
            [
                jnp.stack(query_grads, axis=1),
                jnp.stack(key_grads, axis=1),
                jnp.stack(value_grads, axis=1),
            ],
            axis=2,
        )
        .astype(jnp.bfloat16)
        .reshape(LEN, NGRAM + 1, 3 * D)
    )
    grad_relative = (
        jnp.stack(rel_grads, axis=1).astype(jnp.bfloat16).reshape(LEN, NGRAM + 1, HEADS * BUCKETS)
    )
    grad_in_proj = weight_grad(streams, grad_projected)
    grad_rel_proj = weight_grad(streams, grad_relative)
    grad_streams = (
        grad_first
        + project_back(grad_projected, weights[0])
        + project_back(grad_relative, weights[1])
    )
    column_sums = row_sum(grad_projected)
    grad_biases = jnp.concatenate(
        [
            column_sums[:D],
            column_sums[2 * D :],
            row_sum(grad_relative),
            row_sum(grad_branch),
            row_sum(grad_cross_q),
            row_sum(grad_pairs)[D:],
            row_sum(grad_cross_branch),
            row_sum(grad_hidden),
            row_sum(grad_ffn),
            grad_norm_one,
            grad_norm_two,
            grad_norm_three,
        ]
    )
    grad_gains = jnp.concatenate([grad_gain_one, grad_gain_two, grad_gain_three])
    return (
        (
            grad_in_proj,
            grad_rel_proj,
            grad_out_proj,
            grad_cross_query,
            grad_cross_kv,
            grad_cross_out,
            grad_ffn_in,
            grad_ffn_out,
            grad_gains,
            grad_biases,
        ),
        grad_streams,
        grad_memory,
    )


def shards(
    source,
    dec_in,
    src_lengths,
    tgt_lengths,
    enc_in_proj,
    enc_out_proj,
    enc_ffn_in,
    enc_ffn_out,
    enc_gains,
    enc_biases,
    dec_in_proj,
    dec_rel_proj,
    dec_out_proj,
    cross_query,
    cross_kv,
    cross_out,
    dec_ffn_in,
    dec_ffn_out,
    dec_gains,
    dec_biases,
    enc_cot,
    dec_cot,
):
    enc_weights = (
        lax.all_gather(enc_in_proj, ("dp", "fsdp"), axis=0, tiled=True),
        lax.all_gather(enc_out_proj, ("dp", "fsdp"), axis=0, tiled=True),
        lax.all_gather(enc_ffn_in, ("dp", "fsdp"), axis=0, tiled=True),
        lax.all_gather(enc_ffn_out, ("dp", "fsdp"), axis=0, tiled=True),
        lax.all_gather(enc_gains, ("dp", "fsdp"), axis=0, tiled=True),
        lax.all_gather(enc_biases, ("dp", "fsdp"), axis=0, tiled=True),
    )
    dec_weights = (
        lax.all_gather(dec_in_proj, ("dp", "fsdp"), axis=0, tiled=True),
        lax.all_gather(dec_rel_proj, ("dp", "fsdp"), axis=0, tiled=True),
        lax.all_gather(dec_out_proj, ("dp", "fsdp"), axis=0, tiled=True),
        lax.all_gather(cross_query, ("dp", "fsdp"), axis=0, tiled=True),
        lax.all_gather(cross_kv, ("dp", "fsdp"), axis=0, tiled=True),
        lax.all_gather(cross_out, ("dp", "fsdp"), axis=0, tiled=True),
        lax.all_gather(dec_ffn_in, ("dp", "fsdp"), axis=0, tiled=True),
        lax.all_gather(dec_ffn_out, ("dp", "fsdp"), axis=0, tiled=True),
        lax.all_gather(dec_gains, ("dp", "fsdp"), axis=0, tiled=True),
        lax.all_gather(dec_biases, ("dp", "fsdp"), axis=0, tiled=True),
    )
    positions = jnp.arange(LEN, dtype=jnp.int32)
    src_valid = (positions < src_lengths[0])[None, None, :]
    inside = positions[None, :] < tgt_lengths[0]
    main_valid = ((positions[None, :] <= positions[:, None]) & inside)[None]
    pred_valid = ((positions[None, :] < positions[:, None]) & inside)[None]
    onehot = bucket_table(LEN, BUCKETS)
    mask_set = (src_valid, main_valid, pred_valid, onehot)
    enc_saved, encoded = encoder_forward(source, src_valid, enc_weights)
    memory_low = encoded.astype(jnp.bfloat16)
    self_saved = self_attention(dec_in, dec_weights, mask_set)
    rest_saved, decoded = decoder_rest(dec_in, memory_low, self_saved[3], dec_weights, src_valid)
    back_weights = (
        lax.all_gather(dec_in_proj, ("dp", "fsdp"), axis=0, tiled=True),
        lax.all_gather(dec_rel_proj, ("dp", "fsdp"), axis=0, tiled=True),
        lax.all_gather(dec_out_proj, ("dp", "fsdp"), axis=0, tiled=True),
        lax.all_gather(cross_query, ("dp", "fsdp"), axis=0, tiled=True),
        lax.all_gather(cross_kv, ("dp", "fsdp"), axis=0, tiled=True),
        lax.all_gather(cross_out, ("dp", "fsdp"), axis=0, tiled=True),
        lax.all_gather(dec_ffn_in, ("dp", "fsdp"), axis=0, tiled=True),
        lax.all_gather(dec_ffn_out, ("dp", "fsdp"), axis=0, tiled=True),
        lax.all_gather(dec_gains, ("dp", "fsdp"), axis=0, tiled=True),
        lax.all_gather(dec_biases, ("dp", "fsdp"), axis=0, tiled=True),
    )
    back_saved = self_attention(dec_in, back_weights, mask_set)
    dec_grads, grad_streams, grad_memory = decoder_back(
        dec_in,
        memory_low,
        back_saved,
        rest_saved,
        back_weights,
        mask_set,
        dec_cot.astype(jnp.float32),
    )
    dec_shards = (
        lax.psum_scatter(dec_grads[0], ("dp", "fsdp"), scatter_dimension=0, tiled=True),
        lax.psum_scatter(dec_grads[1], ("dp", "fsdp"), scatter_dimension=0, tiled=True),
        lax.psum_scatter(dec_grads[2], ("dp", "fsdp"), scatter_dimension=0, tiled=True),
        lax.psum_scatter(dec_grads[3], ("dp", "fsdp"), scatter_dimension=0, tiled=True),
        lax.psum_scatter(dec_grads[4], ("dp", "fsdp"), scatter_dimension=0, tiled=True),
        lax.psum_scatter(dec_grads[5], ("dp", "fsdp"), scatter_dimension=0, tiled=True),
        lax.psum_scatter(dec_grads[6], ("dp", "fsdp"), scatter_dimension=0, tiled=True),
        lax.psum_scatter(dec_grads[7], ("dp", "fsdp"), scatter_dimension=0, tiled=True),
        lax.psum_scatter(dec_grads[8], ("dp", "fsdp"), scatter_dimension=0, tiled=True),
        lax.psum_scatter(dec_grads[9], ("dp", "fsdp"), scatter_dimension=0, tiled=True),
    )
    enc_grads, grad_source = encoder_back(
        source, enc_saved, enc_weights, src_valid, enc_cot.astype(jnp.float32) + grad_memory
    )
    enc_shards = (
        lax.psum_scatter(enc_grads[0], ("dp", "fsdp"), scatter_dimension=0, tiled=True),
        lax.psum_scatter(enc_grads[1], ("dp", "fsdp"), scatter_dimension=0, tiled=True),
        lax.psum_scatter(enc_grads[2], ("dp", "fsdp"), scatter_dimension=0, tiled=True),
        lax.psum_scatter(enc_grads[3], ("dp", "fsdp"), scatter_dimension=0, tiled=True),
        lax.psum_scatter(enc_grads[4], ("dp", "fsdp"), scatter_dimension=0, tiled=True),
        lax.psum_scatter(enc_grads[5], ("dp", "fsdp"), scatter_dimension=0, tiled=True),
    )
    shard_list = tuple(enc_shards) + tuple(dec_shards)
    return (
        encoded.astype(jnp.bfloat16),
        decoded.astype(jnp.bfloat16),
        grad_source,
        grad_streams,
        shard_list[0],
        shard_list[1],
        shard_list[2],
        shard_list[3],
        shard_list[4],
        shard_list[5],
        shard_list[6],
        shard_list[7],
        shard_list[8],
        shard_list[9],
        shard_list[10],
        shard_list[11],
        shard_list[12],
        shard_list[13],
        shard_list[14],
        shard_list[15],
    )


def solution(mesh):
    placed = (
        P(("dp", "fsdp"), None),
        P(("dp", "fsdp"), None, None),
        P(("dp", "fsdp")),
        P(("dp", "fsdp")),
        P(("dp", "fsdp"), None),
        P(("dp", "fsdp"), None),
        P(("dp", "fsdp"), None),
        P(("dp", "fsdp"), None),
        P(("dp", "fsdp")),
        P(("dp", "fsdp")),
        P(("dp", "fsdp"), None),
        P(("dp", "fsdp"), None),
        P(("dp", "fsdp"), None),
        P(("dp", "fsdp"), None),
        P(("dp", "fsdp"), None),
        P(("dp", "fsdp"), None),
        P(("dp", "fsdp"), None),
        P(("dp", "fsdp"), None),
        P(("dp", "fsdp")),
        P(("dp", "fsdp")),
        P(("dp", "fsdp"), None),
        P(("dp", "fsdp"), None, None),
    )
    return jax.shard_map(
        shards,
        mesh=mesh,
        in_specs=placed,
        out_specs=(
            P(("dp", "fsdp"), None),
            P(("dp", "fsdp"), None, None),
            P(("dp", "fsdp"), None),
            P(("dp", "fsdp"), None, None),
            P(("dp", "fsdp"), None),
            P(("dp", "fsdp"), None),
            P(("dp", "fsdp"), None),
            P(("dp", "fsdp"), None),
            P(("dp", "fsdp")),
            P(("dp", "fsdp")),
            P(("dp", "fsdp"), None),
            P(("dp", "fsdp"), None),
            P(("dp", "fsdp"), None),
            P(("dp", "fsdp"), None),
            P(("dp", "fsdp"), None),
            P(("dp", "fsdp"), None),
            P(("dp", "fsdp"), None),
            P(("dp", "fsdp"), None),
            P(("dp", "fsdp")),
            P(("dp", "fsdp")),
        ),
        check_vma=False,
    )
```

profile of v0, /device:TPU:0, one launch (start us, length us, event | category | flops | bytes accessed | tf_op | source)
XLA Modules:
  0.0 3046.4 jit_solution(3797172634487764078)
XLA Ops:
  18.8 43.2 %all-reduce.10 = (bf16[10240]{0:T(1024)(128)(2,1)S(1)}, bf16[2048]{0:T(1024)(128)(2,1)S(1)}, bf16[14848]{0:T(1024)(128)(2,1)S(1)}, bf16[3072]{0:T(1024)(128)(2,1)S(1)}) all-reduce(bf16[10240]{0:T(1024)(128)(2,1)S(1)} %dynamic-update-slice, bf16[2048]{0:T(1024)(128)(2,1)S(1)} %dynamic-update-slice.1, ...), channel_id=1, replica_groups=mesh['dp'=4,'fsdp'=8] {'dp','fsdp'}, use_global_device_ids=true, to_apply=%add.1 | all-reduce | flops 30208 | bytes 120832
  81.6 57.7 %all-gather.21.cloned.1.call-done = bf16[1024,3072]{1,0:T(8,128)(2,1)} async-done(((bf16[32,3072]{1,0:T(8,128)(2,1)}), bf16[1024,3072]{1,0:T(8,128)(2,1)}) %all-gather.21.cloned.1.call-update) | async-done | bytes 6291472 | tf_op jit(solution)/shard_map/all_gather | solution.py:574
  155.5 55.0 %all-gather.13.cloned.1.call-done = bf16[1024,3072]{1,0:T(8,128)(2,1)} async-done(((bf16[32,3072]{1,0:T(8,128)(2,1)}), bf16[1024,3072]{1,0:T(8,128)(2,1)}) %all-gather.13.cloned.1.call-update) | async-done | bytes 6291472 | tf_op jit(solution)/shard_map/all_gather | solution.py:566
  227.2 41.1 %all-gather.25.cloned.1.call-done = bf16[1024,1024]{1,0:T(8,128)(2,1)} async-done(((bf16[32,1024]{1,0:T(8,128)(2,1)}), bf16[1024,1024]{1,0:T(8,128)(2,1)}) %all-gather.25.cloned.1.call-update) | async-done | bytes 2097168 | tf_op jit(solution)/shard_map/all_gather | solution.py:576
  272.9 53.7 %all-gather.29.cloned.1.call-done = bf16[1024,1024]{1,0:T(8,128)(2,1)} async-done(((bf16[32,1024]{1,0:T(8,128)(2,1)}), bf16[1024,1024]{1,0:T(8,128)(2,1)}) %all-gather.29.cloned.1.call-update) | async-done | bytes 2097168 | tf_op jit(solution)/shard_map/all_gather | solution.py:577
  337.3 47.4 %all-gather.15.cloned.1.call-done = bf16[1024,1024]{1,0:T(8,128)(2,1)} async-done(((bf16[32,1024]{1,0:T(8,128)(2,1)}), bf16[1024,1024]{1,0:T(8,128)(2,1)}) %all-gather.15.cloned.1.call-update) | async-done | bytes 2097168 | tf_op jit(solution)/shard_map/all_gather | solution.py:567
  387.2 76.7 %all-gather.17.cloned.1.call-done = bf16[1024,4096]{1,0:T(8,128)(2,1)} async-done(((bf16[32,4096]{1,0:T(8,128)(2,1)}), bf16[1024,4096]{1,0:T(8,128)(2,1)}) %all-gather.17.cloned.1.call-update) | async-done | bytes 8388624 | tf_op jit(solution)/shard_map/all_gather | solution.py:568
  473.9 68.9 %all-gather.19.cloned.1.call-done = bf16[4096,1024]{1,0:T(8,128)(2,1)} async-done(((bf16[128,1024]{1,0:T(8,128)(2,1)}), bf16[4096,1024]{1,0:T(8,128)(2,1)}) %all-gather.19.cloned.1.call-update) | async-done | bytes 8388624 | tf_op jit(solution)/shard_map/all_gather | solution.py:569
  548.6 57.9 %all-gather.27.cloned.1.call-done = bf16[1024,2048]{1,0:T(8,128)(2,1)} async-done(((bf16[32,2048]{1,0:T(8,128)(2,1)}), bf16[1024,2048]{1,0:T(8,128)(2,1)}) %all-gather.27.cloned.1.call-update) | async-done | bytes 4194320 | tf_op jit(solution)/shard_map/all_gather | solution.py:578
  622.3 42.1 %all-gather.31.cloned.1.call-done = bf16[1024,1024]{1,0:T(8,128)(2,1)} async-done(((bf16[32,1024]{1,0:T(8,128)(2,1)}), bf16[1024,1024]{1,0:T(8,128)(2,1)}) %all-gather.31.cloned.1.call-update) | async-done | bytes 2097168 | tf_op jit(solution)/shard_map/all_gather | solution.py:579
  669.6 74.2 %all-gather.33.cloned.1.call-done = bf16[1024,4096]{1,0:T(8,128)(2,1)} async-done(((bf16[32,4096]{1,0:T(8,128)(2,1)}), bf16[1024,4096]{1,0:T(8,128)(2,1)}) %all-gather.33.cloned.1.call-update) | async-done | bytes 8388624 | tf_op jit(solution)/shard_map/all_gather | solution.py:580
  770.3 52.3 %all-gather.35.cloned.1.call-done = bf16[4096,1024]{1,0:T(8,128)(2,1)} async-done(((bf16[128,1024]{1,0:T(8,128)(2,1)}), bf16[4096,1024]{1,0:T(8,128)(2,1)}) %all-gather.35.cloned.1.call-update) | async-done | bytes 8388624 | tf_op jit(solution)/shard_map/all_gather | solution.py:581
  1156.8 89.0 %reduce-scatter.41.cloned.1.call-done = f32[32,512]{1,0:T(8,128)} async-done(((f32[1024,512]{1,0:T(8,128)}), f32[32,512]{1,0:T(8,128)}) %reduce-scatter.41.cloned.1.call-update) | async-done | bytes 65552
  1245.8 141.9 %reduce-scatter.19.cloned.1.call-done = f32[32,1024]{1,0:T(8,128)} async-done(((f32[1024,1024]{1,0:T(8,128)}), f32[32,1024]{1,0:T(8,128)}) %reduce-scatter.19.cloned.1.call-update) | async-done | bytes 131088 | tf_op jit(solution)/shard_map/reduce_scatter | solution.py:635
  1387.7 142.5 %reduce-scatter.25.cloned.1.call-done = f32[32,1024]{1,0:T(8,128)} async-done(((f32[1024,1024]{1,0:T(8,128)}), f32[32,1024]{1,0:T(8,128)}) %reduce-scatter.25.cloned.1.call-update) | async-done | bytes 131088 | tf_op jit(solution)/shard_map/reduce_scatter | solution.py:621
  1530.2 142.2 %reduce-scatter.27.cloned.1.call-done = f32[32,1024]{1,0:T(8,128)} async-done(((f32[1024,1024]{1,0:T(8,128)}), f32[32,1024]{1,0:T(8,128)}) %reduce-scatter.27.cloned.1.call-update) | async-done | bytes 131088 | tf_op jit(solution)/shard_map/reduce_scatter | solution.py:622
  1672.4 142.6 %reduce-scatter.31.cloned.1.call-done = f32[32,1024]{1,0:T(8,128)} async-done(((f32[1024,1024]{1,0:T(8,128)}), f32[32,1024]{1,0:T(8,128)}) %reduce-scatter.31.cloned.1.call-update) | async-done | bytes 131088 | tf_op jit(solution)/shard_map/reduce_scatter | solution.py:624
  1815.0 159.9 %reduce-scatter.37.cloned.1.call-done = f32[32,3072]{1,0:T(8,128)} async-done(((f32[1024,3072]{1,0:T(8,128)}), f32[32,3072]{1,0:T(8,128)}) %reduce-scatter.37.cloned.1.call-update) | async-done | bytes 393232
  1974.9 160.9 %reduce-scatter.39.cloned.1.call-done = f32[32,3072]{1,0:T(8,128)} async-done(((f32[1024,3072]{1,0:T(8,128)}), f32[32,3072]{1,0:T(8,128)}) %reduce-scatter.39.cloned.1.call-update) | async-done | bytes 393232
  2135.8 155.0 %reduce-scatter.29.cloned.1.call-done = f32[32,2048]{1,0:T(8,128)} async-done(((f32[1024,2048]{1,0:T(8,128)}), f32[32,2048]{1,0:T(8,128)}) %reduce-scatter.29.cloned.1.call-update) | async-done | bytes 262160 | tf_op jit(solution)/shard_map/reduce_scatter | solution.py:623
  2290.8 186.8 %reduce-scatter.21.cloned.1.call-done = f32[32,4096]{1,0:T(8,128)} async-done(((f32[1024,4096]{1,0:T(8,128)}), f32[32,4096]{1,0:T(8,128)}) %reduce-scatter.21.cloned.1.call-update) | async-done | bytes 524304 | tf_op jit(solution)/shard_map/reduce_scatter | solution.py:636
  2477.7 187.4 %reduce-scatter.23.cloned.1.call-done = f32[128,1024]{1,0:T(8,128)} async-done(((f32[4096,1024]{1,0:T(8,128)}), f32[128,1024]{1,0:T(8,128)}) %reduce-scatter.23.cloned.1.call-update) | async-done | bytes 524304 | tf_op jit(solution)/shard_map/reduce_scatter | solution.py:637
  2665.1 187.2 %reduce-scatter.33.cloned.1.call-done = f32[32,4096]{1,0:T(8,128)} async-done(((f32[1024,4096]{1,0:T(8,128)}), f32[32,4096]{1,0:T(8,128)}) %reduce-scatter.33.cloned.1.call-update) | async-done | bytes 524304 | tf_op jit(solution)/shard_map/reduce_scatter | solution.py:625
  2852.3 187.4 %reduce-scatter.35.cloned.1.call-done = f32[128,1024]{1,0:T(8,128)} async-done(((f32[4096,1024]{1,0:T(8,128)}), f32[128,1024]{1,0:T(8,128)}) %reduce-scatter.35.cloned.1.call-update) | async-done | bytes 524304 | tf_op jit(solution)/shard_map/reduce_scatter | solution.py:626
  (689 shorter events, 475.4 us)
Async XLA Ops:
  7.9 131.4 %all-gather.21.cloned.1.call-start = ((), (), s32[]{:S(2)}) async-start(), calls=%async_computation.16 | async-start | bytes 6488064 | tf_op jit(solution)/shard_map/all_gather | solution.py:574
  8.7 201.8 %all-gather.13.cloned.1.call-start = ((), (), s32[]{:S(2)}) async-start(), calls=%async_computation.12 | async-start | bytes 6488064 | tf_op jit(solution)/shard_map/all_gather | solution.py:566
  9.4 258.9 %all-gather.25.cloned.1.call-start = ((), (), s32[]{:S(2)}) async-start(), calls=%async_computation.18 | async-start | bytes 2162688 | tf_op jit(solution)/shard_map/all_gather | solution.py:576
  10.0 316.6 %all-gather.29.cloned.1.call-start = ((), (), s32[]{:S(2)}) async-start(), calls=%async_computation.20 | async-start | bytes 2162688 | tf_op jit(solution)/shard_map/all_gather | solution.py:577
  10.6 374.2 %all-gather.15.cloned.1.call-start = ((), (), s32[]{:S(2)}) async-start(), calls=%async_computation.13 | async-start | bytes 2162688 | tf_op jit(solution)/shard_map/all_gather | solution.py:567
  11.2 452.8 %all-gather.17.cloned.1.call-start = ((), (), s32[]{:S(2)}) async-start(), calls=%async_computation.14 | async-start | bytes 8650752 | tf_op jit(solution)/shard_map/all_gather | solution.py:568
  11.9 530.9 %all-gather.19.cloned.1.call-start = ((), (), s32[]{:S(2)}) async-start(), calls=%async_computation.15 | async-start | bytes 8650752 | tf_op jit(solution)/shard_map/all_gather | solution.py:569
  12.7 593.9 %all-gather.27.cloned.1.call-start = ((), (), s32[]{:S(2)}) async-start(), calls=%async_computation.19 | async-start | bytes 4325376 | tf_op jit(solution)/shard_map/all_gather | solution.py:578
  13.4 651.1 %all-gather.31.cloned.1.call-start = ((), (), s32[]{:S(2)}) async-start(), calls=%async_computation.21 | async-start | bytes 2162688 | tf_op jit(solution)/shard_map/all_gather | solution.py:579
  14.0 729.7 %all-gather.33.cloned.1.call-start = ((), (), s32[]{:S(2)}) async-start(), calls=%async_computation.22 | async-start | bytes 8650752 | tf_op jit(solution)/shard_map/all_gather | solution.py:580
  14.7 807.9 %all-gather.35.cloned.1.call-start = ((), (), s32[]{:S(2)}) async-start(), calls=%async_computation.23 | async-start | bytes 8650752 | tf_op jit(solution)/shard_map/all_gather | solution.py:581
  15.3 1136.3 %all-reduce.13.cloned.1.call-start = ((), (), s32[]{:S(2)}) async-start(), calls=%async_computation.36 | async-start | bytes 245760
  984.8 261.0 %reduce-scatter.41.cloned.1.call-start = ((), (), s32[]{:S(2)}) async-start(), calls=%async_computation.35 | async-start | bytes 2162688
  991.0 396.7 %reduce-scatter.19.cloned.1.call-start = ((), (), s32[]{:S(2)}) async-start(), calls=%async_computation.24 | async-start | bytes 4325376 | tf_op jit(solution)/shard_map/reduce_scatter | solution.py:635
  995.6 534.6 %reduce-scatter.25.cloned.1.call-start = ((), (), s32[]{:S(2)}) async-start(), calls=%async_computation.27 | async-start | bytes 4325376 | tf_op jit(solution)/shard_map/reduce_scatter | solution.py:621
  1015.3 657.1 %reduce-scatter.27.cloned.1.call-start = ((), (), s32[]{:S(2)}) async-start(), calls=%async_computation.28 | async-start | bytes 4325376 | tf_op jit(solution)/shard_map/reduce_scatter | solution.py:622
  1026.0 789.0 %reduce-scatter.31.cloned.1.call-start = ((), (), s32[]{:S(2)}) async-start(), calls=%async_computation.30 | async-start | bytes 4325376 | tf_op jit(solution)/shard_map/reduce_scatter | solution.py:624
  1037.1 937.8 %reduce-scatter.37.cloned.1.call-start = ((), (), s32[]{:S(2)}) async-start(), calls=%async_computation.33 | async-start | bytes 12976128
  1057.2 1078.6 %reduce-scatter.39.cloned.1.call-start = ((), (), s32[]{:S(2)}) async-start(), calls=%async_computation.34 | async-start | bytes 12976128
  1086.7 1204.1 %reduce-scatter.29.cloned.1.call-start = ((), (), s32[]{:S(2)}) async-start(), calls=%async_computation.29 | async-start | bytes 8650752 | tf_op jit(solution)/shard_map/reduce_scatter | solution.py:623
  1092.5 1385.2 %reduce-scatter.21.cloned.1.call-start = ((), (), s32[]{:S(2)}) async-start(), calls=%async_computation.25 | async-start | bytes 17301504 | tf_op jit(solution)/shard_map/reduce_scatter | solution.py:636
  1102.1 1562.9 %reduce-scatter.23.cloned.1.call-start = ((), (), s32[]{:S(2)}) async-start(), calls=%async_computation.26 | async-start | bytes 17301504 | tf_op jit(solution)/shard_map/reduce_scatter | solution.py:637
  1111.6 1740.8 %reduce-scatter.33.cloned.1.call-start = ((), (), s32[]{:S(2)}) async-start(), calls=%async_computation.31 | async-start | bytes 17301504 | tf_op jit(solution)/shard_map/reduce_scatter | solution.py:625
  1123.2 1916.5 %reduce-scatter.35.cloned.1.call-start = ((), (), s32[]{:S(2)}) async-start(), calls=%async_computation.32 | async-start | bytes 17301504 | tf_op jit(solution)/shard_map/reduce_scatter | solution.py:626
  (188 other events, 5914.2 us)
Sparse Core Ops, SparseCore 0:
  11.0 56.6 all-gather.22
  70.8 68.5 all-gather.20
  142.4 68.1 all-gather.12
  271.2 55.3 all-gather.28
  329.4 55.3 all-gather.14
  387.8 76.1 all-gather.16
  466.9 75.8 all-gather.18
  545.8 60.6 all-gather.26
  609.4 55.0 all-gather.30
  667.4 76.2 all-gather.32
  746.6 75.9 all-gather.34
  985.0 121.4 all-reduce.12
  1109.2 136.5 reduce-scatter.40
  1248.6 139.0 reduce-scatter.18
  1390.5 139.6 reduce-scatter.24
  1533.0 139.3 reduce-scatter.26
  1675.2 139.7 reduce-scatter.30
  1822.6 152.2 reduce-scatter.36
  1981.4 154.4 reduce-scatter.38
  2138.8 151.9 reduce-scatter.28
  2293.8 183.8 reduce-scatter.20
  2480.7 184.3 reduce-scatter.22
  2667.9 184.3 reduce-scatter.32
  2855.3 184.3 reduce-scatter.34
  (1 shorter events, 54.9 us)
where the time goes:
time: 3060 us; the launch traced here: 3050 us
  waiting for transfers between devices  2520 us (82%)
  matrix products  229 us (7%)
  local copies, waits for them, and re-layouts  194 us (6%)
  other arithmetic  43.9 us (1%)
  blocking collectives  43.2 us (1%)
    unnamed x29, waiting for transfers between devices  417 us
    reduce_scatter x1, waiting for transfers between devices, shards(): lax.psum_scatter(enc_grads[3], ('dp', 'fsdp'), scatter_dimension=0, tiled...  187 us
    reduce_scatter x1, waiting for transfers between devices, shards(): lax.psum_scatter(dec_grads[7], ('dp', 'fsdp'), scatter_dimension=0, tiled...  187 us
    reduce_scatter x1, waiting for transfers between devices, shards(): lax.psum_scatter(dec_grads[6], ('dp', 'fsdp'), scatter_dimension=0, tiled...  187 us
    reduce_scatter x1, waiting for transfers between devices, shards(): lax.psum_scatter(enc_grads[2], ('dp', 'fsdp'), scatter_dimension=0, tiled...  187 us
    reduce_scatter x1, waiting for transfers between devices, shards(): lax.psum_scatter(dec_grads[4], ('dp', 'fsdp'), scatter_dimension=0, tiled...  155 us
    reduce_scatter x1, waiting for transfers between devices, shards(): lax.psum_scatter(dec_grads[5], ('dp', 'fsdp'), scatter_dimension=0, tiled...  143 us
    reduce_scatter x1, waiting for transfers between devices, shards(): lax.psum_scatter(dec_grads[2], ('dp', 'fsdp'), scatter_dimension=0, tiled...  143 us
  transfers between devices with their start and end apart: 25, of which 23 were waited for; matrix products, arithmetic and copies ran while one was open for 9% of the time, Pallas kernels for 0%

commit v1 on v0

v1 whole, which is shorter than its diff:
```python
import math

import jax
import jax.numpy as jnp
from jax import lax
from jax.sharding import PartitionSpec as P

D = 1024
HEADS = 16
HEAD = 64
FF = 4096
NGRAM = 2
STREAMS = NGRAM + 1
BUCKETS = 32
LEN = 128
HALF = D // 2
OWN_HEADS = HEADS // 2
REL_HALF = OWN_HEADS * BUCKETS
HIDDEN_HALF = FF // 2
WIDE = 512
EPSILON = 1e-05
MASKED = -1000000000.0
SCALE = 1.0 / math.sqrt(HEAD)
BF = jnp.bfloat16
F32 = jnp.float32
ENC_WIDTHS = (D, D, D, FF, D, D, D)
DEC_WIDTHS = (D, D, HEADS * BUCKETS, D, D, D, D, FF, D, D, D, D)


def bucket_value(distance, bucket_count):
    exact_count = bucket_count // 2
    if distance < exact_count:
        return distance
    return min(
        bucket_count - 1,
        exact_count
        + int(
            math.log(distance / exact_count)
            / math.log(128 / exact_count)
            * (bucket_count - exact_count)
        ),
    )


def bucket_table(length, bucket_count):
    positions = jnp.arange(length, dtype=jnp.int32)
    distance = positions[:, None] - positions[None, :]
    bucket = jnp.zeros((length, length), jnp.int32)
    for target in range(1, bucket_count):
        distance_at = 1
        while bucket_value(distance_at, bucket_count) < target:
            distance_at += 1
        bucket = bucket + (distance >= distance_at).astype(jnp.int32)
    return (bucket[:, :, None] == jnp.arange(bucket_count, dtype=jnp.int32)).astype(F32)


def slices_of(vector, widths):
    starts = 0
    result = []
    for amount in widths:
        result.append(vector[starts : starts + amount])
        starts += amount
    return result


def dot(a, b):
    return lax.dot_general(a, b, (((1,), (0,)), ((), ())), preferred_element_type=F32)


def dot_t(a, b):
    return lax.dot_general(a, b, (((1,), (1,)), ((), ())), preferred_element_type=F32)


def dot_g(a, b):
    return lax.dot_general(a, b, (((0,), (0,)), ((), ())), preferred_element_type=F32)


def norm_stats(values):
    average = jnp.mean(values, axis=-1, keepdims=True)
    centered = values - average
    variance = jnp.mean(centered * centered, axis=-1, keepdims=True)
    inverse = lax.rsqrt(variance + EPSILON)
    return centered * inverse, inverse


def norm(values, gain, shift):
    unit, inverse = norm_stats(values)
    return unit * gain + shift


def norm_back(values, gain, grads):
    unit, inverse = norm_stats(values)
    scaled = grads * gain
    mean_one = jnp.mean(scaled, axis=-1, keepdims=True)
    mean_two = jnp.mean(scaled * unit, axis=-1, keepdims=True)
    return (
        inverse * (scaled - mean_one - unit * mean_two),
        jnp.sum(grads * unit, axis=0),
        jnp.sum(grads, axis=0),
    )


def gelu_exact(inputs):
    return jax.nn.gelu(inputs, approximate=False)


def gelu_back(inputs, gradients):
    outputs, pullback = jax.vjp(gelu_exact, inputs)
    return pullback(gradients)[0]


def col_sum(values):
    return jnp.sum(values.astype(F32), axis=0)


class Layout:
    def __init__(self, ndp, nf):
        self.ndp = ndp
        self.nf = nf
        self.nz = nf // 2
        self.chips = ndp * self.nz
        self.devices = ndp * nf
        self.r = D // self.devices
        self.f = FF // self.devices

    def place(self):
        self.dp = lax.axis_index("dp")
        fs = lax.axis_index("fsdp")
        self.z = fs // 2
        self.core = fs % 2

    def swap(self, value):
        return lax.ppermute(value, "fsdp", [(i, i ^ 1) for i in range(self.nf)])

    def shift_z(self, value, step):
        return lax.ppermute(
            value, "fsdp", [(i, (i + 2 * step) % self.nf) for i in range(self.nf)]
        )

    def flip_dp(self, value, mask):
        return lax.ppermute(value, "dp", [(i, i ^ mask) for i in range(self.ndp)])

    def shift_dp(self, value, step):
        return lax.ppermute(value, "dp", [(i, (i + step) % self.ndp) for i in range(self.ndp)])

    def pick(self, first, second):
        return jnp.where(self.core == 0, first, second)

    def pair(self, own, other, axis):
        return self.pick(
            jnp.concatenate([own, other], axis=axis), jnp.concatenate([other, own], axis=axis)
        )


def tie(value, *others):
    return lax.optimization_barrier((value,) + others)[0]


def gather_z(lay, buf):
    out = jnp.zeros((lay.nz,) + buf.shape, buf.dtype)
    out = lax.dynamic_update_slice(out, buf[None], (lay.z, 0, 0))
    for step in range(1, lay.nz):
        got = lay.shift_z(buf, step)
        out = lax.dynamic_update_slice(out, got[None], ((lay.z - step) % lay.nz, 0, 0))
    return out


def gather_dp_first(lay, buf):
    if lay.ndp == 4:
        return [lay.flip_dp(buf, 1), lay.flip_dp(buf, 2)]
    return [lay.shift_dp(buf, step) for step in range(1, lay.ndp)]


def gather_dp_rest(lay, buf, first):
    half = lay.nz // 2
    out = jnp.zeros((lay.ndp,) + buf.shape, buf.dtype)
    if lay.ndp == 4:
        low = lay.flip_dp(first[0][:half], 2)
        high = lay.flip_dp(first[1][half:], 1)
        parts = [(0, 0, buf), (1, 0, first[0]), (2, 0, first[1]), (3, 0, low), (3, half, high)]
        for flip, at, part in parts:
            out = lax.dynamic_update_slice(out, part[None], (lay.dp ^ flip, at, 0, 0))
        return out
    out = lax.dynamic_update_slice(out, buf[None], (lay.dp, 0, 0, 0))
    for step in range(1, lay.ndp):
        out = lax.dynamic_update_slice(
            out, first[step - 1][None], ((lay.dp - step) % lay.ndp, 0, 0, 0)
        )
    return out


def gather_all(lay, bufs):
    staged = []
    results = []
    firsts = []
    for i, buf in enumerate(bufs):
        if i >= 2:
            buf = tie(buf, *firsts[i - 2])
        z = gather_z(lay, buf)
        staged.append(z)
        firsts.append(gather_dp_first(lay, z))
    for z, first in zip(staged, firsts):
        results.append(gather_dp_rest(lay, z, first))
    return results


def take(buf, index, axis=0):
    return lax.dynamic_index_in_dim(buf, index, axis, keepdims=False)


def add_low(*values):
    return sum(v.astype(F32) for v in values).astype(BF)


def scatter_dp(lay, buf):
    if lay.ndp == 4:
        half = lay.nz // 2
        far = take(buf, lay.dp ^ 3)
        to_x = take(buf, lay.dp ^ 1)
        to_y = take(buf, lay.dp ^ 2)
        own = take(buf, lay.dp)
        low = lay.flip_dp(far[:half], 2)
        high = lay.flip_dp(far[half:], 1)
        to_x = jnp.concatenate([add_low(to_x[:half], low), to_x[half:]], axis=0)
        to_y = jnp.concatenate([to_y[:half], add_low(to_y[half:], high)], axis=0)
        return add_low(own, lay.flip_dp(to_x, 1), lay.flip_dp(to_y, 2))
    parts = [take(buf, lay.dp)]
    for step in range(1, lay.ndp):
        parts.append(lay.shift_dp(take(buf, (lay.dp + step) % lay.ndp), step))
    return add_low(*parts)


def scatter_z(lay, buf):
    total = take(buf, lay.z).astype(F32)
    for step in range(1, lay.nz):
        total = total + lay.shift_z(take(buf, (lay.z + step) % lay.nz), step).astype(F32)
    return total


def attention_forward(queries, keys, values, allowed):
    scores = jnp.einsum("snihe,sjhe->snhij", queries, keys, preferred_element_type=F32) * SCALE
    probs = jax.nn.softmax(jnp.where(allowed, scores, MASKED), axis=-1)
    out = jnp.einsum("snhij,sjhe->snihe", probs.astype(BF), values, preferred_element_type=F32)
    return out.astype(BF), probs


def attention_back(queries, keys, values, probs, grad_out):
    grad_probs = jnp.einsum("snihe,sjhe->snhij", grad_out, values, preferred_element_type=F32)
    grad_values = jnp.einsum(
        "snhij,snihe->sjhe", probs.astype(BF), grad_out, preferred_element_type=F32
    )
    grad_scores = (
        probs * (grad_probs - jnp.sum(probs * grad_probs, axis=-1, keepdims=True))
    ).astype(BF)
    grad_queries = (
        jnp.einsum("snhij,sjhe->snihe", grad_scores, keys, preferred_element_type=F32) * SCALE
    )
    grad_keys = (
        jnp.einsum("snhij,snihe->sjhe", grad_scores, queries, preferred_element_type=F32) * SCALE
    )
    return grad_queries.astype(BF), grad_keys.astype(BF), grad_values.astype(BF)


def ngram_forward(dqkv, rel, tgt, onehot):
    q, k, v = dqkv[:, :, :, 0], dqkv[:, :, :, 1], dqkv[:, :, :, 2]
    positions = jnp.arange(LEN, dtype=jnp.int32)
    inside = positions[None, :] < tgt[:, None]
    main_valid = (positions[None, :] <= positions[:, None])[None] & inside[:, None]
    pred_valid = (positions[None, :] < positions[:, None])[None] & inside[:, None]
    valid = jnp.stack([main_valid] + [pred_valid] * NGRAM, axis=1)[:, :, None]
    main = jnp.einsum("snihe,sjhe->snhij", q, k[:, 0], preferred_element_type=F32) * SCALE
    main = main + jnp.einsum("snihk,ijk->snhij", rel, onehot, precision=lax.Precision.HIGHEST)
    main = jnp.where(valid, main, MASKED)
    own = jnp.einsum("snihe,snihe->snhi", q, k, preferred_element_type=F32) * SCALE
    own = own + jnp.transpose(rel[..., 0], (0, 1, 3, 2))
    stream = jnp.arange(STREAMS)[None, :, None, None]
    own = jnp.where(stream == 0, -jnp.inf, own)
    top = jnp.maximum(jnp.max(main, axis=-1), own)
    main = jnp.exp(main - top[..., None])
    own = jnp.exp(own - top)
    total = jnp.sum(main, axis=-1) + own
    main = main / total[..., None]
    own = own / total
    out = jnp.einsum("snhij,sjhe->snihe", main.astype(BF), v[:, 0], preferred_element_type=F32)
    own_low = jnp.transpose(own.astype(BF), (0, 1, 3, 2)).astype(F32)[..., None]
    out = out + own_low * v.astype(F32)
    return out.astype(BF), main, own


def ngram_back(dqkv, main, own, onehot, grad_out):
    q, k, v = dqkv[:, :, :, 0], dqkv[:, :, :, 1], dqkv[:, :, :, 2]
    grad_main = jnp.einsum("snihe,sjhe->snhij", grad_out, v[:, 0], preferred_element_type=F32)
    grad_own = jnp.einsum("snihe,snihe->snhi", grad_out, v, preferred_element_type=F32)
    inner = jnp.sum(main * grad_main, axis=-1) + own * grad_own
    ds = (main * (grad_main - inner[..., None])).astype(BF)
    ds_own = (own * (grad_own - inner)).astype(BF)
    own_rows = jnp.transpose(ds_own, (0, 1, 3, 2)).astype(F32)[..., None]
    p_rows = jnp.transpose(own.astype(BF), (0, 1, 3, 2)).astype(F32)[..., None]
    gq = (
        jnp.einsum("snhij,sjhe->snihe", ds, k[:, 0], preferred_element_type=F32)
        + own_rows * k.astype(F32)
    ) * SCALE
    gk0 = jnp.einsum("snhij,snihe->sjhe", ds, q, preferred_element_type=F32) * SCALE
    gv0 = jnp.einsum("snhij,snihe->sjhe", main.astype(BF), grad_out, preferred_element_type=F32)
    gk = own_rows * q.astype(F32) * SCALE
    gv = p_rows * grad_out.astype(F32)
    gk = jnp.concatenate([gk0[:, None], gk[:, 1:]], axis=1)
    gv = jnp.concatenate([gv0[:, None], gv[:, 1:]], axis=1)
    gqkv = jnp.stack([gq, gk, gv], axis=3).astype(BF)
    grel = jnp.einsum("snhij,ijk->snihk", ds, onehot.astype(BF), preferred_element_type=F32)
    first = (jnp.arange(BUCKETS) == 0).astype(F32)
    grel = (grel + own_rows * first).astype(BF)
    return gqkv, grel


def shards(
    ndp,
    nf,
    source,
    dec_in,
    src_lengths,
    tgt_lengths,
    enc_in_proj,
    enc_out_proj,
    enc_ffn_in,
    enc_ffn_out,
    enc_gains,
    enc_biases,
    dec_in_proj,
    dec_rel_proj,
    dec_out_proj,
    cross_query,
    cross_kv,
    cross_out,
    dec_ffn_in,
    dec_ffn_out,
    dec_gains,
    dec_biases,
    enc_cot,
    dec_cot,
):
    lay = Layout(ndp, nf)
    lay.place()
    r, f, chips = lay.r, lay.f, lay.chips
    swap, pick, pair = lay.swap, lay.pick, lay.pair
    core = lay.core

    def halves(matrix, groups, width):
        parts = matrix.reshape(r, groups, 2, width)
        return (
            pick(parts[:, :, 0], parts[:, :, 1]).reshape(r, groups * width),
            pick(parts[:, :, 1], parts[:, :, 0]).reshape(r, groups * width),
        )

    split = [
        halves(enc_in_proj, 3, HALF),
        halves(enc_ffn_in, chips, f),
        halves(dec_in_proj, 3, HALF),
        halves(cross_query, 1, HALF),
        halves(cross_kv, 2, HALF),
        halves(dec_ffn_in, chips, f),
        halves(dec_rel_proj, 1, REL_HALF),
    ]
    vec = jnp.concatenate(
        [
            enc_biases,
            enc_gains,
            dec_biases,
            dec_gains,
            src_lengths.astype(BF),
            tgt_lengths.astype(BF),
        ]
    )
    nvec = vec.shape[0]
    padded = -(-nvec // WIDE) * WIDE
    vec = jnp.pad(vec, (0, padded - nvec))
    mine = jnp.concatenate([own for own, other in split], axis=1)
    theirs = jnp.concatenate([other for own, other in split], axis=1)
    theirs_got = swap(theirs)
    vec_got = swap(vec)
    source_got = swap(source)
    dec_in_got = swap(dec_in.reshape(LEN * STREAMS, D))

    def owner_rows(start, width):
        return pair(mine[:, start : start + width], theirs_got[:, start : start + width], 0)

    def column_blocks(start, count):
        return [owner_rows(start + WIDE * i, WIDE) for i in range(count)]

    def row_blocks(matrix):
        return [matrix[:, :WIDE], matrix[:, WIDE:]]

    rel_start = mine.shape[1] - REL_HALF
    rel_own = mine[:, rel_start:]
    rel_other = theirs_got[:, rel_start:]
    vec_pair = pair(vec[None], vec_got[None], 0).reshape(-1, WIDE)
    vec_rows = -(-vec_pair.shape[0] // 16) * 16
    vec_used = vec_pair.shape[0]
    vec_pair = jnp.pad(vec_pair, ((0, vec_rows - vec_used), (0, 0)))
    wide_at = [0, 3 * WIDE, 7 * WIDE, 10 * WIDE, 11 * WIDE, 13 * WIDE]
    chunk_parts = [
        column_blocks(wide_at[0], 3) + row_blocks(enc_out_proj) + [vec_pair],
        column_blocks(wide_at[1], 4) + row_blocks(enc_ffn_out),
        column_blocks(wide_at[2], 3) + [pair(rel_own, rel_other, 1)] + row_blocks(dec_out_proj),
        column_blocks(wide_at[3], 1) + column_blocks(wide_at[4], 2) + row_blocks(cross_out),
        column_blocks(wide_at[5], 4) + row_blocks(dec_ffn_out),
    ]
    bufs = [jnp.concatenate(parts, axis=0) for parts in chunk_parts]
    full = gather_all(lay, bufs)

    def cut(index, block):
        parts = chunk_parts[index]
        at = sum(p.shape[0] for p in parts[:block])
        rows = parts[block].shape[0]
        return full[index][:, :, at : at + rows].reshape(chips * rows, WIDE)

    def columns(index, first, count):
        return jnp.concatenate([cut(index, first + i) for i in range(count)], axis=1)

    def head_rows(index, first):
        rows = columns(index, first, 2)
        low, high = rows[:HALF // 2], rows[HALF // 2 :]
        keep = pick(low, high).reshape(chips // 2, 1, r, D)
        got = swap(pick(high, low)).reshape(chips // 2, 1, r, D)
        return pair(keep, got, 1).reshape(HALF, D)

    w_enc_in = columns(0, 0, 3)
    w_enc_out = head_rows(0, 3)
    w_enc_up = columns(1, 0, 4)
    w_enc_down = columns(1, 4, 2)
    w_dec_in = columns(2, 0, 3)
    w_rel = (
        cut(2, 3)
        .reshape(chips, r, 2, REL_HALF)
        .transpose(0, 2, 1, 3)
        .reshape(D, REL_HALF)
    )
    w_dec_out = head_rows(2, 4)
    w_cross_q = columns(3, 0, 1)
    w_cross_kv = columns(3, 1, 2)
    w_cross_out = head_rows(3, 3)
    w_dec_up = columns(4, 0, 4)
    w_dec_down = columns(4, 4, 2)

    vec_all = (
        cut(0, 5).reshape(chips, vec_rows, WIDE)[:, :vec_used].reshape(lay.devices, padded).astype(F32)
    )
    widths = [enc_biases.shape[0], enc_gains.shape[0], dec_biases.shape[0], dec_gains.shape[0]]
    starts = [0]
    for width in widths:
        starts.append(starts[-1] + width)
    v_enc_b, v_enc_g, v_dec_b, v_dec_g = [
        vec_all[:, starts[i] : starts[i + 1]].reshape(-1) for i in range(4)
    ]
    ebias = slices_of(v_enc_b, ENC_WIDTHS)
    egain = slices_of(v_enc_g, (D, D))
    dbias = slices_of(v_dec_b, DEC_WIDTHS)
    dgain = slices_of(v_dec_g, (D, D, D))

    def half_of(vector):
        parts = vector.reshape(2, -1)
        return pick(parts[0], parts[1])

    def hidden_of(vector):
        parts = vector.reshape(chips, 2, f)
        return pick(parts[:, 0], parts[:, 1]).reshape(-1)

    zero_half = jnp.zeros((HALF,), F32)
    lens = jnp.stack([pair(vec[None], vec_got[None], 0)[:, nvec - 2 + i] for i in range(2)])
    lens = lens.astype(F32).astype(jnp.int32)
    src_len, tgt_len = lens[0], lens[1]
    positions = jnp.arange(LEN, dtype=jnp.int32)
    src_valid = (positions[None, :] < src_len[:, None])[:, None, None, None, :]
    onehot = bucket_table(LEN, BUCKETS)

    def both(partial):
        low = partial.astype(BF)
        return low.astype(F32) + swap(low).astype(F32)

    x = pair(source[None], source_got[None], 0).reshape(2 * LEN, D)
    qkv_bias = jnp.concatenate([half_of(ebias[0]), zero_half, half_of(ebias[1])])
    eqkv = (dot(x, w_enc_in) + qkv_bias).astype(BF).reshape(2, LEN, 3, OWN_HEADS, HEAD)
    eq, ek, ev = eqkv[:, None, :, 0], eqkv[:, :, 1], eqkv[:, :, 2]
    ea, eprobs = attention_forward(eq, ek, ev, src_valid)
    ea = ea.reshape(2 * LEN, HALF)
    ez1 = x.astype(F32) + both(dot(ea, w_enc_out)) + ebias[2]
    eh1 = norm(ez1, egain[0], ebias[5])
    eh1_low = eh1.astype(BF)
    eu = dot(eh1_low, w_enc_up) + hidden_of(ebias[3])
    eg = gelu_exact(eu).astype(BF)
    ez2 = eh1 + both(dot(eg, w_enc_down)) + ebias[4]
    enc = norm(ez2, egain[1], ebias[6])
    enc_low = enc.astype(BF)

    rows = 2 * STREAMS * LEN
    y = pair(
        dec_in.transpose(1, 0, 2)[None], dec_in_got.reshape(LEN, STREAMS, D).transpose(1, 0, 2)[None], 0
    ).reshape(rows, D)
    dqkv_bias = jnp.concatenate([half_of(dbias[0]), zero_half, half_of(dbias[1])])
    dqkv = (dot(y, w_dec_in) + dqkv_bias).astype(BF)
    dqkv = dqkv.reshape(2, STREAMS, LEN, 3, OWN_HEADS, HEAD)
    rel = (dot(y, w_rel) + half_of(dbias[2])).reshape(2, STREAMS, LEN, OWN_HEADS, BUCKETS)
    da, dmain, down = ngram_forward(dqkv, rel, tgt_len, onehot)
    da = da.reshape(rows, HALF)
    dz1 = y.astype(F32) + both(dot(da, w_dec_out)) + dbias[3]
    dh1 = norm(dz1, dgain[0], dbias[9])
    dh1_low = dh1.astype(BF)
    cq = (dot(dh1_low, w_cross_q) + half_of(dbias[4])).astype(BF)
    cq = cq.reshape(2, STREAMS, LEN, OWN_HEADS, HEAD)
    ckv = dot(enc_low, w_cross_kv) + jnp.concatenate([zero_half, half_of(dbias[5])])
    ckv = ckv.astype(BF).reshape(2, LEN, 2, OWN_HEADS, HEAD)
    ck, cv = ckv[:, :, 0], ckv[:, :, 1]
    ca, cprobs = attention_forward(cq, ck, cv, src_valid)
    ca = ca.reshape(rows, HALF)
    dz2 = dh1 + both(dot(ca, w_cross_out)) + dbias[6]
    dh2 = norm(dz2, dgain[1], dbias[10])
    dh2_low = dh2.astype(BF)
    du = dot(dh2_low, w_dec_up) + hidden_of(dbias[7])
    dg = gelu_exact(du).astype(BF)
    dz3 = dh2 + both(dot(dg, w_dec_down)) + dbias[8]
    dec = norm(dz3, dgain[2], dbias[11])

    def own_rows_of(total, count):
        blocks = total[: count * 2 * r].reshape(count, 2, r, WIDE)
        keep = pick(blocks[:, 0], blocks[:, 1])
        got = swap(pick(blocks[:, 1], blocks[:, 0]))
        return pair(keep[:, None], got[:, None], 1)

    def chip_blocks(grad):
        n = grad.shape[1] // WIDE
        shape = (lay.ndp, lay.nz, grad.shape[0] // chips, WIDE)
        low = grad.astype(BF)
        return [low[:, WIDE * i : WIDE * i + WIDE].reshape(shape) for i in range(n)]

    def head_blocks(grad):
        parts = grad.astype(BF).reshape(chips // 2, 2, r, D)
        keep = pick(parts[:, 0], parts[:, 1])
        got = swap(pick(parts[:, 1], parts[:, 0]))
        return chip_blocks(pair(keep, got, 0).reshape(chips * r, D))

    def scatter(parts, previous):
        buf = jnp.concatenate(parts, axis=2)
        if previous is not None:
            buf = tie(buf, previous)
        first = scatter_dp(lay, buf)
        return scatter_z(lay, first), first

    def split_rows(total, sizes):
        at = 0
        result = []
        for size in sizes:
            result.append(total[at : at + size])
            at += size
        return result

    dcot_got = swap(dec_cot.reshape(LEN * STREAMS, D)).reshape(LEN, STREAMS, D)
    dcot = pair(dec_cot.transpose(1, 0, 2)[None], dcot_got.transpose(1, 0, 2)[None], 0)
    dcot = dcot.reshape(rows, D).astype(F32)
    gz3, ggain3, gnorm3 = norm_back(dz3, dgain[2], dcot)
    gf = gz3.astype(BF)
    g_down = dot_g(dg, gf)
    gu = gelu_back(du, dot_t(gf, w_dec_down)).astype(BF)
    g_up = dot_g(dh2_low, gu)
    total4, first4 = scatter(chip_blocks(g_up) + chip_blocks(g_down), None)
    gz2, ggain2, gnorm2 = norm_back(dz2, dgain[1], gz3 + both(dot_t(gu, w_dec_up)))
    gx = gz2.astype(BF)
    g_cross_out = dot_g(ca, gx)
    gca = dot_t(gx, w_cross_out).astype(BF).reshape(2, STREAMS, LEN, OWN_HEADS, HEAD)
    gcq, gck, gcv = attention_back(cq, ck, cv, cprobs, gca)
    gcq = gcq.reshape(rows, HALF)
    gckv = jnp.stack([gck, gcv], axis=2).reshape(2 * LEN, D)
    g_cross_q = dot_g(dh1_low, gcq)
    g_cross_kv = dot_g(enc_low, gckv)
    total3, first3 = scatter(
        chip_blocks(g_cross_q) + chip_blocks(g_cross_kv) + head_blocks(g_cross_out), first4
    )
    ecot_got = swap(enc_cot)
    ecot = pair(enc_cot[None], ecot_got[None], 0).reshape(2 * LEN, D).astype(F32)
    genc = ecot + both(dot_t(gckv, w_cross_kv))
    gz1, ggain1, gnorm1 = norm_back(dz1, dgain[0], gz2 + both(dot_t(gcq, w_cross_q)))
    go = gz1.astype(BF)
    g_dec_out = dot_g(da, go)
    gda = dot_t(go, w_dec_out).astype(BF).reshape(2, STREAMS, LEN, OWN_HEADS, HEAD)
    gqkv, grel = ngram_back(dqkv, dmain, down, onehot, gda)
    gqkv = gqkv.reshape(rows, 3 * HALF)
    grel = grel.reshape(rows, REL_HALF)
    g_dec_in = dot_g(y, gqkv)
    g_rel = dot_g(y, grel)
    rel_block = (
        g_rel.astype(BF)
        .reshape(chips, 2, r, REL_HALF)
        .transpose(0, 2, 1, 3)
        .reshape(lay.ndp, lay.nz, r, WIDE)
    )
    total2, first2 = scatter(chip_blocks(g_dec_in) + [rel_block] + head_blocks(g_dec_out), first3)

    def own_sequence(partial, count):
        parts = partial.reshape(2, count, D)
        keep = pick(parts[0], parts[1])
        return keep + swap(pick(parts[1], parts[0]).astype(BF)).astype(F32)

    def own_part(values, count):
        parts = values.reshape(2, count, D)
        return pick(parts[0], parts[1])

    dec_rows = STREAMS * LEN
    g_dec_input = own_part(gz1, dec_rows) + own_sequence(
        dot_t(gqkv, w_dec_in) + dot_t(grel, w_rel), dec_rows
    )

    def widen(vector):
        zeros = jnp.zeros_like(vector)
        return pick(jnp.concatenate([vector, zeros]), jnp.concatenate([zeros, vector]))

    def widen_hidden(vector):
        parts = vector.reshape(chips, 1, f)
        zeros = jnp.zeros_like(parts)
        return pick(
            jnp.concatenate([parts, zeros], axis=1), jnp.concatenate([zeros, parts], axis=1)
        ).reshape(-1)

    column_sums = col_sum(gqkv)
    dec_vec = jnp.concatenate(
        [
            widen(column_sums[:HALF]),
            widen(column_sums[2 * HALF :]),
            widen(col_sum(grel)),
            0.5 * col_sum(go),
            widen(col_sum(gcq)),
            widen(col_sum(gckv)[HALF:]),
            0.5 * col_sum(gx),
            widen_hidden(col_sum(gu)),
            0.5 * col_sum(gf),
            0.5 * gnorm1,
            0.5 * gnorm2,
            0.5 * gnorm3,
            0.5 * ggain1,
            0.5 * ggain2,
            0.5 * ggain3,
        ]
    )

    gz2e, eggain2, egnorm2 = norm_back(ez2, egain[1], genc)
    gfe = gz2e.astype(BF)
    ge_down = dot_g(eg, gfe)
    gue = gelu_back(eu, dot_t(gfe, w_enc_down)).astype(BF)
    ge_up = dot_g(eh1_low, gue)
    total1, first1 = scatter(chip_blocks(ge_up) + chip_blocks(ge_down), first2)
    gz1e, eggain1, egnorm1 = norm_back(ez1, egain[0], gz2e + both(dot_t(gue, w_enc_up)))
    goe = gz1e.astype(BF)
    ge_out = dot_g(ea, goe)
    gae = dot_t(goe, w_enc_out).astype(BF).reshape(2, 1, LEN, OWN_HEADS, HEAD)
    geq, gek, gev = attention_back(eq, ek, ev, eprobs, gae)
    geqkv = jnp.stack([geq[:, 0], gek, gev], axis=2).reshape(2 * LEN, 3 * HALF)
    ge_in = dot_g(x, geqkv)
    total0, first0 = scatter(chip_blocks(ge_in) + head_blocks(ge_out), first1)
    g_source = own_part(gz1e, LEN) + own_sequence(dot_t(geqkv, w_enc_in), LEN)
    ecolumn_sums = col_sum(geqkv)
    enc_vec = jnp.concatenate(
        [
            widen(ecolumn_sums[:HALF]),
            widen(ecolumn_sums[2 * HALF :]),
            0.5 * col_sum(goe),
            widen_hidden(col_sum(gue)),
            0.5 * col_sum(gfe),
            0.5 * egnorm1,
            0.5 * egnorm2,
            0.5 * eggain1,
            0.5 * eggain2,
        ]
    )
    me = lay.dp * lay.nf + lax.axis_index("fsdp")

    def own_slice(vector):
        return take(vector.reshape(lay.devices, -1), me)

    dec_vec = lax.psum(dec_vec, ("dp", "fsdp"))
    enc_vec = lax.psum(enc_vec, ("dp", "fsdp"))
    nb = sum(ENC_WIDTHS)
    g_enc_biases, g_enc_gains = own_slice(enc_vec[:nb]), own_slice(enc_vec[nb:])
    nb = sum(DEC_WIDTHS)
    g_dec_biases, g_dec_gains = own_slice(dec_vec[:nb]), own_slice(dec_vec[nb:])

    def in_rows(blocks):
        return blocks.transpose(2, 0, 1, 3).reshape(r, -1)

    def up_rows(blocks):
        per = WIDE // f
        return blocks.reshape(4, 2, r, per, f).transpose(2, 0, 3, 1, 4).reshape(r, FF)

    def side(low, high):
        return jnp.concatenate([low, high], axis=1)

    t0 = split_rows(total0, [6 * r, r, r])
    o_enc_in, o_enc_out = in_rows(own_rows_of(t0[0], 3)), side(t0[1], t0[2])
    t1 = split_rows(total1, [8 * r, f, f])
    o_enc_up, o_enc_down = up_rows(own_rows_of(t1[0], 4)), side(t1[1], t1[2])
    t2 = split_rows(total2, [6 * r, r, r, r])
    o_dec_in, o_dec_out = in_rows(own_rows_of(t2[0], 3)), side(t2[2], t2[3])
    relp = t2[1].reshape(r, 2, REL_HALF)
    rel_keep = pick(relp[:, 0], relp[:, 1])
    o_rel = pair(rel_keep, swap(pick(relp[:, 1], relp[:, 0])), 1)
    t3 = split_rows(total3, [2 * r, 4 * r, r, r])
    o_cross_q = in_rows(own_rows_of(t3[0], 1))
    o_cross_kv = in_rows(own_rows_of(t3[1], 2))
    o_cross_out = side(t3[2], t3[3])
    t4 = split_rows(total4, [8 * r, f, f])
    o_dec_up, o_dec_down = up_rows(own_rows_of(t4[0], 4)), side(t4[1], t4[2])

    return (
        own_part(enc_low, LEN),
        own_part(dec.astype(BF), dec_rows).reshape(STREAMS, LEN, D).transpose(1, 0, 2),
        g_source,
        g_dec_input.reshape(STREAMS, LEN, D).transpose(1, 0, 2),
        o_enc_in,
        o_enc_out,
        o_enc_up,
        o_enc_down,
        g_enc_gains,
        g_enc_biases,
        o_dec_in,
        o_rel,
        o_dec_out,
        o_cross_q,
        o_cross_kv,
        o_cross_out,
        o_dec_up,
        o_dec_down,
        g_dec_gains,
        g_dec_biases,
    )


def solution(mesh):
    ndp, nf = mesh.shape["dp"], mesh.shape["fsdp"]
    whole = ("dp", "fsdp")
    one, two, three = P(whole), P(whole, None), P(whole, None, None)
    args = (two, three, one, one) + (two,) * 4 + (one,) * 2 + (two,) * 8 + (one,) * 2 + (two, three)
    outs = (two, three, two, three) + (two,) * 4 + (one,) * 2 + (two,) * 8 + (one,) * 2

    def body(*arrays):
        return shards(ndp, nf, *arrays)

    return jax.shard_map(body, mesh=mesh, in_specs=args, out_specs=outs, check_vma=False)
```

time: 3060 us -> 1150 us (0.38)
  waiting for transfers between devices: 2520 us -> 276 us
  other arithmetic: 43.9 us -> 195 us
  starting transfers between devices: 1.17 us -> 136 us
  local copies, waits for them, and re-layouts: 194 us -> 321 us
  matrix products: 229 us -> 138 us
    reduce_scatter x9 -> x0, waiting for transfers between devices: 1470 us -> none  [the longest x1 187 us: shards(): lax.psum_scatter(enc_grads[3], ('dp', 'fsdp'), scatter_dimension=0, tiled...]
    all_gather x12 -> x0, waiting for transfers between devices: 627 us -> none  [the longest x1 76.7 us: shards(): lax.all_gather(enc_ffn_in, ('dp', 'fsdp'), axis=0, tiled=True)]
    unnamed x29 -> x1, waiting for transfers between devices: 417 us -> 0.02 us
    ppermute x0 -> x100, waiting for transfers between devices: none -> 276 us  [the longest x40 145 us: flip_dp(): return lax.ppermute(value, 'dp', [(i, i ^ mask) for i in range(self.ndp)])]
    ppermute x0 -> x100, starting transfers between devices: none -> 136 us  [the longest x30 85.7 us: shift_z(): lax.ppermute(value, 'fsdp', [(i, (i + 2 * step) % self.nf) for i in range...]
    dot_general x72 -> x56, matrix products: 229 us -> 138 us  [the longest x12 52.3 us: dot(): lax.dot_general(a, b, (((1,), (0,)), ((), ())), preferred_element_type=F32)]
    slice x16 -> x84, local copies, waits for them, and re-layouts: 5.2 us -> 65.1 us  [the longest x11 15.3 us: cut(): return full[index][:, :, at:at + rows].reshape(chips * rows, WIDE)]
    dynamic_update_slice x0 -> x45, local copies, waits for them, and re-layouts: none -> 52.6 us  [the longest x25 32.3 us: gather_dp_rest(): out = lax.dynamic_update_slice(out, part[None], (lay.dp ^ flip, at, 0, 0))]
  transfers between devices with their start and end apart: 25 -> 101, of which waited for: 23 -> 36; matrix products, arithmetic and copies ran while one was open for 9% -> 50% of each run, Pallas kernels for 0% -> 0%
where the time goes in v1:
time: 1150 us; the launch traced here: 1130 us
  local copies, waits for them, and re-layouts  321 us (28%)
  waiting for transfers between devices  276 us (24%)
  other arithmetic  195 us (17%)
  matrix products  138 us (12%)
  starting transfers between devices  136 us (12%)
  blocking collectives  46.1 us (4%)
  between operations  20.1 us (2%)
    ppermute x40, waiting for transfers between devices, flip_dp(): return lax.ppermute(value, 'dp', [(i, i ^ mask) for i in range(self.ndp)])  145 us
    ppermute x30, waiting for transfers between devices, shift_z(): lax.ppermute(value, 'fsdp', [(i, (i + 2 * step) % self.nf) for i in range...  125 us
    ppermute x30, starting transfers between devices, shift_z(): lax.ppermute(value, 'fsdp', [(i, (i + 2 * step) % self.nf) for i in range...  85.7 us
    unnamed x523, local copies, waits for them, and re-layouts  77.7 us
    dot_general x12, matrix products, dot(): lax.dot_general(a, b, (((1,), (0,)), ((), ())), preferred_element_type=F32)  52.3 us
    psum x1, blocking collectives, shards(): enc_vec = lax.psum(enc_vec, ('dp', 'fsdp'))  46.1 us
    ppermute x40, starting transfers between devices, flip_dp(): return lax.ppermute(value, 'dp', [(i, i ^ mask) for i in range(self.ndp)])  43.9 us
    unnamed x41, other arithmetic  40.5 us
  transfers between devices with their start and end apart: 101, of which 36 were waited for; matrix products, arithmetic and copies ran while one was open for 50% of the time, Pallas kernels for 0%

profile of v1, /device:TPU:0, one launch (start us, length us, event | category | flops | bytes accessed | tf_op | source)
XLA Modules:
  0.0 1131.6 jit_solution(15101725473254964751)
XLA Ops:
  94.0 20.6 %collective-permute-done.4 = bf16[272,512]{1,0:T(8,128)(2,1)} collective-permute-done((bf16[272,512]{1,0:T(8,128)(2,1)}, bf16[272,512]{1,0:T(8,128)(2,1)}, u32[]{:S(2)}, u32[]{:S(2)}) %collective-permute-start.4) | collective-permute-done | bytes 278560 | tf_op jit(solution)/shard_map/ppermute | solution.py:136
  135.3 13.5 %collective-permute-done.6 = bf16[4,272,512]{2,1,0:T(8,128)(2,1)S(1)} collective-permute-done((bf16[4,272,512]{2,1,0:T(8,128)(2,1)}, bf16[4,272,512]{2,1,0:T(8,128)(2,1)S(1)}, u32[]{:S(2)}, u32[]{:S(2)}) %collective-permute-start.6) | collective-permute-done | bytes 1114144 | tf_op jit(solution)/shard_map/ppermute | solution.py:141
  177.1 27.0 %collective-permute-done.8 = bf16[2,272,512]{2,1,0:T(8,128)(2,1)S(1)} collective-permute-done((bf16[2,272,512]{2,1,0:T(8,128)(2,1)S(1)}, bf16[2,272,512]{2,1,0:T(8,128)(2,1)S(1)}, u32[]{:S(2)}, u32[]{:S(2)}) %collective-permute-start.8) | collective-permute-done | bytes 557088 | tf_op jit(solution)/shard_map/ppermute | solution.py:141
  261.0 7.2 collective-permute-done.25
  286.3 8.1 collective-permute-done.39
  295.9 19.1 %collective-permute-done.40 = bf16[512,512]{1,0:T(8,128)(2,1)S(1)} collective-permute-done((bf16[512,512]{1,0:T(8,128)(2,1)}, bf16[512,512]{1,0:T(8,128)(2,1)S(1)}, u32[]{:S(2)}, u32[]{:S(2)}) %collective-permute-start.40) | collective-permute-done | bytes 524320 | tf_op jit(solution)/shard_map/ppermute | solution.py:136
  318.7 11.1 collective-permute-done.26
  340.2 6.9 reshape.1456
  406.8 7.6 multiply_convert_fusion.1
  429.4 26.4 %collective-permute-done.35 = bf16[2,256,512]{2,1,0:T(8,128)(2,1)S(1)} collective-permute-done((bf16[2,256,512]{2,1,0:T(8,128)(2,1)S(1)}, bf16[2,256,512]{2,1,0:T(8,128)(2,1)S(1)}, u32[]{:S(2)}, u32[]{:S(2)}) %collective-permute-start.35) | collective-permute-done | bytes 524320 | tf_op jit(solution)/shard_map/ppermute | solution.py:141
  522.7 20.8 %multiply_convert_fusion = (bf16[768,2048]{1,0:T(8,128)(2,1)S(1)}, f32[768,2048]{1,0:T(8,128)}, f32[768,2048]{1,0:T(8,128)}) fusion(f32[2048]{0:T(1024)S(1)} %bitcast.1086, bf16[1024,512]{1,0:T(8,128)(2,1)S(1)} %bitcast.1049, bf16[1024,512]{1,0:T(8,128)(2,1)S(1)} %bitcast.1051, bf16[1024,512]{1,0:T(8,128)(2,1)S(1)} %bitcast.1053, ...), kind=kOutput, calls=%fused_computation.5 | convolution fusion | flops 3345743872 | bytes 23091200 | tf_op jit(solution)/shard_map/dot_general | solution.py:67
  574.9 8.5 convert_reduce_fusion
  611.9 8.0 collective-permute-done.58
  764.5 11.4 %collective-permute-start.96 = (bf16[512,512]{1,0:T(8,128)(2,1)}, bf16[512,512]{1,0:T(8,128)(2,1)}, u32[]{:S(2)}, u32[]{:S(2)}) collective-permute-start(bf16[512,512]{1,0:T(8,128)(2,1)} %get-tuple-element.174), channel_id=1, source_target_pairs={{0,2},{1,3},{2,4},{3,5},{4,6},{5,7},{6,0},{7,1},{8,10},{9,11},{10,... | collective-permute-start | bytes 1572872 | tf_op jit(solution)/shard_map/ppermute | solution.py:136
  783.9 6.9 convert_element_type.1091
  832.8 15.0 %collective-permute-done.63 = bf16[4,256,512]{2,1,0:T(8,128)(2,1)S(1)} collective-permute-done((bf16[4,256,512]{2,1,0:T(8,128)(2,1)S(1)}, bf16[4,256,512]{2,1,0:T(8,128)(2,1)S(1)}, u32[]{:S(2)}, u32[]{:S(2)}) %collective-permute-start.63) | collective-permute-done | bytes 1048608 | tf_op jit(solution)/shard_map/ppermute | solution.py:141
  855.7 46.1 %psum.14 = f32[12288]{0:T(1024)S(1)} all-reduce(f32[12288]{0:T(1024)} %constant_dynamic-update-slice_fusion.73), channel_id=1, replica_groups=mesh['dp'=4,'fsdp'=8] {'dp','fsdp'}, use_global_device_ids=true, to_apply=%region_37.38 | all-reduce | flops 12288 | bytes 98304 | tf_op jit(solution)/shard_map/psum | solution.py:678
  928.4 11.7 %collective-permute-done.67 = bf16[4,288,512]{2,1,0:T(8,128)(2,1)} collective-permute-done((bf16[4,288,512]{2,1,0:T(8,128)(2,1)}, bf16[4,288,512]{2,1,0:T(8,128)(2,1)}, u32[]{:S(2)}, u32[]{:S(2)}) %collective-permute-start.67) | collective-permute-done | bytes 1179680 | tf_op jit(solution)/shard_map/ppermute | solution.py:141
  972.0 7.0 collective-permute-done.92
  1003.1 12.0 %collective-permute-done.87 = bf16[288,512]{1,0:T(8,128)(2,1)S(1)} collective-permute-done((bf16[288,512]{1,0:T(8,128)(2,1)S(1)}, bf16[288,512]{1,0:T(8,128)(2,1)S(1)}, u32[]{:S(2)}, u32[]{:S(2)}) %collective-permute-start.87) | collective-permute-done | bytes 294944 | tf_op jit(solution)/shard_map/ppermute | solution.py:136
  1016.1 14.7 %collective-permute-done.71 = bf16[4,512,512]{2,1,0:T(8,128)(2,1)} collective-permute-done((bf16[4,512,512]{2,1,0:T(8,128)(2,1)}, bf16[4,512,512]{2,1,0:T(8,128)(2,1)}, u32[]{:S(2)}, u32[]{:S(2)}) %collective-permute-start.71) | collective-permute-done | bytes 2097184 | tf_op jit(solution)/shard_map/ppermute | solution.py:141
  1066.6 14.8 %collective-permute-done.83 = bf16[512,512]{1,0:T(8,128)(2,1)} collective-permute-done((bf16[512,512]{1,0:T(8,128)(2,1)S(1)}, bf16[512,512]{1,0:T(8,128)(2,1)}, u32[]{:S(2)}, u32[]{:S(2)}) %collective-permute-start.83) | collective-permute-done | bytes 524320 | tf_op jit(solution)/shard_map/ppermute | solution.py:136
  1087.9 10.9 collective-permute-start.78
  1109.1 11.1 collective-permute-done.79
  (1213 shorter events, 765.1 us)
Async XLA Ops:
  7.2 912.2 %all-reduce.23.cloned.1.call-start = ((), (), s32[]{:S(2)}) async-start(), calls=%async_computation | async-start | bytes 147456 | tf_op jit(solution)/shard_map/psum | solution.py:677
  21.6 61.5 %collective-permute-start.20 = (bf16[384,1024]{1,0:T(8,128)(2,1)}, bf16[384,1024]{1,0:T(8,128)(2,1)S(1)}, u32[]{:S(2)}, u32[]{:S(2)}) collective-permute-start(bf16[384,1024]{1,0:T(8,128)(2,1)} %reshape.1321), channel_id=1, source_target_pairs={{0,1},{1,0},{2,3},{3,2},{4,5},{5,4},{6,7},{7,6},{8,9},{9,8},{10,11... | collective-permute-start | bytes 2359304 | tf_op jit(solution)/shard_map/ppermute | solution.py:133
  45.4 80.5 %collective-permute-start.12 = (bf16[512,512]{1,0:T(8,128)(2,1)}, bf16[512,512]{1,0:T(8,128)(2,1)}, u32[]{:S(2)}, u32[]{:S(2)}) collective-permute-start(bf16[512,512]{1,0:T(8,128)(2,1)} %constant_dynamic-update-slice_fusion.13), channel_id=1, source_target_pairs={{0,2},{1,3},{2,4},{3,5},{4,6},{5,7},{6,0},{7,1},{8,10},{9,11},{10,... | collective-permute-start | bytes 1572872 | tf_op jit(solution)/shard_map/ppermute | solution.py:136
  48.4 79.5 %collective-permute-start.13 = (bf16[512,512]{1,0:T(8,128)(2,1)}, bf16[512,512]{1,0:T(8,128)(2,1)}, u32[]{:S(2)}, u32[]{:S(2)}) collective-permute-start(bf16[512,512]{1,0:T(8,128)(2,1)} %constant_dynamic-update-slice_fusion.13), channel_id=1, source_target_pairs={{0,4},{1,5},{2,6},{3,7},{4,0},{5,1},{6,2},{7,3},{8,12},{9,13},{10,... | collective-permute-start | bytes 1572872 | tf_op jit(solution)/shard_map/ppermute | solution.py:136
  51.0 78.7 %collective-permute-start.14 = (bf16[512,512]{1,0:T(8,128)(2,1)}, bf16[512,512]{1,0:T(8,128)(2,1)}, u32[]{:S(2)}, u32[]{:S(2)}) collective-permute-start(bf16[512,512]{1,0:T(8,128)(2,1)} %constant_dynamic-update-slice_fusion.13), channel_id=1, source_target_pairs={{0,6},{1,7},{2,0},{3,1},{4,2},{5,3},{6,4},{7,5},{8,14},{9,15},{10,... | collective-permute-start | bytes 1572872 | tf_op jit(solution)/shard_map/ppermute | solution.py:136
  125.9 422.9 %collective-permute-start.48 = (bf16[384,1024]{1,0:T(8,128)(2,1)}, bf16[384,1024]{1,0:T(8,128)(2,1)}, u32[]{:S(2)}, u32[]{:S(2)}) collective-permute-start(bf16[384,1024]{1,0:T(8,128)(2,1)} %reshape.1352), channel_id=1, source_target_pairs={{0,1},{1,0},{2,3},{3,2},{4,5},{5,4},{6,7},{7,6},{8,9},{9,8},{10,11... | collective-permute-start | bytes 2359304 | tf_op jit(solution)/shard_map/ppermute | solution.py:133
  131.6 110.1 %collective-permute-start.15 = (bf16[4,512,512]{2,1,0:T(8,128)(2,1)}, bf16[4,512,512]{2,1,0:T(8,128)(2,1)}, u32[]{:S(2)}, u32[]{:S(2)}) collective-permute-start(bf16[4,512,512]{2,1,0:T(8,128)(2,1)} %bitcast_dynamic-update-slice_fusion.29), channel_id=1, source_target_pairs={{0,8},{8,0},{16,24},{24,16},{1,9},{9,1},{17,25},{25,17},{2,10},{10... | collective-permute-start | bytes 6291464 | tf_op jit(solution)/shard_map/ppermute | solution.py:141
  132.1 109.9 %collective-permute-start.16 = (bf16[4,512,512]{2,1,0:T(8,128)(2,1)}, bf16[4,512,512]{2,1,0:T(8,128)(2,1)}, u32[]{:S(2)}, u32[]{:S(2)}) collective-permute-start(bf16[4,512,512]{2,1,0:T(8,128)(2,1)} %bitcast_dynamic-update-slice_fusion.29), channel_id=1, source_target_pairs={{0,16},{8,24},{16,0},{24,8},{1,17},{9,25},{17,1},{25,9},{2,18},{10... | collective-permute-start | bytes 6291464 | tf_op jit(solution)/shard_map/ppermute | solution.py:141
  204.1 52.1 %collective-permute-start.24 = (bf16[4,288,512]{2,1,0:T(8,128)(2,1)}, bf16[4,288,512]{2,1,0:T(8,128)(2,1)}, u32[]{:S(2)}, u32[]{:S(2)}) collective-permute-start(bf16[4,288,512]{2,1,0:T(8,128)(2,1)} %bitcast_dynamic-update-slice_fusion.33), channel_id=1, source_target_pairs={{0,8},{8,0},{16,24},{24,16},{1,9},{9,1},{17,25},{25,17},{2,10},{10... | collective-permute-start | bytes 3538952 | tf_op jit(solution)/shard_map/ppermute | solution.py:141
  275.1 120.8 %collective-permute-start.17 = (bf16[2,512,512]{2,1,0:T(8,128)(2,1)}, bf16[2,512,512]{2,1,0:T(8,128)(2,1)}, u32[]{:S(2)}, u32[]{:S(2)}) collective-permute-start(bf16[2,512,512]{2,1,0:T(8,128)(2,1)} %slice.1363), channel_id=1, source_target_pairs={{0,16},{8,24},{16,0},{24,8},{1,17},{9,25},{17,1},{25,9},{2,18},{10... | collective-permute-start | bytes 3145736 | tf_op jit(solution)/shard_map/ppermute | solution.py:141
  294.3 104.8 %collective-permute-start.18 = (bf16[2,512,512]{2,1,0:T(8,128)(2,1)}, bf16[2,512,512]{2,1,0:T(8,128)(2,1)}, u32[]{:S(2)}, u32[]{:S(2)}) collective-permute-start(bf16[2,512,512]{2,1,0:T(8,128)(2,1)} %slice.1364), channel_id=1, source_target_pairs={{0,8},{8,0},{16,24},{24,16},{1,9},{9,1},{17,25},{25,17},{2,10},{10... | collective-permute-start | bytes 3145736 | tf_op jit(solution)/shard_map/ppermute | solution.py:141
  329.8 87.0 %collective-permute-start.33 = (bf16[4,256,512]{2,1,0:T(8,128)(2,1)}, bf16[4,256,512]{2,1,0:T(8,128)(2,1)}, u32[]{:S(2)}, u32[]{:S(2)}) collective-permute-start(bf16[4,256,512]{2,1,0:T(8,128)(2,1)} %bitcast_dynamic-update-slice_fusion.41), channel_id=1, source_target_pairs={{0,8},{8,0},{16,24},{24,16},{1,9},{9,1},{17,25},{25,17},{2,10},{10... | collective-permute-start | bytes 3145736 | tf_op jit(solution)/shard_map/ppermute | solution.py:141
  331.4 88.5 %collective-permute-start.34 = (bf16[4,256,512]{2,1,0:T(8,128)(2,1)}, bf16[4,256,512]{2,1,0:T(8,128)(2,1)}, u32[]{:S(2)}, u32[]{:S(2)}) collective-permute-start(bf16[4,256,512]{2,1,0:T(8,128)(2,1)} %bitcast_dynamic-update-slice_fusion.41), channel_id=1, source_target_pairs={{0,16},{8,24},{16,0},{24,8},{1,17},{9,25},{17,1},{25,9},{2,18},{10... | collective-permute-start | bytes 3145736 | tf_op jit(solution)/shard_map/ppermute | solution.py:141
  395.9 75.4 %collective-permute-start.42 = (bf16[4,512,512]{2,1,0:T(8,128)(2,1)S(1)}, bf16[4,512,512]{2,1,0:T(8,128)(2,1)}, u32[]{:S(2)}, u32[]{:S(2)}) collective-permute-start(bf16[4,512,512]{2,1,0:T(8,128)(2,1)S(1)} %copy-done.39), channel_id=1, source_target_pairs={{0,8},{8,0},{16,24},{24,16},{1,9},{9,1},{17,25},{25,17},{2,10},{10... | collective-permute-start | bytes 6291464 | tf_op jit(solution)/shard_map/ppermute | solution.py:141
  399.2 75.4 %collective-permute-start.43 = (bf16[4,512,512]{2,1,0:T(8,128)(2,1)S(1)}, bf16[4,512,512]{2,1,0:T(8,128)(2,1)}, u32[]{:S(2)}, u32[]{:S(2)}) collective-permute-start(bf16[4,512,512]{2,1,0:T(8,128)(2,1)S(1)} %copy-done.39), channel_id=1, source_target_pairs={{0,16},{8,24},{16,0},{24,8},{1,17},{9,25},{17,1},{25,9},{2,18},{10... | collective-permute-start | bytes 6291464 | tf_op jit(solution)/shard_map/ppermute | solution.py:141
  625.0 133.7 %collective-permute-start.59 = (bf16[4,512,512]{2,1,0:T(8,128)(2,1)}, bf16[4,512,512]{2,1,0:T(8,128)(2,1)}, u32[]{:S(2)}, u32[]{:S(2)}) collective-permute-start(bf16[4,512,512]{2,1,0:T(8,128)(2,1)} %pad_maximum_fusion.11), channel_id=1, source_target_pairs={{0,8},{8,0},{16,24},{24,16},{1,9},{9,1},{17,25},{25,17},{2,10},{10... | collective-permute-start | bytes 6291464 | tf_op jit(solution)/shard_map/ppermute | solution.py:141
  627.2 131.5 %collective-permute-start.61 = (bf16[4,512,512]{2,1,0:T(8,128)(2,1)}, bf16[4,512,512]{2,1,0:T(8,128)(2,1)}, u32[]{:S(2)}, u32[]{:S(2)}) collective-permute-start(bf16[4,512,512]{2,1,0:T(8,128)(2,1)} %pad_maximum_fusion.12), channel_id=1, source_target_pairs={{0,16},{8,24},{16,0},{24,8},{1,17},{9,25},{17,1},{25,9},{2,18},{10... | collective-permute-start | bytes 6291464 | tf_op jit(solution)/shard_map/ppermute | solution.py:141
  690.5 215.5 %collective-permute-start.55 = (bf16[8,32,1024]{2,1,0:T(8,128)(2,1)}, bf16[8,32,1024]{2,1,0:T(8,128)(2,1)}, u32[]{:S(2)}, u32[]{:S(2)}) collective-permute-start(bf16[8,32,1024]{2,1,0:T(8,128)(2,1)} %fusion.115), channel_id=1, source_target_pairs={{0,1},{1,0},{2,3},{3,2},{4,5},{5,4},{6,7},{7,6},{8,9},{9,8},{10,11... | collective-permute-start | bytes 1572872 | tf_op jit(solution)/shard_map/ppermute | solution.py:133
  764.5 157.8 %collective-permute-start.96 = (bf16[512,512]{1,0:T(8,128)(2,1)}, bf16[512,512]{1,0:T(8,128)(2,1)}, u32[]{:S(2)}, u32[]{:S(2)}) collective-permute-start(bf16[512,512]{1,0:T(8,128)(2,1)} %get-tuple-element.174), channel_id=1, source_target_pairs={{0,2},{1,3},{2,4},{3,5},{4,6},{5,7},{6,0},{7,1},{8,10},{9,11},{10,... | collective-permute-start | bytes 1572872 | tf_op jit(solution)/shard_map/ppermute | solution.py:136
  780.0 46.9 %collective-permute-start.56 = (bf16[8,32,1024]{2,1,0:T(8,128)(2,1)}, bf16[8,32,1024]{2,1,0:T(8,128)(2,1)}, u32[]{:S(2)}, u32[]{:S(2)}) collective-permute-start(bf16[8,32,1024]{2,1,0:T(8,128)(2,1)} %get-tuple-element.205), channel_id=1, source_target_pairs={{0,1},{1,0},{2,3},{3,2},{4,5},{5,4},{6,7},{7,6},{8,9},{9,8},{10,11... | collective-permute-start | bytes 1572872 | tf_op jit(solution)/shard_map/ppermute | solution.py:133
  827.0 95.3 %collective-permute-start.97 = (bf16[512,512]{1,0:T(8,128)(2,1)}, bf16[512,512]{1,0:T(8,128)(2,1)}, u32[]{:S(2)}, u32[]{:S(2)}) collective-permute-start(bf16[512,512]{1,0:T(8,128)(2,1)} %get-tuple-element.176), channel_id=1, source_target_pairs={{0,4},{1,5},{2,6},{3,7},{4,0},{5,1},{6,2},{7,3},{8,12},{9,13},{10,... | collective-permute-start | bytes 1572872 | tf_op jit(solution)/shard_map/ppermute | solution.py:136
  853.5 56.3 %collective-permute-start.66 = (bf16[2,288,512]{2,1,0:T(8,128)(2,1)}, bf16[2,288,512]{2,1,0:T(8,128)(2,1)}, u32[]{:S(2)}, u32[]{:S(2)}) collective-permute-start(bf16[2,288,512]{2,1,0:T(8,128)(2,1)} %get-tuple-element.120), channel_id=1, source_target_pairs={{0,16},{8,24},{16,0},{24,8},{1,17},{9,25},{17,1},{25,9},{2,18},{10... | collective-permute-start | bytes 1769480 | tf_op jit(solution)/shard_map/ppermute | solution.py:141
  854.6 55.2 %collective-permute-start.68 = (bf16[2,288,512]{2,1,0:T(8,128)(2,1)}, bf16[2,288,512]{2,1,0:T(8,128)(2,1)}, u32[]{:S(2)}, u32[]{:S(2)}) collective-permute-start(bf16[2,288,512]{2,1,0:T(8,128)(2,1)} %get-tuple-element.122), channel_id=1, source_target_pairs={{0,8},{8,0},{16,24},{24,16},{1,9},{9,1},{17,25},{25,17},{2,10},{10... | collective-permute-start | bytes 1769480 | tf_op jit(solution)/shard_map/ppermute | solution.py:141
  984.7 46.1 %collective-permute-start.71 = (bf16[4,512,512]{2,1,0:T(8,128)(2,1)}, bf16[4,512,512]{2,1,0:T(8,128)(2,1)}, u32[]{:S(2)}, u32[]{:S(2)}) collective-permute-start(bf16[4,512,512]{2,1,0:T(8,128)(2,1)} %pad_maximum_fusion.13), channel_id=1, source_target_pairs={{0,8},{8,0},{16,24},{24,16},{1,9},{9,1},{17,25},{25,17},{2,10},{10... | collective-permute-start | bytes 6291464 | tf_op jit(solution)/shard_map/ppermute | solution.py:141
  (312 other events, 4853.0 us)
Sparse Core Ops, SparseCore 0:
  756.7 130.9 all-reduce.22

commit v2 on v1

--- a/solution.py
+++ b/solution.py
@@ -3,6 +3,8 @@
 import jax
 import jax.numpy as jnp
 from jax import lax
+from jax.experimental import pallas as pl
+from jax.experimental.pallas import tpu as pltpu
 from jax.sharding import PartitionSpec as P
 
 D = 1024
@@ -731,6 +733,1385 @@
     )
 
 
+BUDGET = 58 * 1024 * 1024
+PIECES = 8
+
+
+def run(body, grid, ins, outs, scratch=()):
+    arrays = [a for a, s in ins]
+    return pl.pallas_call(
+        body,
+        grid=(grid,),
+        in_specs=[s for a, s in ins],
+        out_specs=[s for a, s in outs],
+        out_shape=[a for a, s in outs],
+        scratch_shapes=list(scratch),
+        compiler_params=pltpu.CompilerParams(vmem_limit_bytes=BUDGET),
+    )(*arrays)
+
+
+def full(array):
+    zeros = (0,) * array.ndim
+    return array, pl.BlockSpec(array.shape, lambda t: zeros, pipeline_mode=pl.Buffered(1))
+
+
+def small(array):
+    return array, pl.BlockSpec(memory_space=pltpu.SMEM)
+
+
+def out_full(shape, dtype):
+    zeros = (0,) * len(shape)
+    return jax.ShapeDtypeStruct(shape, dtype), pl.BlockSpec(shape, lambda t: zeros)
+
+
+def out_cols(rows, cols, dtype, index):
+    return (
+        jax.ShapeDtypeStruct((rows, cols), dtype),
+        pl.BlockSpec((rows, WIDE), lambda t: (0, index(t))),
+    )
+
+
+def in_cols(array, index, width=WIDE):
+    return array, pl.BlockSpec((array.shape[0], width), lambda t: (0, index(t)))
+
+
+def blocks(pieces, rows, index):
+    return [
+        (p, pl.BlockSpec((2, rows, WIDE), lambda t: (0, index(t), 0))) for p in pieces
+    ]
+
+
+def assemble(refs, scr, place):
+    dp, z = place[0], place[1]
+    for i in range(4):
+        for half in range(2):
+            for j in range(2):
+                step = 2 * half + j
+                scr[jnp.bitwise_xor(dp, i), jnp.bitwise_and(z - step, 3)] = refs[2 * i + half][j]
+
+
+def weight_scratch(rows, width=WIDE):
+    return pltpu.VMEM((4, 4, rows, width), BF)
+
+
+def matrix_of(scr):
+    a, b, c, d = scr.shape
+    return scr[...].reshape(a * b * c, d)
+
+
+def pick_matrix(parity):
+    i = lax.broadcasted_iota(jnp.int32, (HALF, HALF // 2), 0)
+    j = lax.broadcasted_iota(jnp.int32, (HALF, HALF // 2), 1)
+    from_row = ((j >> 5) << 6) + (parity << 5) + (j & 31)
+    return jnp.where(i == from_row, 1.0, 0.0).astype(BF)
+
+
+def head_masks():
+    lane = lax.broadcasted_iota(jnp.int32, (1, 128), 1)
+    first = jnp.where(lane < HEAD, 1.0, 0.0)
+    return first.astype(BF), (1.0 - first).astype(BF)
+
+
+def first_lanes(rows):
+    return lax.broadcasted_iota(jnp.int32, (rows, 128), 1) < HEAD
+
+
+def soft_rows(scores):
+    top = jnp.max(scores, axis=-1, keepdims=True)
+    raised = jnp.exp(scores - top)
+    return raised * (1.0 / jnp.sum(raised, axis=-1, keepdims=True))
+
+
+def masked_probs(queries, keys, count):
+    scores = dot_t(queries, keys) * SCALE
+    column = lax.broadcasted_iota(jnp.int32, scores.shape, 1)
+    return soft_rows(jnp.where(column < count, scores, MASKED))
+
+
+def attend(q, k, v, count):
+    rows = q.shape[0]
+    out = []
+    for mask in head_masks():
+        probs = masked_probs(q * mask, k, count).astype(BF)
+        out.append(dot(probs, v))
+    return jnp.where(first_lanes(rows), out[0], out[1]).astype(BF)
+
+
+def attend_back(q, k, v, g, count):
+    gq, gk, gv = [], 0.0, 0.0
+    for mask in head_masks():
+        qm, gm = q * mask, g * mask
+        probs = masked_probs(qm, k, count)
+        gp = dot_t(gm, v)
+        ds = (probs * (gp - jnp.sum(probs * gp, axis=-1, keepdims=True))).astype(BF)
+        gq.append(dot(ds, k))
+        gk = gk + dot_g(ds, qm)
+        gv = gv + dot_g(probs.astype(BF), gm)
+    gq = jnp.where(first_lanes(q.shape[0]), gq[0], gq[1]) * SCALE
+    return gq.astype(BF), (gk * SCALE).astype(BF), gv.astype(BF)
+
+
+def split_parity(heads, place, keep, send):
+    core = place[2]
+    keep[...] = dot(heads[...], pick_matrix(core)).astype(BF)
+    send[...] = dot(heads[...], pick_matrix(1 - core)).astype(BF)
+
+
+def join_parity(keep, got, place, heads):
+    core = place[2]
+    heads[...] = (
+        dot_t(keep[...], pick_matrix(core)) + dot_t(got[...], pick_matrix(1 - core))
+    ).astype(BF)
+
+
+def enc_attention(place, x, bias, pieces):
+    rows = x.shape[0]
+
+    def body(place, x, bias, *refs):
+        w, (qkv, keep, send, scr, heads) = refs[:PIECES], refs[PIECES:]
+        t = pl.program_id(0)
+        assemble(w, scr, place)
+        qkv[:, pl.ds(t * WIDE, WIDE)] = (dot(x[...], matrix_of(scr)) + bias[...]).astype(BF)
+
+        @pl.when(t == 2)
+        def _():
+            for s in range(2):
+                r = slice(s * LEN, s * LEN + LEN)
+                for j in range(4):
+                    c = [slice(HALF * i + 128 * j, HALF * i + 128 * j + 128) for i in range(3)]
+                    heads[r, c[0]] = attend(qkv[r, c[0]], qkv[r, c[1]], qkv[r, c[2]], place[3 + s])
+            split_parity(heads, place, keep, send)
+
+    return run(
+        body,
+        3,
+        [small(place), full(x), in_cols(bias, lambda t: t)] + blocks(pieces, 64, lambda t: t),
+        [
+            out_full((rows, 3 * HALF), BF),
+            out_full((rows, HALF // 2), BF),
+            out_full((rows, HALF // 2), BF),
+        ],
+        [weight_scratch(64), pltpu.VMEM((rows, HALF), BF)],
+    )
+
+
+def out_projection(place, keep, got, pieces):
+    rows = keep.shape[0]
+
+    def body(place, keep, got, *refs):
+        w, (out, scr) = refs[:PIECES], refs[PIECES:]
+        assemble(w, scr, place)
+        core = place[2]
+        mine = scr[pl.ds(2 * core, 2)].reshape(HALF // 2, WIDE)
+        theirs = scr[pl.ds(2 - 2 * core, 2)].reshape(HALF // 2, WIDE)
+        out[...] = (dot(keep[...], mine) + dot(got[...], theirs)).astype(BF)
+
+    return run(
+        body,
+        2,
+        [small(place), full(keep), full(got)] + blocks(pieces, 32, lambda t: 6 + t),
+        [out_cols(rows, D, BF, lambda t: t)],
+        [weight_scratch(32)],
+    )[0]
+
+
+def stats(v):
+    centered = v - jnp.mean(v, axis=-1, keepdims=True)
+    inverse = lax.rsqrt(jnp.mean(centered * centered, axis=-1, keepdims=True) + EPSILON)
+    return centered * inverse, inverse
+
+
+def each_tile(rows, tile, step):
+    def loop(m, carry):
+        step(pl.multiple_of(m * tile, tile))
+        return carry
+
+    lax.fori_loop(0, rows // tile, loop, 0)
+
+
+def norm_tiles(rows, base, affine, own, other, bias, gain, shift, unit_out, inv_out, low_out, at=0):
+    def step(r):
+        here = pl.ds(r, LEN)
+        v = base[here].astype(F32)
+        if affine is not None:
+            v = v * affine[0] + affine[1]
+        there = pl.ds(r + at, LEN)
+        v = v + (own[there].astype(F32) + other[there].astype(F32)) + bias
+        unit, inverse = stats(v)
+        unit_out[here] = unit
+        inv_out[here] = jnp.broadcast_to(inverse, (LEN, 128))
+        low_out[here] = (unit * gain + shift).astype(BF)
+
+    each_tile(rows, LEN, step)
+
+
+ROOT_HALF = math.sqrt(0.5)
+ROOT_TWO_PI = math.sqrt(0.5 / math.pi)
+
+
+def gelu_pair(u):
+    phi = 0.5 + 0.5 * lax.erf(u * ROOT_HALF)
+    return u * phi, phi + u * (jnp.exp(-0.5 * u * u) * ROOT_TWO_PI)
+
+
+def ffn_forward(place, base, affine, own, other, vecs, hidden_bias, pieces):
+    rows = base.shape[0]
+    hidden = hidden_bias.shape[1]
+    ups = hidden // WIDE
+    tile = 256
+
+    def body(place, base, own, other, vecs, hb, *refs):
+        wu, wd = refs[:PIECES], refs[PIECES : 2 * PIECES]
+        unit, inv, low, g, gp, part, scr_u, scr_d, acts = refs[2 * PIECES :]
+        t = pl.program_id(0)
+
+        @pl.when(t == 0)
+        def _():
+            aff = (vecs[0:1], vecs[1:2]) if affine else None
+            norm_tiles(
+                rows, base, aff, own, other, vecs[2:3], vecs[3:4], vecs[4:5], unit, inv, low
+            )
+
+        @pl.when(t < ups)
+        def _():
+            assemble(wu, scr_u, place)
+            w = matrix_of(scr_u)
+
+            def step(r):
+                here = pl.ds(r, tile)
+                a, b = gelu_pair(dot(low[here], w) + hb[...])
+                a = a.astype(BF)
+                g[here] = a
+                acts[here, pl.ds(t * WIDE, WIDE)] = a
+                gp[here] = b.astype(BF)
+
+            each_tile(rows, tile, step)
+
+        @pl.when(t >= ups)
+        def _():
+            assemble(wd, scr_d, place)
+            part[...] = dot(acts[...], matrix_of(scr_d)).astype(BF)
+
+    up = lambda t: jnp.minimum(t, ups - 1)
+    down = lambda t: jnp.maximum(t - ups, 0)
+    return run(
+        body,
+        ups + 2,
+        [small(place), full(base), full(own), full(other), full(vecs), in_cols(hidden_bias, up)]
+        + blocks(pieces, 64, up)
+        + blocks(pieces, 128, lambda t: 2 + down(t)),
+        [
+            out_full((rows, D), F32),
+            out_full((rows, 128), F32),
+            out_full((rows, D), BF),
+            out_cols(rows, hidden, BF, up),
+            out_cols(rows, hidden, BF, up),
+            out_cols(rows, D, BF, down),
+        ],
+        [weight_scratch(64), weight_scratch(128), pltpu.VMEM((rows, hidden), BF)],
+    )
+
+
+def distance_buckets(reverse):
+    row = lax.broadcasted_iota(jnp.int32, (128, 128), 0) & (BUCKETS - 1)
+    lane = lax.broadcasted_iota(jnp.int32, (128, 128), 1)
+    distance = ((lane + 1) if reverse else (128 - lane)) & 127
+    bucket = jnp.zeros((128, 128), jnp.int32)
+    for target in range(1, BUCKETS):
+        at = 1
+        while bucket_value(at, BUCKETS) < target:
+            at += 1
+        bucket = bucket + jnp.where(distance >= at, 1, 0)
+    return jnp.where(bucket == row, 1.0, 0.0).astype(BF)
+
+
+def skew(values):
+    parts = [values[128 * n : 128 * n + 128] for n in range(values.shape[0] // 128)]
+    return jnp.concatenate(
+        [pltpu.roll(part, 0, 1, stride=1, stride_axis=0) for part in parts], axis=0
+    )
+
+
+def mirror():
+    row = lax.broadcasted_iota(jnp.int32, (128, 128), 0)
+    lane = lax.broadcasted_iota(jnp.int32, (128, 128), 1)
+    return jnp.where(row + lane == 127, 1.0, 0.0).astype(BF)
+
+
+def quarter_mask(h):
+    lane = lax.broadcasted_iota(jnp.int32, (1, 128), 1)
+    return jnp.where((lane >> 5) == h, 1.0, 0.0).astype(BF)
+
+
+def ngram_probs(qm, prod, k0, rel_high, rel_low, table, count, h, first):
+    mask = quarter_mask(h % 4)
+    turned = dot(rel_high * mask, table) + dot(rel_low * mask, table)
+    scores = dot_t(qm, k0) * SCALE + skew(turned)
+    row = lax.broadcasted_iota(jnp.int32, scores.shape, 0)
+    column = lax.broadcasted_iota(jnp.int32, scores.shape, 1)
+    token = row & (LEN - 1)
+    reach = jnp.where(row < LEN, token, token - 1)
+    scores = jnp.where((column <= reach) & (column < count), scores, MASKED)
+    own = jnp.sum(prod * first, axis=-1, keepdims=True) * SCALE + turned[:, 0:1]
+    main = lax.broadcasted_iota(jnp.int32, own.shape, 0) < LEN
+    own = jnp.where(main, 2.0 * MASKED, own)
+    top = jnp.maximum(jnp.max(scores, axis=-1, keepdims=True), own)
+    raised = jnp.exp(scores - top)
+    own = jnp.exp(own - top)
+    scale = 1.0 / (jnp.sum(raised, axis=-1, keepdims=True) + own)
+    return raised * scale, own * scale
+
+
+def split_high(values):
+    high = values.astype(BF)
+    return high, (values - high.astype(F32)).astype(BF)
+
+
+def half_rows(rows):
+    first = jnp.where(lax.broadcasted_iota(jnp.int32, (rows, 128), 1) < HEAD, 1.0, 0.0)
+    return first, 1.0 - first
+
+
+def ngram_attention(place, y, bias, rel_bias, pieces):
+    rows = y.shape[0]
+    span = STREAMS * LEN
+
+    def body(place, y, bias, rbias, *refs):
+        w, wr = refs[:PIECES], refs[PIECES : 2 * PIECES]
+        qkv, rel, keep, send, scr, scr_r, heads, table = refs[2 * PIECES :]
+        t = pl.program_id(0)
+
+        @pl.when(t < 3)
+        def _():
+            assemble(w, scr, place)
+            qkv[:, pl.ds(pl.multiple_of(t * WIDE, WIDE), WIDE)] = (
+                dot(y[...], matrix_of(scr)) + bias[...]
+            ).astype(BF)
+
+        @pl.when(t == 3)
+        def _():
+            assemble_rel(wr, scr_r, place)
+            rel[...] = dot(y[...], scr_r[...].reshape(D, REL_HALF)) + rbias[...]
+            table[...] = distance_buckets(False)
+            lanes = half_rows(span)
+
+            def step(s, carry):
+                r = pl.ds(pl.multiple_of(s * span, span), span)
+                r0 = pl.ds(pl.multiple_of(s * span, span), LEN)
+                count = place[5 + s]
+                for j in range(4):
+                    c = [slice(HALF * i + 128 * j, HALF * i + 128 * j + 128) for i in range(3)]
+                    q, k, v = qkv[r, c[0]], qkv[r, c[1]], qkv[r, c[2]]
+                    k0, v0 = qkv[r0, c[1]], qkv[r0, c[2]]
+                    high, low = split_high(rel[r, 128 * (j // 2) : 128 * (j // 2) + 128])
+                    prod = q.astype(F32) * k.astype(F32)
+                    out = []
+                    for i, mask in enumerate(head_masks()):
+                        probs, own = ngram_probs(
+                            q * mask, prod, k0, high, low, table[...], count, 2 * j + i, lanes[i]
+                        )
+                        own = own.astype(BF).astype(F32)
+                        out.append(dot(probs.astype(BF), v0) + own * v.astype(F32))
+                    heads[r, c[0]] = jnp.where(first_lanes(span), out[0], out[1]).astype(BF)
+                return carry
+
+            lax.fori_loop(0, 2, step, 0)
+            split_parity(heads, place, keep, send)
+
+    third = lambda t: jnp.minimum(t, 2)
+    return run(
+        body,
+        4,
+        [small(place), full(y), in_cols(bias, third), full(rel_bias)]
+        + blocks(pieces, 64, third)
+        + blocks(pieces, 32, lambda t: 8),
+        [
+            out_full((rows, 3 * HALF), BF),
+            out_full((rows, REL_HALF), F32),
+            out_full((rows, HALF // 2), BF),
+            out_full((rows, HALF // 2), BF),
+        ],
+        [
+            weight_scratch(64),
+            pltpu.VMEM((4, 4, 2, 32, REL_HALF), BF),
+            pltpu.VMEM((rows, HALF), BF),
+            pltpu.VMEM((128, 128), BF),
+        ],
+    )
+
+
+def assemble_rel(refs, scr, place):
+    dp, z = place[0], place[1]
+    for i in range(4):
+        for half in range(2):
+            for j in range(2):
+                block = refs[2 * i + half][j]
+                a, b = jnp.bitwise_xor(dp, i), jnp.bitwise_and(z - (2 * half + j), 3)
+                scr[a, b, 0] = block[:, :REL_HALF]
+                scr[a, b, 1] = block[:, REL_HALF:]
+
+
+def cross_forward(place, y, own, other, vecs, eunit, evecs, eown, eother, q_bias, kv_bias, pieces):
+    rows, mem = y.shape[0], eunit.shape[0]
+    span = STREAMS * LEN
+
+    def body(place, y, own, other, vecs, eunit, evecs, eown, eother, qb, kvb, *refs):
+        w = refs[:PIECES]
+        unit, inv, low, eunit2, einv2, elow, q, kv, keep, send, scr, heads = refs[PIECES:]
+        t = pl.program_id(0)
+        assemble(w, scr, place)
+
+        @pl.when(t == 0)
+        def _():
+            norm_tiles(
+                rows, y, None, own, other, vecs[0:1], vecs[1:2], vecs[2:3], unit, inv, low
+            )
+            norm_tiles(
+                mem,
+                eunit,
+                (evecs[0:1], evecs[1:2]),
+                eown,
+                eother,
+                evecs[2:3],
+                evecs[3:4],
+                evecs[4:5],
+                eunit2,
+                einv2,
+                elow,
+            )
+            q[...] = (dot(low[...], matrix_of(scr)) + qb[...]).astype(BF)
+
+        @pl.when(t > 0)
+        def _():
+            at = pl.multiple_of((t - 1) * WIDE, WIDE)
+            kv[:, pl.ds(at, WIDE)] = (dot(elow[...], matrix_of(scr)) + kvb[...]).astype(BF)
+
+        @pl.when(t == 2)
+        def _():
+            for s in range(2):
+                r = slice(s * span, s * span + span)
+                m = slice(s * LEN, s * LEN + LEN)
+                for j in range(4):
+                    c = slice(128 * j, 128 * j + 128)
+                    c2 = slice(HALF + 128 * j, HALF + 128 * j + 128)
+                    heads[r, c] = attend(q[r, c], kv[m, c], kv[m, c2], place[3 + s])
+            split_parity(heads, place, keep, send)
+
+    return run(
+        body,
+        3,
+        [small(place)]
+        + [full(a) for a in (y, own, other, vecs, eunit, evecs, eown, eother, q_bias)]
+        + [in_cols(kv_bias, lambda t: jnp.maximum(t - 1, 0))]
+        + blocks(pieces, 64, lambda t: t),
+        [
+            out_full((rows, D), F32),
+            out_full((rows, 128), F32),
+            out_full((rows, D), BF),
+            out_full((mem, D), F32),
+            out_full((mem, 128), F32),
+            out_full((mem, D), BF),
+            out_full((rows, HALF), BF),
+            out_full((mem, D), BF),
+            out_full((rows, HALF // 2), BF),
+            out_full((rows, HALF // 2), BF),
+        ],
+        [weight_scratch(64), pltpu.VMEM((rows, HALF), BF)],
+    )
+
+
+def fold(values):
+    return jnp.sum(values.reshape(values.shape[0] // 8, 8, values.shape[1]), axis=0)
+
+
+def norm_back_tile(total, unit, inverse, gain):
+    scaled = total * gain
+    one = jnp.mean(scaled, axis=-1, keepdims=True)
+    two = jnp.mean(scaled * unit, axis=-1, keepdims=True)
+    return inverse * (scaled - one - unit * two)
+
+
+def ffn_back(place, final, total_ins, unit_ins, vecs, gp, pieces):
+    rows, hidden = gp.shape
+    ups = hidden // WIDE
+    n_total, n_unit = len(total_ins), len(unit_ins)
+    mine = rows // 2
+
+    def body(place, vecs, gp, *refs):
+        at = 0
+
+        def take_refs(n):
+            nonlocal at
+            at += n
+            return refs[at - n : at]
+
+        tot, uni = take_refs(n_total), take_refs(n_unit)
+        wu, wd = take_refs(PIECES), take_refs(PIECES)
+        outs = take_refs(1) if final else ()
+        gz, gf, gu, part, s_gain, s_shift, s_gf, s_gu = take_refs(8)
+        scr_u, scr_d, all_u, scr_all_u, acc = refs[at:]
+        t = pl.program_id(0)
+
+        @pl.when(t == 0)
+        def _():
+            acc[...] = jnp.zeros_like(acc)
+
+            def step(r):
+                here = pl.ds(r, LEN)
+                if final:
+                    v = uni[0][here] * vecs[0:1] + vecs[1:2]
+                    v = v + (uni[1][here].astype(F32) + uni[2][here].astype(F32)) + vecs[2:3]
+                    unit, inverse = stats(v)
+
+                    @pl.when((r >= mine) == (place[2] == 1))
+                    def _():
+                        to = pl.ds(pl.multiple_of(r - mine * place[2], LEN), LEN)
+                        outs[0][to] = (unit * vecs[3:4] + vecs[4:5]).astype(BF)
+
+                else:
+                    unit, inverse = uni[0][here], uni[1][here, 0:1]
+                total = tot[0][here].astype(F32)
+                if n_total > 1:
+                    there = pl.ds(r + tot[1].shape[0] - rows, LEN)
+                    total = total + (tot[1][there].astype(F32) + tot[2][there].astype(F32))
+                acc[0:8] += fold(total * unit)
+                acc[8:16] += fold(total)
+                back = norm_back_tile(total, unit, inverse, vecs[3:4])
+                gz[here] = back
+                low = back.astype(BF)
+                gf[here] = low
+                acc[16:24] += fold(low.astype(F32))
+
+            each_tile(rows, LEN, step)
+            s_gain[...] = jnp.sum(acc[0:8], axis=0, keepdims=True)
+            s_shift[...] = jnp.sum(acc[8:16], axis=0, keepdims=True)
+            s_gf[...] = jnp.sum(acc[16:24], axis=0, keepdims=True)
+
+        @pl.when(t < 2)
+        def _():
+            assemble(wd, scr_d.at[t], place)
+
+        @pl.when(t >= 2)
+        def _():
+            b = t - 2
+            assemble(wu, scr_u, place)
+            scr_all_u[:, pl.ds(pl.multiple_of(b * WIDE, WIDE), WIDE)] = matrix_of(scr_u)
+            w0 = scr_d[0, b].reshape(WIDE, WIDE)
+            w1 = scr_d[1, b].reshape(WIDE, WIDE)
+            back = dot_t(gf[:, :WIDE], w0) + dot_t(gf[:, WIDE:], w1)
+            low = (back * gp[...].astype(F32)).astype(BF)
+            gu[...] = low
+            all_u[:, pl.ds(pl.multiple_of(b * WIDE, WIDE), WIDE)] = low
+            s_gu[...] = jnp.sum(fold(low.astype(F32)), axis=0, keepdims=True)
+
+        @pl.when(t == ups + 1)
+        def _():
+            part[...] = dot_t(all_u[...], scr_all_u[...]).astype(BF)
+
+    up = lambda t: jnp.maximum(t - 2, 0)
+    down = lambda t: jnp.minimum(t, 1)
+    outs = [out_full((mine, D), BF)] if final else []
+    outs += [
+        out_full((rows, D), F32),
+        out_full((rows, D), BF),
+        out_cols(rows, hidden, BF, up),
+        out_full((rows, D), BF),
+        out_full((1, D), F32),
+        out_full((1, D), F32),
+        out_full((1, D), F32),
+        out_cols(1, hidden, F32, up),
+    ]
+    return run(
+        body,
+        ups + 2,
+        [small(place), full(vecs), in_cols(gp, up)]
+        + [full(a) for a in total_ins]
+        + [full(a) for a in unit_ins]
+        + blocks(pieces, 64, up)
+        + blocks(pieces, 128, lambda t: 2 + down(t)),
+        outs,
+        [
+            weight_scratch(64),
+            pltpu.VMEM((2, 4, 4, 128, WIDE), BF),
+            pltpu.VMEM((rows, hidden), BF),
+            pltpu.VMEM((D, hidden), BF),
+            pltpu.VMEM((24, D), F32),
+        ],
+    )
+
+
+def branch_back(place, resid, own, other, unit, inv, gain, pieces):
+    rows = resid.shape[0]
+
+    def body(place, resid, own, other, unit, inv, gain, *refs):
+        w = refs[:PIECES]
+        gz, gx, keep, send, s_gain, s_shift, s_gx, scr, total_out, acc = refs[PIECES:]
+        t = pl.program_id(0)
+        assemble(w, scr, place)
+
+        @pl.when(t == 0)
+        def _():
+            acc[...] = jnp.zeros_like(acc)
+
+            def step(r):
+                here = pl.ds(r, LEN)
+                total = resid[here] + (own[here].astype(F32) + other[here].astype(F32))
+                acc[0:8] += fold(total * unit[here])
+                acc[8:16] += fold(total)
+                back = norm_back_tile(total, unit[here], inv[here, 0:1], gain[...])
+                gz[here] = back
+                low = back.astype(BF)
+                gx[here] = low
+                acc[16:24] += fold(low.astype(F32))
+
+            each_tile(rows, LEN, step)
+            s_gain[...] = jnp.sum(acc[0:8], axis=0, keepdims=True)
+            s_shift[...] = jnp.sum(acc[8:16], axis=0, keepdims=True)
+            s_gx[...] = jnp.sum(acc[16:24], axis=0, keepdims=True)
+            total_out[...] = dot_t(gx[:, :WIDE], matrix_of(scr))
+
+        @pl.when(t == 1)
+        def _():
+            total_out[...] += dot_t(gx[:, WIDE:], matrix_of(scr))
+            core = place[2]
+            quarter = HALF // 2
+            keep[...] = total_out[:, pl.ds(pl.multiple_of(quarter * core, 128), quarter)].astype(BF)
+            send[...] = total_out[
+                :, pl.ds(pl.multiple_of(quarter * (1 - core), 128), quarter)
+            ].astype(BF)
+
+    return run(
+        body,
+        2,
+        [small(place)]
+        + [full(a) for a in (resid, own, other, unit, inv, gain)]
+        + blocks(pieces, 32, lambda t: 6 + t),
+        [
+            out_full((rows, D), F32),
+            out_full((rows, D), BF),
+            out_full((rows, HALF // 2), BF),
+            out_full((rows, HALF // 2), BF),
+            out_full((1, D), F32),
+            out_full((1, D), F32),
+            out_full((1, D), F32),
+        ],
+        [weight_scratch(32), pltpu.VMEM((rows, HALF), F32), pltpu.VMEM((24, D), F32)],
+    )
+
+
+def column_sums(out, values):
+    out[...] = jnp.sum(fold(values.astype(F32)), axis=0, keepdims=True)
+
+
+def cross_back(place, q, kv, keep, got, pieces):
+    rows, mem = q.shape[0], kv.shape[0]
+    span = STREAMS * LEN
+
+    def body(place, q, kv, keep, got, *refs):
+        w = refs[:PIECES]
+        gq, gkv, part, s_gq, s_gkv, scr, g, acc = refs[PIECES:]
+        t = pl.program_id(0)
+        assemble(w, scr, place)
+
+        @pl.when(t == 0)
+        def _():
+            join_parity(keep, got, place, g)
+            for s in range(2):
+                r = slice(s * span, s * span + span)
+                m = slice(s * LEN, s * LEN + LEN)
+                for j in range(4):
+                    c = slice(128 * j, 128 * j + 128)
+                    c2 = slice(HALF + 128 * j, HALF + 128 * j + 128)
+                    gq[r, c], gkv[m, c], gkv[m, c2] = attend_back(
+                        q[r, c], kv[m, c], kv[m, c2], g[r, c], place[3 + s]
+                    )
+            column_sums(s_gq, gq[...])
+            column_sums(s_gkv, gkv[...])
+            part[:rows] = dot_t(gq[...], matrix_of(scr)).astype(BF)
+
+        @pl.when(t == 1)
+        def _():
+            acc[...] = dot_t(gkv[:, :HALF], matrix_of(scr))
+
+        @pl.when(t == 2)
+        def _():
+            part[rows:] = (acc[...] + dot_t(gkv[:, HALF:], matrix_of(scr))).astype(BF)
+
+    return run(
+        body,
+        3,
+        [small(place), full(q), full(kv), full(keep), full(got)]
+        + blocks(pieces, 64, lambda t: t),
+        [
+            out_full((rows, HALF), BF),
+            out_full((mem, D), BF),
+            out_full((rows + mem, D), BF),
+            out_full((1, HALF), F32),
+            out_full((1, D), F32),
+        ],
+        [weight_scratch(64), pltpu.VMEM((rows, HALF), BF), pltpu.VMEM((mem, D), F32)],
+    )
+
+
+def input_grads(place, gz, parts, keep, send):
+    rows = gz.shape[0] // 2
+    core = place[2]
+    here = pl.ds(pl.multiple_of(rows * core, LEN), rows)
+    there = pl.ds(pl.multiple_of(rows * (1 - core), LEN), rows)
+    total = gz[here]
+    for g, w in parts:
+        total = total + dot_t(g[here], w)
+    keep[...] = total
+    total = 0.0
+    for g, w in parts:
+        total = total + dot_t(g[there], w)
+    send[...] = total.astype(BF)
+
+
+def enc_attention_back(place, qkv, keep, got, gz, pieces):
+    rows = qkv.shape[0]
+
+    def body(place, qkv, keep, got, gz, *refs):
+        w = refs[:PIECES]
+        gqkv, out, send, sums, scr, g, win = refs[PIECES:]
+        t = pl.program_id(0)
+        assemble(w, scr, place)
+        win[:, pl.ds(pl.multiple_of(t * WIDE, WIDE), WIDE)] = matrix_of(scr)
+
+        @pl.when(t == 0)
+        def _():
+            join_parity(keep, got, place, g)
+            for s in range(2):
+                r = slice(s * LEN, s * LEN + LEN)
+                for j in range(4):
+                    c = [slice(HALF * i + 128 * j, HALF * i + 128 * j + 128) for i in range(3)]
+                    gqkv[r, c[0]], gqkv[r, c[1]], gqkv[r, c[2]] = attend_back(
+                        qkv[r, c[0]], qkv[r, c[1]], qkv[r, c[2]], g[r, c[0]], place[3 + s]
+                    )
+            column_sums(sums, gqkv[...])
+
+        @pl.when(t == 2)
+        def _():
+            input_grads(place, gz, [(gqkv, win[...])], out, send)
+
+    return run(
+        body,
+        3,
+        [small(place), full(qkv), full(keep), full(got), full(gz)]
+        + blocks(pieces, 64, lambda t: t),
+        [
+            out_full((rows, 3 * HALF), BF),
+            out_full((rows // 2, D), F32),
+            out_full((rows // 2, D), BF),
+            out_full((1, 3 * HALF), F32),
+        ],
+        [weight_scratch(64), pltpu.VMEM((rows, HALF), BF), pltpu.VMEM((D, 3 * HALF), BF)],
+    )
+
+
+def ngram_back_kernel(place, qkv, rel, keep, got, gz, pieces):
+    rows = qkv.shape[0]
+    span = STREAMS * LEN
+
+    def body(place, qkv, rel, keep, got, gz, *refs):
+        w, wr = refs[:PIECES], refs[PIECES : 2 * PIECES]
+        gqkv, grel, out, send, sums, s_rel, scr, scr_r, g, win, *tables = refs[2 * PIECES :]
+        table, table_back, flip = tables
+        t = pl.program_id(0)
+
+        @pl.when(t < 3)
+        def _():
+            assemble(w, scr, place)
+            win[:, pl.ds(pl.multiple_of(t * WIDE, WIDE), WIDE)] = matrix_of(scr)
+
+        @pl.when(t == 0)
+        def _():
+            join_parity(keep, got, place, g)
+            table[...] = distance_buckets(False)
+            table_back[...] = distance_buckets(True)
+            flip[...] = mirror()
+            lanes = half_rows(span)
+
+            def step(s, carry):
+                r = pl.ds(pl.multiple_of(s * span, span), span)
+                r0 = pl.ds(pl.multiple_of(s * span, span), LEN)
+                r1 = pl.ds(pl.multiple_of(s * span + LEN, LEN), span - LEN)
+                count = place[5 + s]
+                for j in range(4):
+                    c = [slice(HALF * i + 128 * j, HALF * i + 128 * j + 128) for i in range(3)]
+                    q, k, v = qkv[r, c[0]], qkv[r, c[1]], qkv[r, c[2]]
+                    k0, v0 = qkv[r0, c[1]], qkv[r0, c[2]]
+                    go = g[r, c[0]]
+                    high, low = split_high(rel[r, 128 * (j // 2) : 128 * (j // 2) + 128])
+                    prod = q.astype(F32) * k.astype(F32)
+                    prod_g = go.astype(F32) * v.astype(F32)
+                    gq, gk0, gv0, p_own, d_own, turned = [], 0.0, 0.0, [], [], []
+                    for i, mask in enumerate(head_masks()):
+                        qm, gm = q * mask, go * mask
+                        h = 2 * j + i
+                        probs, own = ngram_probs(
+                            qm, prod, k0, high, low, table[...], count, h, lanes[i]
+                        )
+                        gp = dot_t(gm, v0)
+                        g_own = jnp.sum(prod_g * lanes[i], axis=-1, keepdims=True)
+                        inner = jnp.sum(probs * gp, axis=-1, keepdims=True) + own * g_own
+                        ds = (probs * (gp - inner)).astype(BF)
+                        ds_own = (own * (g_own - inner)).astype(BF).astype(F32)
+                        gq.append(dot(ds, k0))
+                        gk0 = gk0 + dot_g(ds, qm)
+                        gv0 = gv0 + dot_g(probs.astype(BF), gm)
+                        p_own.append(own.astype(BF).astype(F32))
+                        d_own.append(ds_own)
+                        back = skew(dot(ds, flip[...]))
+                        lane = lax.broadcasted_iota(jnp.int32, back.shape, 1)
+                        main = lax.broadcasted_iota(jnp.int32, back.shape, 0) < LEN
+                        back = jnp.where((lane == 127) & jnp.logical_not(main), ds_own, back)
+                        grads = dot_t(back.astype(BF), table_back[...])
+                        turned.append(grads * quarter_mask(h % 4).astype(F32))
+                    first = first_lanes(span)
+                    d_own = jnp.where(first, d_own[0], d_own[1])
+                    p_own = jnp.where(first, p_own[0], p_own[1])
+                    gqf = jnp.where(first, gq[0], gq[1]) + d_own * k.astype(F32)
+                    gqkv[r, c[0]] = (gqf * SCALE).astype(BF)
+                    gkn = d_own * q.astype(F32) * SCALE
+                    gvn = p_own * go.astype(F32)
+                    gqkv[r0, c[1]] = (gk0 * SCALE).astype(BF)
+                    gqkv[r0, c[2]] = gv0.astype(BF)
+                    gqkv[r1, c[1]] = gkn[LEN:].astype(BF)
+                    gqkv[r1, c[2]] = gvn[LEN:].astype(BF)
+                    both = turned[0] + turned[1]
+                    at = slice(128 * (j // 2), 128 * (j // 2) + 128)
+                    if j % 2 == 0:
+                        held = both
+                    else:
+                        grel[r, at] = (held + both).astype(BF)
+                return carry
+
+            lax.fori_loop(0, 2, step, 0)
+            column_sums(sums, gqkv[...])
+            column_sums(s_rel, grel[...])
+
+        @pl.when(t == 3)
+        def _():
+            assemble_rel(wr, scr_r, place)
+            wrel = scr_r[...].reshape(D, REL_HALF)
+            input_grads(place, gz, [(gqkv, win[...]), (grel, wrel)], out, send)
+
+    third = lambda t: jnp.minimum(t, 2)
+    return run(
+        body,
+        4,
+        [small(place), full(qkv), full(rel), full(keep), full(got), full(gz)]
+        + blocks(pieces, 64, third)
+        + blocks(pieces, 32, lambda t: 8),
+        [
+            out_full((rows, 3 * HALF), BF),
+            out_full((rows, REL_HALF), BF),
+            out_full((rows // 2, D), F32),
+            out_full((rows // 2, D), BF),
+            out_full((1, 3 * HALF), F32),
+            out_full((1, REL_HALF), F32),
+        ],
+        [
+            weight_scratch(64),
+            pltpu.VMEM((4, 4, 2, 32, REL_HALF), BF),
+            pltpu.VMEM((rows, HALF), BF),
+            pltpu.VMEM((D, 3 * HALF), BF),
+        ]
+        + [pltpu.VMEM((128, 128), BF)] * 3,
+    )
+
+
+def grad_chunk(place, arrays, terms, total_rows):
+    n = len(arrays)
+
+    def body(place, *refs):
+        ins, outs, scr = refs[:n], refs[n : n + 7], refs[n + 7]
+        t = pl.program_id(0)
+        dp, z, core = place[0], place[1], place[2]
+
+        def spread(value, at, rows):
+            v = value.astype(BF).reshape(4, 4, rows, WIDE)
+            scr[:, :, :rows] = v
+            for i in range(4):
+                for step in range(4):
+                    block = scr[jnp.bitwise_xor(dp, i), jnp.bitwise_and(z + step, 3), :rows]
+                    if i == 0:
+                        outs[0][step, at : at + rows] = block
+                    else:
+                        outs[2 * i - 1 + step // 2][step % 2, at : at + rows] = block
+
+        for index, (kind, at, x, g, col) in enumerate(terms):
+
+            @pl.when(t == index)
+            def _(kind=kind, at=at, x=x, g=g, col=col):
+                if kind == "whole":
+                    spread(ins[x][...], at, ins[x].shape[0] // 16)
+                    return
+                if kind == "heads":
+                    right = ins[g][:, col : col + WIDE]
+                    mine, theirs = ins[x][...], ins[x + 1][...]
+                    keep, got = dot_g(mine, right), dot_g(theirs, right)
+                    quarter = (2, 4, 32, WIDE)
+                    scr[pl.ds(2 * core, 2), :, :32] = keep.astype(BF).reshape(quarter)
+                    scr[pl.ds(2 - 2 * core, 2), :, :32] = got.astype(BF).reshape(quarter)
+                    spread(scr[:, :, :32], at, 32)
+                    return
+                if kind == "rel":
+                    v = dot_g(ins[x][...], ins[g][...]).astype(BF).reshape(16, 2, 32, REL_HALF)
+                    spread(jnp.concatenate([v[:, 0], v[:, 1]], axis=-1), at, 32)
+                    return
+                value = dot_g(ins[x][...], ins[g][:, col : col + WIDE])
+                spread(value, at, value.shape[0] // 16)
+
+    shape = (2, total_rows, WIDE)
+    return run(
+        body,
+        len(terms),
+        [small(place)] + [full(a) for a in arrays],
+        [out_full((4, total_rows, WIDE), BF)] + [out_full(shape, BF)] * 6,
+        [weight_scratch(128)],
+    )
+
+
+def vec_chunk(place, pieces):
+    def body(place, *refs):
+        assemble(refs[:PIECES], refs[PIECES], place)
+
+    return run(
+        body,
+        1,
+        [small(place)] + blocks(pieces, 16, lambda t: 18),
+        [out_full((4, 4, 16, WIDE), BF)],
+    )[0]
+
+
+def gather_pieces(lay, buf):
+    got = [buf] + [lay.shift_z(buf, step) for step in range(1, 4)]
+    low = jnp.stack(got[:2])
+    high = jnp.stack(got[2:])
+    x_low, y_low = lay.flip_dp(low, 1), lay.flip_dp(low, 2)
+    x_high, y_high = lay.flip_dp(high, 1), lay.flip_dp(high, 2)
+    d_low = lay.flip_dp(x_low, 2)
+    d_high = lay.flip_dp(y_high, 1)
+    return [low, high, x_low, x_high, y_low, y_high, d_low, d_high]
+
+
+def scatter_pieces(lay, parts):
+    own, x_low, x_high, y_low, y_high, d_low, d_high = parts
+    d_low = lay.flip_dp(d_low, 2)
+    d_high = lay.flip_dp(d_high, 1)
+    x_high = lay.flip_dp(x_high, 1)
+    y_low = lay.flip_dp(y_low, 2)
+    x_low = lay.flip_dp(add_low(x_low, d_low), 1)
+    y_high = lay.flip_dp(add_low(y_high, d_high), 2)
+    sides = [(x_low, y_low, 0), (x_low, y_low, 1), (x_high, y_high, 0), (x_high, y_high, 1)]
+    sums = [add_low(own[s], x[i], y[i]) for s, (x, y, i) in enumerate(sides)]
+    total = sums[0].astype(F32)
+    for step in range(1, 4):
+        total = total + lay.shift_z(sums[step], step).astype(F32)
+    return total
+
+
+def shards_fast(
+    ndp,
+    nf,
+    source,
+    dec_in,
+    src_lengths,
+    tgt_lengths,
+    enc_in_proj,
+    enc_out_proj,
+    enc_ffn_in,
+    enc_ffn_out,
+    enc_gains,
+    enc_biases,
+    dec_in_proj,
+    dec_rel_proj,
+    dec_out_proj,
+    cross_query,
+    cross_kv,
+    cross_out,
+    dec_ffn_in,
+    dec_ffn_out,
+    dec_gains,
+    dec_biases,
+    enc_cot,
+    dec_cot,
+):
+    lay = Layout(ndp, nf)
+    lay.place()
+    r, f, chips = lay.r, lay.f, lay.chips
+    swap, pick, pair = lay.swap, lay.pick, lay.pair
+    core = lay.core
+    dec_rows = STREAMS * LEN
+
+    def halves(matrix, groups, width):
+        parts = matrix.reshape(r, groups, 2, width)
+        return (
+            pick(parts[:, :, 0], parts[:, :, 1]).reshape(r, groups * width),
+            pick(parts[:, :, 1], parts[:, :, 0]).reshape(r, groups * width),
+        )
+
+    split = [
+        halves(enc_in_proj, 3, HALF),
+        halves(enc_ffn_in, chips, f),
+        halves(dec_in_proj, 3, HALF),
+        halves(cross_query, 1, HALF),
+        halves(cross_kv, 2, HALF),
+        halves(dec_ffn_in, chips, f),
+        halves(dec_rel_proj, 1, REL_HALF),
+    ]
+    vec = jnp.concatenate(
+        [
+            enc_biases,
+            enc_gains,
+            dec_biases,
+            dec_gains,
+            src_lengths.astype(BF),
+            tgt_lengths.astype(BF),
+        ]
+    )
+    nvec = vec.shape[0]
+    padded = -(-nvec // WIDE) * WIDE
+    vec = jnp.pad(vec, (0, padded - nvec))
+    mine = jnp.concatenate([own for own, other in split], axis=1)
+    theirs = jnp.concatenate([other for own, other in split], axis=1)
+    theirs_got = swap(theirs)
+    vec_got = swap(vec)
+    source_got = swap(source)
+    dec_own = dec_in.transpose(1, 0, 2).reshape(dec_rows, D)
+    dec_got = swap(dec_own)
+
+    def column_blocks(start, count):
+        return [
+            pair(
+                mine[:, start + WIDE * i : start + WIDE * i + WIDE],
+                theirs_got[:, start + WIDE * i : start + WIDE * i + WIDE],
+                0,
+            )
+            for i in range(count)
+        ]
+
+    def row_blocks(matrix):
+        return [matrix[:, :WIDE], matrix[:, WIDE:]]
+
+    rel_start = mine.shape[1] - REL_HALF
+    rel_block = pair(mine[:, rel_start:], theirs_got[:, rel_start:], 1)
+    vec_pair = pair(vec[None], vec_got[None], 0)
+    vec_used = 2 * padded // WIDE
+    vec_block = jnp.pad(vec_pair.reshape(vec_used, WIDE), ((0, 16 - vec_used), (0, 0)))
+    at = [0, 3 * WIDE, 7 * WIDE, 10 * WIDE, 11 * WIDE, 13 * WIDE]
+    chunk_parts = {
+        "enc": column_blocks(at[0], 3) + row_blocks(enc_out_proj),
+        "enc_ffn": column_blocks(at[1], 4) + row_blocks(enc_ffn_out),
+        "dec": column_blocks(at[2], 3) + row_blocks(dec_out_proj) + [rel_block, vec_block],
+        "cross": column_blocks(at[3], 1) + column_blocks(at[4], 2) + row_blocks(cross_out),
+        "dec_ffn": column_blocks(at[5], 4) + row_blocks(dec_ffn_out),
+    }
+    w = {}
+    order = ["dec", "enc", "enc_ffn", "cross", "dec_ffn"]
+    for i, name in enumerate(order):
+        buf = jnp.concatenate(chunk_parts[name], axis=0)
+        if i >= 2:
+            buf = tie(buf, *w[order[i - 2]][2:4])
+        w[name] = gather_pieces(lay, buf)
+
+    lens = vec_pair[:, nvec - 2 :].T.reshape(-1).astype(F32).astype(jnp.int32)
+    place = jnp.concatenate(
+        [jnp.stack([lay.dp, lay.z, core]).astype(jnp.int32), lens, jnp.zeros((1,), jnp.int32)]
+    )
+
+    vec_all = vec_chunk(place, w["dec"]).reshape(chips, 16, WIDE)[:, :vec_used]
+    vec_all = vec_all.reshape(lay.devices, padded).astype(F32)
+    widths = [enc_biases.shape[0], enc_gains.shape[0], dec_biases.shape[0], dec_gains.shape[0]]
+    starts = [0]
+    for width in widths:
+        starts.append(starts[-1] + width)
+    v_enc_b, v_enc_g, v_dec_b, v_dec_g = [
+        vec_all[:, starts[i] : starts[i + 1]].reshape(-1) for i in range(4)
+    ]
+    eb, eg_rows = v_enc_b.reshape(-1, D), v_enc_g.reshape(2, D)
+    dg_rows = v_dec_g.reshape(3, D)
+    d_split = 2 * D + HEADS * BUCKETS
+    db = v_dec_b[d_split:].reshape(-1, D)
+
+    def half_of(vector):
+        parts = vector.reshape(2, -1)
+        return pick(parts[0], parts[1])
+
+    def hidden_of(vector):
+        parts = vector.reshape(chips, 2, f)
+        return pick(parts[:, 0], parts[:, 1]).reshape(1, -1)
+
+    zero_half = jnp.zeros((HALF,), F32)
+
+    def qkv_bias(q, v):
+        return jnp.concatenate([half_of(q), zero_half, half_of(v)])[None]
+
+    def rows_of(*vectors):
+        return jnp.stack(vectors)
+
+    x = pair(source, source_got, 0)
+    y = pair(dec_own, dec_got, 0)
+    dqkv, rel, da_keep, da_send = ngram_attention(
+        place,
+        y,
+        qkv_bias(v_dec_b[:D], v_dec_b[D : 2 * D]),
+        half_of(v_dec_b[2 * D : d_split])[None],
+        w["dec"],
+    )
+    da_got = swap(da_send)
+    p3 = out_projection(place, da_keep, da_got, w["dec"])
+    p3_got = swap(p3)
+    eqkv, ea_keep, ea_send = enc_attention(place, x, qkv_bias(eb[0], eb[1]), w["enc"])
+    ea_got = swap(ea_send)
+    p1 = out_projection(place, ea_keep, ea_got, w["enc"])
+    p1_got = swap(p1)
+    eunit1, einv1, eh1_low, eg, egp, p2 = ffn_forward(
+        place,
+        x,
+        False,
+        p1,
+        p1_got,
+        rows_of(eb[2], eb[2], eb[2], eg_rows[0], eb[8]),
+        hidden_of(eb[3:7]),
+        w["enc_ffn"],
+    )
+    p2_got = swap(p2)
+    dunit1, dinv1, dh1_low, eunit2, einv2, enc_low, cq, ckv, ca_keep, ca_send = cross_forward(
+        place,
+        y,
+        p3,
+        p3_got,
+        rows_of(db[0], dg_rows[0], db[9]),
+        eunit1,
+        rows_of(eg_rows[0], eb[8], eb[7], eg_rows[1], eb[9]),
+        p2,
+        p2_got,
+        half_of(db[1])[None],
+        jnp.concatenate([zero_half, half_of(db[2])])[None],
+        w["cross"],
+    )
+    ca_got = swap(ca_send)
+    p4 = out_projection(place, ca_keep, ca_got, w["cross"])
+    p4_got = swap(p4)
+    dunit2, dinv2, dh2_low, dg, dgp, p5 = ffn_forward(
+        place,
+        dunit1,
+        True,
+        p4,
+        p4_got,
+        rows_of(dg_rows[0], db[9], db[3], dg_rows[1], db[10]),
+        hidden_of(db[4:8]),
+        w["dec_ffn"],
+    )
+    p5_got = swap(p5)
+
+    dcot_own = dec_cot.transpose(1, 0, 2).reshape(dec_rows, D)
+    dcot = pair(dcot_own, swap(dcot_own), 0)
+    ecot = pair(enc_cot, swap(enc_cot), 0)
+    dec_out, gz3, gf, gu, p6, s_gain3, s_shift3, s_gf, s_gu = ffn_back(
+        place,
+        True,
+        [dcot],
+        [dunit2, p5, p5_got],
+        rows_of(dg_rows[1], db[10], db[8], dg_rows[2], db[11]),
+        dgp,
+        w["dec_ffn"],
+    )
+    p6_got = swap(p6)
+    up_terms = [("plain", 64 * b, 0, 1, WIDE * b) for b in range(4)]
+    down_terms = [("plain", 256 + 128 * h, 2, 3, WIDE * h) for h in range(2)]
+    total4 = scatter_pieces(
+        lay, grad_chunk(place, [dh2_low, gu, dg, gf], up_terms + down_terms, 512)
+    )
+    gz2, gx, gca_keep, gca_send, s_gain2, s_shift2, s_gx = branch_back(
+        place, gz3, p6, p6_got, dunit2, dinv2, dg_rows[1:2], w["cross"]
+    )
+    gca_got = swap(gca_send)
+    gcq, gckv, p7, s_gcq, s_gckv = cross_back(place, cq, ckv, gca_keep, gca_got, w["cross"])
+    p7_got = swap(p7)
+    total3 = scatter_pieces(
+        lay,
+        grad_chunk(
+            place,
+            [dh1_low, gcq, enc_low, gckv, ca_keep, ca_got, gx],
+            [
+                ("plain", 0, 0, 1, 0),
+                ("plain", 64, 2, 3, 0),
+                ("plain", 128, 2, 3, WIDE),
+                ("heads", 192, 4, 6, 0),
+                ("heads", 224, 4, 6, WIDE),
+            ],
+            256,
+        ),
+    )
+    gz1, go, gda_keep, gda_send, s_gain1, s_shift1, s_go = branch_back(
+        place, gz2, p7, p7_got, dunit1, dinv1, dg_rows[0:1], w["dec"]
+    )
+    gda_got = swap(gda_send)
+    gqkv, grel, p8, p8_send, s_gqkv, s_grel = ngram_back_kernel(
+        place, dqkv, rel, gda_keep, gda_got, gz1, w["dec"]
+    )
+    p8_got = swap(p8_send)
+    total2 = scatter_pieces(
+        lay,
+        grad_chunk(
+            place,
+            [y, gqkv, da_keep, da_got, go, grel],
+            [("plain", 64 * b, 0, 1, WIDE * b) for b in range(3)]
+            + [("heads", 192, 2, 4, 0), ("heads", 224, 2, 4, WIDE), ("rel", 256, 0, 5, 0)],
+            288,
+        ),
+    )
+    gz2e, gfe, gue, p9, e_gain2, e_shift2, s_gfe, s_gue = ffn_back(
+        place,
+        False,
+        [ecot, p7, p7_got],
+        [eunit2, einv2],
+        rows_of(*([eg_rows[1]] * 5)),
+        egp,
+        w["enc_ffn"],
+    )
+    p9_got = swap(p9)
+    total1 = scatter_pieces(
+        lay, grad_chunk(place, [eh1_low, gue, eg, gfe], up_terms + down_terms, 512)
+    )
+    gz1e, goe, gea_keep, gea_send, e_gain1, e_shift1, s_goe = branch_back(
+        place, gz2e, p9, p9_got, eunit1, einv1, eg_rows[0:1], w["enc"]
+    )
+    gea_got = swap(gea_send)
+    geqkv, p10, p10_send, s_geqkv = enc_attention_back(
+        place, eqkv, gea_keep, gea_got, gz1e, w["enc"]
+    )
+    p10_got = swap(p10_send)
+
+    def widen(vector):
+        zeros = jnp.zeros_like(vector)
+        return pick(jnp.concatenate([vector, zeros]), jnp.concatenate([zeros, vector]))
+
+    def widen_hidden(vector):
+        parts = vector.reshape(chips, 1, f)
+        zeros = jnp.zeros_like(parts)
+        return pick(
+            jnp.concatenate([parts, zeros], axis=1), jnp.concatenate([zeros, parts], axis=1)
+        ).reshape(-1)
+
+    def owned(*vectors):
+        return jnp.concatenate(vectors).reshape(lay.devices, -1)
+
+    vec_grads = jnp.concatenate(
+        [
+            owned(
+                widen(s_geqkv[0, :HALF]),
+                widen(s_geqkv[0, 2 * HALF :]),
+                0.5 * s_goe[0],
+                widen_hidden(s_gue),
+                0.5 * s_gfe[0],
+                0.5 * e_shift1[0],
+                0.5 * e_shift2[0],
+            ),
+            owned(0.5 * e_gain1[0], 0.5 * e_gain2[0]),
+            owned(
+                widen(s_gqkv[0, :HALF]),
+                widen(s_gqkv[0, 2 * HALF :]),
+                widen(s_grel[0]),
+                0.5 * s_go[0],
+                widen(s_gcq[0]),
+                widen(s_gckv[0, HALF:]),
+                0.5 * s_gx[0],
+                widen_hidden(s_gu),
+                0.5 * s_gf[0],
+                0.5 * s_shift1[0],
+                0.5 * s_shift2[0],
+                0.5 * s_shift3[0],
+            ),
+            owned(0.5 * s_gain1[0], 0.5 * s_gain2[0], 0.5 * s_gain3[0]),
+        ],
+        axis=1,
+    ).astype(BF)
+    vec_width = vec_grads.shape[1]
+    vec_grads = jnp.pad(vec_grads, ((0, 0), (0, padded - vec_width)))
+    vec_grads = vec_grads.reshape(chips, vec_used, WIDE)
+    vec_grads = jnp.pad(vec_grads, ((0, 0), (0, 16 - vec_used), (0, 0))).reshape(chips * 16, WIDE)
+    total0 = scatter_pieces(
+        lay,
+        grad_chunk(
+            place,
+            [x, geqkv, ea_keep, ea_got, goe, vec_grads],
+            [("plain", 64 * b, 0, 1, WIDE * b) for b in range(3)]
+            + [("heads", 192, 2, 4, 0), ("heads", 224, 2, 4, WIDE), ("whole", 256, 5, 5, 0)],
+            272,
+        ),
+    )
+
+    def split_rows(total, sizes):
+        at = 0
+        result = []
+        for size in sizes:
+            result.append(total[at : at + size])
+            at += size
+        return result
+
+    def own_rows_of(total, count):
+        rows = total.reshape(count, 2, r, WIDE)
+        keep = pick(rows[:, 0], rows[:, 1])
+        got = swap(pick(rows[:, 1], rows[:, 0]))
+        return pair(keep[:, None], got[:, None], 1)
+
+    def in_rows(rows):
+        return rows.transpose(2, 0, 1, 3).reshape(r, -1)
+
+    def up_rows(rows):
+        per = WIDE // f
+        return rows.reshape(4, 2, r, per, f).transpose(2, 0, 3, 1, 4).reshape(r, FF)
+
+    def side(low, high):
+        return jnp.concatenate([low, high], axis=1)
+
+    t0 = split_rows(total0, [6 * r, r, r, 16])
+    o_enc_in, o_enc_out = in_rows(own_rows_of(t0[0], 3)), side(t0[1], t0[2])
+    vec_sum = t0[3][:vec_used].reshape(2, padded)
+    vec_sum = pick(vec_sum[0], vec_sum[1]) + swap(pick(vec_sum[1], vec_sum[0]))
+    o_vec = [vec_sum[starts[i] : starts[i + 1]] for i in range(4)]
+    t1 = split_rows(total1, [8 * r, f, f])
+    o_enc_up, o_enc_down = up_rows(own_rows_of(t1[0], 4)), side(t1[1], t1[2])
+    t2 = split_rows(total2, [6 * r, r, r, r])
+    o_dec_in, o_dec_out = in_rows(own_rows_of(t2[0], 3)), side(t2[1], t2[2])
+    relp = t2[3].reshape(r, 2, REL_HALF)
+    o_rel = pair(pick(relp[:, 0], relp[:, 1]), swap(pick(relp[:, 1], relp[:, 0])), 1)
+    t3 = split_rows(total3, [2 * r, 4 * r, r, r])
+    o_cross_q = in_rows(own_rows_of(t3[0], 1))
+    o_cross_kv = in_rows(own_rows_of(t3[1], 2))
+    o_cross_out = side(t3[2], t3[3])
+    t4 = split_rows(total4, [8 * r, f, f])
+    o_dec_up, o_dec_down = up_rows(own_rows_of(t4[0], 4)), side(t4[1], t4[2])
+
+    return (
+        pick(enc_low[:LEN], enc_low[LEN:]),
+        dec_out.reshape(STREAMS, LEN, D).transpose(1, 0, 2),
+        p10 + p10_got.astype(F32),
+        (p8 + p8_got.astype(F32)).reshape(STREAMS, LEN, D).transpose(1, 0, 2),
+        o_enc_in,
+        o_enc_out,
+        o_enc_up,
+        o_enc_down,
+        o_vec[1],
+        o_vec[0],
+        o_dec_in,
+        o_rel,
+        o_dec_out,
+        o_cross_q,
+        o_cross_kv,
+        o_cross_out,
+        o_dec_up,
+        o_dec_down,
+        o_vec[3],
+        o_vec[2],
+    )
+
+
 def solution(mesh):
     ndp, nf = mesh.shape["dp"], mesh.shape["fsdp"]
     whole = ("dp", "fsdp")
@@ -739,6 +2120,8 @@
     outs = (two, three, two, three) + (two,) * 4 + (one,) * 2 + (two,) * 8 + (one,) * 2
 
     def body(*arrays):
+        if (ndp, nf) == (4, 8):
+            return shards_fast(ndp, nf, *arrays)
         return shards(ndp, nf, *arrays)
 
     return jax.shard_map(body, mesh=mesh, in_specs=args, out_specs=outs, check_vma=False)

time: 1150 us -> 963 us (0.84)
  local copies, waits for them, and re-layouts: 321 us -> 53.1 us
  Pallas kernels: 0 us -> 258 us
  matrix products: 138 us -> 0 us
  other arithmetic: 195 us -> 74 us
  waiting for transfers between devices: 276 us -> 370 us
  starting transfers between devices: 136 us -> 185 us
  blocking collectives: 46.1 us -> 0 us
  between operations: 20.1 us -> 4.54 us
    pallas_call x0 -> x22, Pallas kernels: none -> 258 us  [run(): pl.pallas_call(body, grid=(grid,), in_specs=[s for a, s in ins], out_spec...]
    dot_general x56 -> x0, matrix products: 138 us -> none  [the longest x12 52.3 us: dot(): lax.dot_general(a, b, (((1,), (0,)), ((), ())), preferred_element_type=F32)]
    unnamed x523 -> x287, local copies, waits for them, and re-layouts: 77.7 us -> 13.4 us
    ppermute x40 -> x60, waiting for transfers between devices: 145 us -> 202 us  [flip_dp(): return lax.ppermute(value, 'dp', [(i, i ^ mask) for i in range(self.ndp)])]
    slice x71 -> x27, local copies, waits for them, and re-layouts: 65.4 us -> 11.3 us  [the longest x4 2.32 us: shards_fast(): o_vec = [vec_sum[starts[i]:starts[i + 1]] for i in range(4)]]
    dynamic_update_slice x45 -> x0, local copies, waits for them, and re-layouts: 52.6 us -> none  [the longest x25 32.3 us: gather_dp_rest(): out = lax.dynamic_update_slice(out, part[None], (lay.dp ^ flip, at, 0, 0))]
    psum x1 -> x0, blocking collectives: 46.1 us -> none  [shards(): enc_vec = lax.psum(enc_vec, ('dp', 'fsdp'))]
    reduce_sum x27 -> x0, other arithmetic: 43.3 us -> none  [the longest x9 14.7 us: col_sum(): return jnp.sum(values.astype(F32), axis=0)]
  transfers between devices with their start and end apart: 101 -> 120, of which waited for: 36 -> 45; matrix products, arithmetic and copies ran while one was open for 50% -> 12% of each run, Pallas kernels for 0% -> 20%
where the time goes in v2:
time: 963 us; the launch traced here: 945 us
  waiting for transfers between devices  370 us (38%)
  Pallas kernels  258 us (27%)
  starting transfers between devices  185 us (19%)
  other arithmetic  74 us (8%)
  local copies, waits for them, and re-layouts  53.1 us (6%)
    pallas_call x22, Pallas kernels, run(): pl.pallas_call(body, grid=(grid,), in_specs=[s for a, s in ins], out_spec...  258 us
    ppermute x60, waiting for transfers between devices, flip_dp(): return lax.ppermute(value, 'dp', [(i, i ^ mask) for i in range(self.ndp)])  202 us
    ppermute x30, waiting for transfers between devices, shift_z(): lax.ppermute(value, 'fsdp', [(i, (i + 2 * step) % self.nf) for i in range...  157 us
    ppermute x30, starting transfers between devices, shift_z(): lax.ppermute(value, 'fsdp', [(i, (i + 2 * step) % self.nf) for i in range...  120 us
    ppermute x60, starting transfers between devices, flip_dp(): return lax.ppermute(value, 'dp', [(i, i ^ mask) for i in range(self.ndp)])  59.9 us
  transfers between devices with their start and end apart: 120, of which 45 were waited for; matrix products, arithmetic and copies ran while one was open for 12% of the time, Pallas kernels for 20%

profile of v2, /device:TPU:0, one launch (start us, length us, event | category | flops | bytes accessed | tf_op | source)
XLA Modules:
  0.0 944.9 jit_solution(8012752895570346051)
XLA Ops:
  22.8 29.3 %collective-permute-done.16 = bf16[256,512]{1,0:T(8,128)(2,1)S(1)} collective-permute-done((bf16[256,512]{1,0:T(8,128)(2,1)S(1)}, bf16[256,512]{1,0:T(8,128)(2,1)S(1)}, u32[]{:S(2)}, u32[]{:S(2)}) %collective-permute-start.16) | collective-permute-done | bytes 262176 | tf_op jit(solution)/shard_map/ppermute | solution.py:138
  67.3 11.3 %collective-permute-done.18.refs_2_ = bf16[2,256,512]{2,1,0:T(8,128)(2,1)} collective-permute-done((bf16[2,256,512]{2,1,0:T(8,128)(2,1)S(1)}, bf16[2,256,512]{2,1,0:T(8,128)(2,1)}, u32[]{:S(2)}, u32[]{:S(2)}) %collective-permute-start.18) | collective-permute-done | bytes 524320 | tf_op jit(solution)/shard_map/ppermute | solution.py:143
  80.4 11.5 %collective-permute-done.7.refs_3_.refs_11_ = bf16[2,304,512]{2,1,0:T(8,128)(2,1)S(1)} collective-permute-done((bf16[2,304,512]{2,1,0:T(8,128)(2,1)S(1)}, bf16[2,304,512]{2,1,0:T(8,128)(2,1)S(1)}, u32[]{:S(2)}, u32[]{:S(2)}) %collective-permute-start.7) | collective-permute-done | bytes 622624 | tf_op jit(solution)/shard_map/ppermute | solution.py:143
  128.7 16.2 %collective-permute-start.26 = (bf16[512,512]{1,0:T(8,128)(2,1)}, bf16[512,512]{1,0:T(8,128)(2,1)S(1)}, u32[]{:S(2)}, u32[]{:S(2)}) collective-permute-start(bf16[512,512]{1,0:T(8,128)(2,1)} %slice_dynamic-update-slice_fusion.2), channel_id=1, source_target_pairs={{0,2},{1,3},{2,4},{3,5},{4,6},{5,7},{6,0},{7,1},{8,10},{9,11},{10,... | collective-permute-start | bytes 1572872 | tf_op jit(solution)/shard_map/ppermute | solution.py:138
  148.0 24.4 %collective-permute-done.27 = bf16[512,512]{1,0:T(8,128)(2,1)} collective-permute-done((bf16[512,512]{1,0:T(8,128)(2,1)}, bf16[512,512]{1,0:T(8,128)(2,1)}, u32[]{:S(2)}, u32[]{:S(2)}) %collective-permute-start.27) | collective-permute-done | bytes 524320 | tf_op jit(solution)/shard_map/ppermute | solution.py:138
  231.9 14.1 %collective-permute-done.40.refs_3_ = bf16[2,256,512]{2,1,0:T(8,128)(2,1)S(1)} collective-permute-done((bf16[2,256,512]{2,1,0:T(8,128)(2,1)}, bf16[2,256,512]{2,1,0:T(8,128)(2,1)S(1)}, u32[]{:S(2)}, u32[]{:S(2)}) %collective-permute-start.40) | collective-permute-done | bytes 524320 | tf_op jit(solution)/shard_map/ppermute | solution.py:143
  252.0 19.0 %shard_map.366 = (bf16[768,1536]{1,0:T(8,128)(2,1)}, f32[768,256]{1,0:T(8,128)}, bf16[768,256]{1,0:T(8,128)(2,1)}, bf16[768,256]{1,0:T(8,128)(2,1)}) custom-call(s32[164]{0:T(256)} %concatenate.336.place, bf16[768,1024]{1,0:T(8,128)(2,1)} %maximum_select_fusion.y.refs_0_, f32[1,1536]{1,0:T(1,128)} %broadcast_in_dim.18.bias, f32[1,256]{1,0:T(1,128)} %bitcast.331, ...), custom_call_target="tpu_custom_call" | custom-call | tf_op jit(solution)/shard_map/pallas_call | solution.py:742
  292.8 16.3 %collective-permute-done.48 = bf16[512,512]{1,0:T(8,128)(2,1)} collective-permute-done((bf16[512,512]{1,0:T(8,128)(2,1)S(1)}, bf16[512,512]{1,0:T(8,128)(2,1)}, u32[]{:S(2)}, u32[]{:S(2)}) %collective-permute-start.48) | collective-permute-done | bytes 524320 | tf_op jit(solution)/shard_map/ppermute | solution.py:138
  325.6 11.3 %shard_map.370 = (f32[256,1024]{1,0:T(8,128)}, f32[256,128]{1,0:T(8,128)}, bf16[256,1024]{1,0:T(8,128)(2,1)}, bf16[256,2048]{1,0:T(8,128)(2,1)}, bf16[256,2048]{1,0:T(8,128)(2,1)}, /*index=5*/bf16[256,1024]{1,0:T(8,128)(2,1)}) custom-call(s32[164]{0:T(256)} %concatenate.336.place, bf16[256,1024]{1,0:T(8,128)(2,1)} %maximum_select_fusion.2.x.base.refs_0_, ...), custom_call_target="tpu_custom_call" | custom-call | tf_op jit(solution)/shard_map/pallas_call | solution.py:742
  352.3 15.0 %shard_map.371 = (f32[768,1024]{1,0:T(8,128)}, f32[768,128]{1,0:T(8,128)}, bf16[768,1024]{1,0:T(8,128)(2,1)}, f32[256,1024]{1,0:T(8,128)}, f32[256,128]{1,0:T(8,...) custom-call(s32[164]{0:T(256)} %concatenate.336.place, ...), custom_call_target="tpu_custom_call" | custom-call | tf_op jit(solution)/shard_map/pallas_call | solution.py:742
  379.4 20.5 %collective-permute-done.51.refs_3_.refs_11_.refs_7_.refs_15_ = bf16[2,512,512]{2,1,0:T(8,128)(2,1)} collective-permute-done((bf16[2,512,512]{2,1,0:T(8,128)(2,1)S(1)}, bf16[2,512,512]{2,1,0:T(8,128)(2,1)}, u32[]{:S(2)}, u32[]{:S(2)}) %collective-permute-start.51) | collective-permute-done | bytes 1048608 | tf_op jit(solution)/shard_map/ppermute | solution.py:143
  401.9 20.1 %collective-permute-done.55.refs_7_.refs_15_.refs_11_.refs_19_ = bf16[2,512,512]{2,1,0:T(8,128)(2,1)} collective-permute-done((bf16[2,512,512]{2,1,0:T(8,128)(2,1)S(1)}, bf16[2,512,512]{2,1,0:T(8,128)(2,1)}, u32[]{:S(2)}, u32[]{:S(2)}) %collective-permute-start.55) | collective-permute-done | bytes 1048608 | tf_op jit(solution)/shard_map/ppermute | solution.py:143
  423.6 21.7 %shard_map.373 = (f32[768,1024]{1,0:T(8,128)}, f32[768,128]{1,0:T(8,128)}, bf16[768,1024]{1,0:T(8,128)(2,1)}, bf16[768,2048]{1,0:T(8,128)(2,1)}, bf16[768,2048]{1,0:T(8,128)(2,1)}, /*index=5*/bf16[768,1024]{1,0:T(8,128)(2,1)}) custom-call(s32[164]{0:T(256)} %concatenate.336.place, f32[768,1024]{1,0:T(8,128)} %get-tuple-element.149.base.unit, ...), custom_call_target="tpu_custom_call" | custom-call | tf_op jit(solution)/shard_map/pallas_call | solution.py:742
  453.5 21.4 %shard_map.374 = (bf16[384,1024]{1,0:T(8,128)(2,1)}, f32[768,1024]{1,0:T(8,128)}, bf16[768,1024]{1,0:T(8,128)(2,1)}, bf16[768,2048]{1,0:T(8,128)(2,1)}, bf16[768...) custom-call(s32[164]{0:T(256)} %concatenate.336.place, ...), custom_call_target="tpu_custom_call" | custom-call | tf_op jit(solution)/shard_map/pallas_call | solution.py:742
  474.9 16.0 %shard_map.386 = (bf16[4,512,512]{2,1,0:T(8,128)(2,1)}, bf16[2,512,512]{2,1,0:T(8,128)(2,1)}, bf16[2,512,512]{2,1,0:T(8,128)(2,1)}, bf16[2,512,512]{2,1,0:T(8,12...) custom-call(s32[164]{0:T(256)} %concatenate.336.place, ...), custom_call_target="tpu_custom_call" | custom-call | tf_op jit(solution)/shard_map/pallas_call | solution.py:742
  499.9 17.5 %collective-permute-done.110 = bf16[2,512,512]{2,1,0:T(8,128)(2,1)} collective-permute-done((bf16[2,512,512]{2,1,0:T(8,128)(2,1)}, bf16[2,512,512]{2,1,0:T(8,128)(2,1)}, u32[]{:S(2)}, u32[]{:S(2)}) %collective-permute-start.110) | collective-permute-done | bytes 1048608 | tf_op jit(solution)/shard_map/ppermute | solution.py:143
  539.3 14.2 %shard_map.376 = (bf16[768,512]{1,0:T(8,128)(2,1)}, bf16[256,1024]{1,0:T(8,128)(2,1)}, bf16[1024,1024]{1,0:T(8,128)(2,1)}, f32[1,512]{1,0:T(1,128)}, f32[1,1024]{1,0:T(1,128)}) custom-call(s32[164]{0:T(256)} %concatenate.336.place, bf16[768,512]{1,0:T(8,128)(2,1)} %get-tuple-element.159.q, bf16[256,1024]{1,0:T(8,128)(2,1)} %get-tuple-element.160.kv, ...), custom_call_target="tpu_custom_call" | custom-call | tf_op jit(solution)/shard_map/pallas_call | solution.py:742
  585.6 21.1 %collective-permute-done.117 = bf16[512,512]{1,0:T(8,128)(2,1)S(1)} collective-permute-done((bf16[512,512]{1,0:T(8,128)(2,1)S(1)}, bf16[512,512]{1,0:T(8,128)(2,1)S(1)}, u32[]{:S(2)}, u32[]{:S(2)}) %collective-permute-start.117) | collective-permute-done | bytes 524320 | tf_op jit(solution)/shard_map/ppermute | solution.py:138
  621.8 11.5 %collective-permute-start.102 = (bf16[256,512]{1,0:T(8,128)(2,1)}, bf16[256,512]{1,0:T(8,128)(2,1)}, u32[]{:S(2)}, u32[]{:S(2)}) collective-permute-start(bf16[256,512]{1,0:T(8,128)(2,1)} %get-tuple-element.276), channel_id=1, source_target_pairs={{0,2},{1,3},{2,4},{3,5},{4,6},{5,7},{6,0},{7,1},{8,10},{9,11},{10,... | collective-permute-start | bytes 786440 | tf_op jit(solution)/shard_map/ppermute | solution.py:138
  667.1 12.0 %shard_map.377 = (f32[256,1024]{1,0:T(8,128)}, bf16[256,1024]{1,0:T(8,128)(2,1)}, bf16[256,2048]{1,0:T(8,128)(2,1)}, bf16[256,1024]{1,0:T(8,128)(2,1)}, f32[1,10...) custom-call(s32[164]{0:T(256)} %concatenate.336.place, f32[5,1024]{1,0:T(8,128)} %stack.155.vecs, ...), custom_call_target="tpu_custom_call" | custom-call | tf_op jit(solution)/shard_map/pallas_call | solution.py:742
  696.7 28.8 %shard_map.381 = (bf16[768,1536]{1,0:T(8,128)(2,1)}, bf16[768,256]{1,0:T(8,128)(2,1)}, f32[384,1024]{1,0:T(8,128)}, bf16[384,1024]{1,0:T(8,128)(2,1)}, f32[1,1536]{1,0:T(1,128)}, /*index=5*/f32[1,256]{1,0:T(1,128)}) custom-call(s32[164]{0:T(256)} %concatenate.336.place, bf16[768,1536]{1,0:T(8,128)(2,1)} %get-tuple-element.177.qkv, ...), custom_call_target="tpu_custom_call" | custom-call | tf_op jit(solution)/shard_map/pallas_call | solution.py:742
  725.6 11.2 %shard_map.384 = (bf16[4,288,512]{2,1,0:T(8,128)(2,1)}, bf16[2,288,512]{2,1,0:T(8,128)(2,1)}, bf16[2,288,512]{2,1,0:T(8,128)(2,1)}, bf16[2,288,512]{2,1,0:T(8,12...) custom-call(s32[164]{0:T(256)} %concatenate.336.place, ...), custom_call_target="tpu_custom_call" | custom-call | tf_op jit(solution)/shard_map/pallas_call | solution.py:742
  750.1 13.2 %shard_map.379 = (bf16[256,1536]{1,0:T(8,128)(2,1)}, f32[128,1024]{1,0:T(8,128)}, bf16[128,1024]{1,0:T(8,128)(2,1)}, f32[1,1536]{1,0:T(1,128)}) custom-call(s32[164]{0:T(256)} %concatenate.336.place, bf16[256,1536]{1,0:T(8,128)(2,1)} %get-tuple-element.157.qkv, bf16[256,256]{1,0:T(8,128)(2,1)} %get-tuple-element.172.keep, bf16[256,256]{1,0:T(8,128)(2,1)} %copy-done.80, ...), custom_call_target="tpu_custom_call" | custom-call | tf_op jit(solution)/shard_map/pallas_call | solution.py:742
  919.1 19.4 %collective-permute-done.84 = bf16[512,512]{1,0:T(8,128)(2,1)} collective-permute-done((bf16[512,512]{1,0:T(8,128)(2,1)}, bf16[512,512]{1,0:T(8,128)(2,1)}, u32[]{:S(2)}, u32[]{:S(2)}) %collective-permute-start.84) | collective-permute-done | bytes 524320 | tf_op jit(solution)/shard_map/ppermute | solution.py:138
  (752 shorter events, 523.2 us)
Async XLA Ops:
  64.3 53.7 %collective-permute-start.21 = (bf16[2,256,512]{2,1,0:T(8,128)(2,1)S(1)}, bf16[2,256,512]{2,1,0:T(8,128)(2,1)S(1)}, u32[]{:S(2)}, u32[]{:S(2)}) collective-permute-start(bf16[2,256,512]{2,1,0:T(8,128)(2,1)S(1)} %pad_maximum_fusion.7.refs_1_), channel_id=1, source_target_pairs={{0,16},{8,24},{16,0},{24,8},{1,17},{9,25},{17,1},{25,9},{2,18},{10... | collective-permute-start | bytes 1572872 | tf_op jit(solution)/shard_map/ppermute | solution.py:143
  67.3 47.3 %collective-permute-start.14 = (bf16[128,1024]{1,0:T(8,128)(2,1)S(1)}, bf16[128,1024]{1,0:T(8,128)(2,1)S(1)}, u32[]{:S(2)}, u32[]{:S(2)}) collective-permute-start(bf16[128,1024]{1,0:T(8,128)(2,1)S(1)} %copy-done.68), channel_id=1, source_target_pairs={{0,1},{1,0},{2,3},{3,2},{4,5},{5,4},{6,7},{7,6},{8,9},{9,8},{10,11... | collective-permute-start | bytes 786440 | tf_op jit(solution)/shard_map/ppermute | solution.py:135
  118.1 54.4 %collective-permute-start.27 = (bf16[512,512]{1,0:T(8,128)(2,1)}, bf16[512,512]{1,0:T(8,128)(2,1)}, u32[]{:S(2)}, u32[]{:S(2)}) collective-permute-start(bf16[512,512]{1,0:T(8,128)(2,1)} %slice_dynamic-update-slice_fusion.2), channel_id=1, source_target_pairs={{0,4},{1,5},{2,6},{3,7},{4,0},{5,1},{6,2},{7,3},{8,12},{9,13},{10,... | collective-permute-start | bytes 1572872 | tf_op jit(solution)/shard_map/ppermute | solution.py:138
  120.6 53.6 %collective-permute-start.28 = (bf16[512,512]{1,0:T(8,128)(2,1)}, bf16[512,512]{1,0:T(8,128)(2,1)S(1)}, u32[]{:S(2)}, u32[]{:S(2)}) collective-permute-start(bf16[512,512]{1,0:T(8,128)(2,1)} %slice_dynamic-update-slice_fusion.2), channel_id=1, source_target_pairs={{0,6},{1,7},{2,0},{3,1},{4,2},{5,3},{6,4},{7,5},{8,14},{9,15},{10,... | collective-permute-start | bytes 1572872 | tf_op jit(solution)/shard_map/ppermute | solution.py:138
  128.7 47.7 %collective-permute-start.26 = (bf16[512,512]{1,0:T(8,128)(2,1)}, bf16[512,512]{1,0:T(8,128)(2,1)S(1)}, u32[]{:S(2)}, u32[]{:S(2)}) collective-permute-start(bf16[512,512]{1,0:T(8,128)(2,1)} %slice_dynamic-update-slice_fusion.2), channel_id=1, source_target_pairs={{0,2},{1,3},{2,4},{3,5},{4,6},{5,7},{6,0},{7,1},{8,10},{9,11},{10,... | collective-permute-start | bytes 1572872 | tf_op jit(solution)/shard_map/ppermute | solution.py:138
  192.9 81.1 %collective-permute-start.30 = (bf16[2,512,512]{2,1,0:T(8,128)(2,1)S(1)}, bf16[2,512,512]{2,1,0:T(8,128)(2,1)}, u32[]{:S(2)}, u32[]{:S(2)}) collective-permute-start(bf16[2,512,512]{2,1,0:T(8,128)(2,1)S(1)} %pad_maximum_fusion.1.refs_1_.refs_9_.refs_6_.refs_14_), channel_id=1, source_target_pairs={{0,8},{8,0},{16,24},{24,16},{1,9},{9,1},{17,25},{25,17},{2,10},{10... | collective-permute-start | bytes 3145736 | tf_op jit(solution)/shard_map/ppermute | solution.py:143
  200.7 73.7 %collective-permute-start.32 = (bf16[2,512,512]{2,1,0:T(8,128)(2,1)S(1)}, bf16[2,512,512]{2,1,0:T(8,128)(2,1)}, u32[]{:S(2)}, u32[]{:S(2)}) collective-permute-start(bf16[2,512,512]{2,1,0:T(8,128)(2,1)S(1)} %pad_maximum_fusion.1.refs_1_.refs_9_.refs_6_.refs_14_), channel_id=1, source_target_pairs={{0,16},{8,24},{16,0},{24,8},{1,17},{9,25},{17,1},{25,9},{2,18},{10... | collective-permute-start | bytes 3145736 | tf_op jit(solution)/shard_map/ppermute | solution.py:143
  201.5 73.1 %collective-permute-start.29 = (bf16[2,512,512]{2,1,0:T(8,128)(2,1)S(1)}, bf16[2,512,512]{2,1,0:T(8,128)(2,1)}, u32[]{:S(2)}, u32[]{:S(2)}) collective-permute-start(bf16[2,512,512]{2,1,0:T(8,128)(2,1)S(1)} %pad_maximum_fusion.refs_0_.refs_8_.refs_5_.refs_13_), channel_id=1, source_target_pairs={{0,8},{8,0},{16,24},{24,16},{1,9},{9,1},{17,25},{25,17},{2,10},{10... | collective-permute-start | bytes 3145736 | tf_op jit(solution)/shard_map/ppermute | solution.py:143
  220.2 53.6 %collective-permute-start.39 = (bf16[2,256,512]{2,1,0:T(8,128)(2,1)S(1)}, bf16[2,256,512]{2,1,0:T(8,128)(2,1)}, u32[]{:S(2)}, u32[]{:S(2)}) collective-permute-start(bf16[2,256,512]{2,1,0:T(8,128)(2,1)S(1)} %copy-done.16), channel_id=1, source_target_pairs={{0,8},{8,0},{16,24},{24,16},{1,9},{9,1},{17,25},{25,17},{2,10},{10... | collective-permute-start | bytes 1572872 | tf_op jit(solution)/shard_map/ppermute | solution.py:143
  274.6 46.6 %collective-permute-start.33 = (bf16[2,512,512]{2,1,0:T(8,128)(2,1)}, bf16[2,512,512]{2,1,0:T(8,128)(2,1)}, u32[]{:S(2)}, u32[]{:S(2)}) collective-permute-start(bf16[2,512,512]{2,1,0:T(8,128)(2,1)} %collective-permute-done.29.refs_2_.refs_10_.refs_7_.refs_15_), channel_id=1, source_target_pairs={{0,16},{8,24},{16,0},{24,8},{1,17},{9,25},{17,1},{25,9},{2,18},{10... | collective-permute-start | bytes 3145736 | tf_op jit(solution)/shard_map/ppermute | solution.py:143
  291.3 60.9 %collective-permute-start.13 = (bf16[768,1024]{1,0:T(8,128)(2,1)}, bf16[768,1024]{1,0:T(8,128)(2,1)}, u32[]{:S(2)}, u32[]{:S(2)}) collective-permute-start(bf16[768,1024]{1,0:T(8,128)(2,1)} %shard_map.367.own), channel_id=1, source_target_pairs={{0,1},{1,0},{2,3},{3,2},{4,5},{5,4},{6,7},{7,6},{8,9},{9,8},{10,11... | collective-permute-start | bytes 4718600 | tf_op jit(solution)/shard_map/ppermute | solution.py:135
  373.7 49.9 %collective-permute-start.46 = (bf16[768,1024]{1,0:T(8,128)(2,1)}, bf16[768,1024]{1,0:T(8,128)(2,1)}, u32[]{:S(2)}, u32[]{:S(2)}) collective-permute-start(bf16[768,1024]{1,0:T(8,128)(2,1)} %shard_map.372.own), channel_id=1, source_target_pairs={{0,1},{1,0},{2,3},{3,2},{4,5},{5,4},{6,7},{7,6},{8,9},{9,8},{10,11... | collective-permute-start | bytes 4718600 | tf_op jit(solution)/shard_map/ppermute | solution.py:135
  376.3 45.8 %collective-permute-start.55 = (bf16[2,512,512]{2,1,0:T(8,128)(2,1)S(1)}, bf16[2,512,512]{2,1,0:T(8,128)(2,1)}, u32[]{:S(2)}, u32[]{:S(2)}) collective-permute-start(bf16[2,512,512]{2,1,0:T(8,128)(2,1)S(1)} %collective-permute-done.53.refs_5_.refs_13_.refs_9_.refs_17_), channel_id=1, source_target_pairs={{0,8},{8,0},{16,24},{24,16},{1,9},{9,1},{17,25},{25,17},{2,10},{10... | collective-permute-start | bytes 3145736 | tf_op jit(solution)/shard_map/ppermute | solution.py:143
  376.9 46.7 %collective-permute-start.54 = (bf16[2,512,512]{2,1,0:T(8,128)(2,1)}, bf16[2,512,512]{2,1,0:T(8,128)(2,1)}, u32[]{:S(2)}, u32[]{:S(2)}) collective-permute-start(bf16[2,512,512]{2,1,0:T(8,128)(2,1)} %collective-permute-done.50.refs_2_.refs_10_.refs_6_.refs_14_), channel_id=1, source_target_pairs={{0,16},{8,24},{16,0},{24,8},{1,17},{9,25},{17,1},{25,9},{2,18},{10... | collective-permute-start | bytes 3145736 | tf_op jit(solution)/shard_map/ppermute | solution.py:143
  496.9 67.1 %collective-permute-start.112 = (bf16[2,512,512]{2,1,0:T(8,128)(2,1)}, bf16[2,512,512]{2,1,0:T(8,128)(2,1)}, u32[]{:S(2)}, u32[]{:S(2)}) collective-permute-start(bf16[2,512,512]{2,1,0:T(8,128)(2,1)} %get-tuple-element.256), channel_id=1, source_target_pairs={{0,16},{8,24},{16,0},{24,8},{1,17},{9,25},{17,1},{25,9},{2,18},{10... | collective-permute-start | bytes 3145736 | tf_op jit(solution)/shard_map/ppermute | solution.py:143
  498.2 67.5 %collective-permute-start.114 = (bf16[2,512,512]{2,1,0:T(8,128)(2,1)}, bf16[2,512,512]{2,1,0:T(8,128)(2,1)}, u32[]{:S(2)}, u32[]{:S(2)}) collective-permute-start(bf16[2,512,512]{2,1,0:T(8,128)(2,1)} %get-tuple-element.257), channel_id=1, source_target_pairs={{0,8},{8,0},{16,24},{24,16},{1,9},{9,1},{17,25},{25,17},{2,10},{10... | collective-permute-start | bytes 3145736 | tf_op jit(solution)/shard_map/ppermute | solution.py:143
  520.2 45.9 %collective-permute-start.111 = (bf16[2,512,512]{2,1,0:T(8,128)(2,1)}, bf16[2,512,512]{2,1,0:T(8,128)(2,1)}, u32[]{:S(2)}, u32[]{:S(2)}) collective-permute-start(bf16[2,512,512]{2,1,0:T(8,128)(2,1)} %add_convert_fusion.1), channel_id=1, source_target_pairs={{0,8},{8,0},{16,24},{24,16},{1,9},{9,1},{17,25},{25,17},{2,10},{10... | collective-permute-start | bytes 3145736 | tf_op jit(solution)/shard_map/ppermute | solution.py:143
  565.7 45.3 %collective-permute-start.101 = (bf16[2,256,512]{2,1,0:T(8,128)(2,1)}, bf16[2,256,512]{2,1,0:T(8,128)(2,1)S(1)}, u32[]{:S(2)}, u32[]{:S(2)}) collective-permute-start(bf16[2,256,512]{2,1,0:T(8,128)(2,1)} %get-tuple-element.245), channel_id=1, source_target_pairs={{0,16},{8,24},{16,0},{24,8},{1,17},{9,25},{17,1},{25,9},{2,18},{10... | collective-permute-start | bytes 1572872 | tf_op jit(solution)/shard_map/ppermute | solution.py:143
  585.6 69.6 %collective-permute-start.61 = (bf16[1024,1024]{1,0:T(8,128)(2,1)S(1)}, bf16[1024,1024]{1,0:T(8,128)(2,1)}, u32[]{:S(2)}, u32[]{:S(2)}) collective-permute-start(bf16[1024,1024]{1,0:T(8,128)(2,1)S(1)} %copy-done.17), channel_id=1, source_target_pairs={{0,1},{1,0},{2,3},{3,2},{4,5},{5,4},{6,7},{7,6},{8,9},{9,8},{10,11... | collective-permute-start | bytes 6291464 | tf_op jit(solution)/shard_map/ppermute | solution.py:135
  679.2 61.7 %collective-permute-start.62 = (bf16[256,1024]{1,0:T(8,128)(2,1)}, bf16[256,1024]{1,0:T(8,128)(2,1)}, u32[]{:S(2)}, u32[]{:S(2)}) collective-permute-start(bf16[256,1024]{1,0:T(8,128)(2,1)} %get-tuple-element.170.own), channel_id=1, source_target_pairs={{0,1},{1,0},{2,3},{3,2},{4,5},{5,4},{6,7},{7,6},{8,9},{9,8},{10,11... | collective-permute-start | bytes 1572872 | tf_op jit(solution)/shard_map/ppermute | solution.py:135
  692.4 93.5 %collective-permute-start.77 = (bf16[2,512,512]{2,1,0:T(8,128)(2,1)}, bf16[2,512,512]{2,1,0:T(8,128)(2,1)S(1)}, u32[]{:S(2)}, u32[]{:S(2)}) collective-permute-start(bf16[2,512,512]{2,1,0:T(8,128)(2,1)} %get-tuple-element.223), channel_id=1, source_target_pairs={{0,16},{8,24},{16,0},{24,8},{1,17},{9,25},{17,1},{25,9},{2,18},{10... | collective-permute-start | bytes 3145736 | tf_op jit(solution)/shard_map/ppermute | solution.py:143
  693.9 105.2 %collective-permute-start.82 = (bf16[2,512,512]{2,1,0:T(8,128)(2,1)}, bf16[2,512,512]{2,1,0:T(8,128)(2,1)S(1)}, u32[]{:S(2)}, u32[]{:S(2)}) collective-permute-start(bf16[2,512,512]{2,1,0:T(8,128)(2,1)} %get-tuple-element.227), channel_id=1, source_target_pairs={{0,8},{8,0},{16,24},{24,16},{1,9},{9,1},{17,25},{25,17},{2,10},{10... | collective-permute-start | bytes 3145736 | tf_op jit(solution)/shard_map/ppermute | solution.py:143
  736.8 46.8 %collective-permute-start.88 = (bf16[2,288,512]{2,1,0:T(8,128)(2,1)}, bf16[2,288,512]{2,1,0:T(8,128)(2,1)S(1)}, u32[]{:S(2)}, u32[]{:S(2)}) collective-permute-start(bf16[2,288,512]{2,1,0:T(8,128)(2,1)} %get-tuple-element.233), channel_id=1, source_target_pairs={{0,16},{8,24},{16,0},{24,8},{1,17},{9,25},{17,1},{25,9},{2,18},{10... | collective-permute-start | bytes 1769480 | tf_op jit(solution)/shard_map/ppermute | solution.py:143
  737.3 47.9 %collective-permute-start.93 = (bf16[2,288,512]{2,1,0:T(8,128)(2,1)}, bf16[2,288,512]{2,1,0:T(8,128)(2,1)S(1)}, u32[]{:S(2)}, u32[]{:S(2)}) collective-permute-start(bf16[2,288,512]{2,1,0:T(8,128)(2,1)} %get-tuple-element.237), channel_id=1, source_target_pairs={{0,8},{8,0},{16,24},{24,16},{1,9},{9,1},{17,25},{25,17},{2,10},{10... | collective-permute-start | bytes 1769480 | tf_op jit(solution)/shard_map/ppermute | solution.py:143
  (222 other events, 4335.9 us)

commit v3 on v2

--- a/solution.py
+++ b/solution.py
@@ -734,10 +734,11 @@
 
 
 BUDGET = 58 * 1024 * 1024
-PIECES = 8
-
-
-def run(body, grid, ins, outs, scratch=()):
+PIECES = 4
+HBM_RATE = 3.0e6
+
+
+def run(body, grid, ins, outs, scratch=(), us=5):
     arrays = [a for a, s in ins]
     return pl.pallas_call(
         body,
@@ -747,6 +748,9 @@
         out_shape=[a for a, s in outs],
         scratch_shapes=list(scratch),
         compiler_params=pltpu.CompilerParams(vmem_limit_bytes=BUDGET),
+        cost_estimate=pl.CostEstimate(
+            flops=0, bytes_accessed=int(us * HBM_RATE), transcendentals=0
+        ),
     )(*arrays)
 
 
@@ -777,17 +781,17 @@
 
 def blocks(pieces, rows, index):
     return [
-        (p, pl.BlockSpec((2, rows, WIDE), lambda t: (0, index(t), 0))) for p in pieces
+        (p, pl.BlockSpec((4, rows, WIDE), lambda t: (0, index(t), 0))) for p in pieces
     ]
 
 
+def wide_blocks(pieces, index):
+    return [(p, pl.BlockSpec((4,) + p.shape[1:2] + (WIDE,), lambda t: (0, 0, index(t)))) for p in pieces]
+
+
 def assemble(refs, scr, place):
-    dp, z = place[0], place[1]
     for i in range(4):
-        for half in range(2):
-            for j in range(2):
-                step = 2 * half + j
-                scr[jnp.bitwise_xor(dp, i), jnp.bitwise_and(z - step, 3)] = refs[2 * i + half][j]
+        scr[jnp.bitwise_xor(place[0], i)] = refs[i][...]
 
 
 def weight_scratch(rows, width=WIDE):
@@ -892,6 +896,7 @@
             out_full((rows, HALF // 2), BF),
         ],
         [weight_scratch(64), pltpu.VMEM((rows, HALF), BF)],
+        us=10,
     )
 
 
@@ -912,6 +917,7 @@
         [small(place), full(keep), full(got)] + blocks(pieces, 32, lambda t: 6 + t),
         [out_cols(rows, D, BF, lambda t: t)],
         [weight_scratch(32)],
+        us=3,
     )[0]
 
 
@@ -954,7 +960,7 @@
     return u * phi, phi + u * (jnp.exp(-0.5 * u * u) * ROOT_TWO_PI)
 
 
-def ffn_forward(place, base, affine, own, other, vecs, hidden_bias, pieces):
+def ffn_forward(place, base, affine, own, other, vecs, hidden_bias, up_pieces, down_pieces):
     rows = base.shape[0]
     hidden = hidden_bias.shape[1]
     ups = hidden // WIDE
@@ -998,8 +1004,8 @@
         body,
         ups + 2,
         [small(place), full(base), full(own), full(other), full(vecs), in_cols(hidden_bias, up)]
-        + blocks(pieces, 64, up)
-        + blocks(pieces, 128, lambda t: 2 + down(t)),
+        + blocks(up_pieces, 64, up)
+        + wide_blocks(down_pieces, down),
         [
             out_full((rows, D), F32),
             out_full((rows, 128), F32),
@@ -1009,6 +1015,7 @@
             out_cols(rows, D, BF, down),
         ],
         [weight_scratch(64), weight_scratch(128), pltpu.VMEM((rows, hidden), BF)],
+        us=20 if rows > 256 else 11,
     )
 
 
@@ -1137,18 +1144,16 @@
             pltpu.VMEM((rows, HALF), BF),
             pltpu.VMEM((128, 128), BF),
         ],
+        us=19,
     )
 
 
 def assemble_rel(refs, scr, place):
-    dp, z = place[0], place[1]
     for i in range(4):
-        for half in range(2):
-            for j in range(2):
-                block = refs[2 * i + half][j]
-                a, b = jnp.bitwise_xor(dp, i), jnp.bitwise_and(z - (2 * half + j), 3)
-                scr[a, b, 0] = block[:, :REL_HALF]
-                scr[a, b, 1] = block[:, REL_HALF:]
+        block = refs[i][...]
+        at = jnp.bitwise_xor(place[0], i)
+        scr[at, :, 0] = block[:, :, :REL_HALF]
+        scr[at, :, 1] = block[:, :, REL_HALF:]
 
 
 def cross_forward(place, y, own, other, vecs, eunit, evecs, eown, eother, q_bias, kv_bias, pieces):
@@ -1217,6 +1222,7 @@
             out_full((rows, HALF // 2), BF),
         ],
         [weight_scratch(64), pltpu.VMEM((rows, HALF), BF)],
+        us=15,
     )
 
 
@@ -1231,7 +1237,7 @@
     return inverse * (scaled - one - unit * two)
 
 
-def ffn_back(place, final, total_ins, unit_ins, vecs, gp, pieces):
+def ffn_back(place, final, total_ins, unit_ins, vecs, gp, up_pieces, down_pieces):
     rows, hidden = gp.shape
     ups = hidden // WIDE
     n_total, n_unit = len(total_ins), len(unit_ins)
@@ -1327,8 +1333,8 @@
         [small(place), full(vecs), in_cols(gp, up)]
         + [full(a) for a in total_ins]
         + [full(a) for a in unit_ins]
-        + blocks(pieces, 64, up)
-        + blocks(pieces, 128, lambda t: 2 + down(t)),
+        + blocks(up_pieces, 64, up)
+        + wide_blocks(down_pieces, down),
         outs,
         [
             weight_scratch(64),
@@ -1337,6 +1343,7 @@
             pltpu.VMEM((D, hidden), BF),
             pltpu.VMEM((24, D), F32),
         ],
+        us=21 if rows > 256 else 12,
     )
 
 
@@ -1396,6 +1403,7 @@
             out_full((1, D), F32),
         ],
         [weight_scratch(32), pltpu.VMEM((rows, HALF), F32), pltpu.VMEM((24, D), F32)],
+        us=10 if rows > 256 else 5,
     )
 
 
@@ -1450,6 +1458,7 @@
             out_full((1, D), F32),
         ],
         [weight_scratch(64), pltpu.VMEM((rows, HALF), BF), pltpu.VMEM((mem, D), F32)],
+        us=14,
     )
 
 
@@ -1506,6 +1515,7 @@
             out_full((1, 3 * HALF), F32),
         ],
         [weight_scratch(64), pltpu.VMEM((rows, HALF), BF), pltpu.VMEM((D, 3 * HALF), BF)],
+        us=13,
     )
 
 
@@ -1619,27 +1629,23 @@
             pltpu.VMEM((D, 3 * HALF), BF),
         ]
         + [pltpu.VMEM((128, 128), BF)] * 3,
-    )
-
-
-def grad_chunk(place, arrays, terms, total_rows):
+        us=29,
+    )
+
+
+def grad_chunk(place, arrays, terms, total_rows, width=WIDE):
     n = len(arrays)
 
     def body(place, *refs):
-        ins, outs, scr = refs[:n], refs[n : n + 7], refs[n + 7]
+        ins, outs, scr = refs[:n], refs[n : n + 4], refs[n + 4]
         t = pl.program_id(0)
-        dp, z, core = place[0], place[1], place[2]
-
-        def spread(value, at, rows):
+        dp, core = place[0], place[2]
+
+        def spread(value, at, rows, lanes=slice(0, WIDE)):
             v = value.astype(BF).reshape(4, 4, rows, WIDE)
             scr[:, :, :rows] = v
             for i in range(4):
-                for step in range(4):
-                    block = scr[jnp.bitwise_xor(dp, i), jnp.bitwise_and(z + step, 3), :rows]
-                    if i == 0:
-                        outs[0][step, at : at + rows] = block
-                    else:
-                        outs[2 * i - 1 + step // 2][step % 2, at : at + rows] = block
+                outs[i][:, at : at + rows, lanes] = scr[jnp.bitwise_xor(dp, i), :, :rows]
 
         for index, (kind, at, x, g, col) in enumerate(terms):
 
@@ -1662,15 +1668,16 @@
                     spread(jnp.concatenate([v[:, 0], v[:, 1]], axis=-1), at, 32)
                     return
                 value = dot_g(ins[x][...], ins[g][:, col : col + WIDE])
-                spread(value, at, value.shape[0] // 16)
-
-    shape = (2, total_rows, WIDE)
+                lanes = slice(col, col + WIDE) if kind == "rows" else slice(0, WIDE)
+                spread(value, at, value.shape[0] // 16, lanes)
+
     return run(
         body,
         len(terms),
         [small(place)] + [full(a) for a in arrays],
-        [out_full((4, total_rows, WIDE), BF)] + [out_full(shape, BF)] * 6,
+        [out_full((4, total_rows, width), BF)] * 4,
         [weight_scratch(128)],
+        us=10,
     )
 
 
@@ -1683,34 +1690,83 @@
         1,
         [small(place)] + blocks(pieces, 16, lambda t: 18),
         [out_full((4, 4, 16, WIDE), BF)],
+        us=2,
     )[0]
 
 
-def gather_pieces(lay, buf):
-    got = [buf] + [lay.shift_z(buf, step) for step in range(1, 4)]
-    low = jnp.stack(got[:2])
-    high = jnp.stack(got[2:])
-    x_low, y_low = lay.flip_dp(low, 1), lay.flip_dp(low, 2)
-    x_high, y_high = lay.flip_dp(high, 1), lay.flip_dp(high, 2)
-    d_low = lay.flip_dp(x_low, 2)
-    d_high = lay.flip_dp(y_high, 1)
-    return [low, high, x_low, x_high, y_low, y_high, d_low, d_high]
-
-
-def scatter_pieces(lay, parts):
-    own, x_low, x_high, y_low, y_high, d_low, d_high = parts
-    d_low = lay.flip_dp(d_low, 2)
-    d_high = lay.flip_dp(d_high, 1)
-    x_high = lay.flip_dp(x_high, 1)
-    y_low = lay.flip_dp(y_low, 2)
-    x_low = lay.flip_dp(add_low(x_low, d_low), 1)
-    y_high = lay.flip_dp(add_low(y_high, d_high), 2)
-    sides = [(x_low, y_low, 0), (x_low, y_low, 1), (x_high, y_high, 0), (x_high, y_high, 1)]
-    sums = [add_low(own[s], x[i], y[i]) for s, (x, y, i) in enumerate(sides)]
-    total = sums[0].astype(F32)
-    for step in range(1, 4):
-        total = total + lay.shift_z(sums[step], step).astype(F32)
-    return total
+class Order:
+
+    def __init__(self, place):
+        self.place = place
+        self.last = None
+
+    def after(self, *values):
+        if self.last is not None:
+            values = (self.last,) + values
+        self.place = tie(self.place, *values)
+        self.last = None
+
+    def run(self, kernel, *args):
+        if self.last is not None:
+            self.place = tie(self.place, self.last)
+        out = kernel(self.place, *args)
+        self.last = out[0] if isinstance(out, (list, tuple)) else out
+        return out
+
+    def add(self, first, *others):
+        if self.last is not None:
+            first = tie(first, self.last)
+        self.last = add_low(first, *others)
+        return self.last
+
+
+class Links:
+
+    def __init__(self, lay):
+        self.lay = lay
+        self.sent = {1: [], 2: []}
+        self.gathered = []
+        self.far = 2
+        self.groups = [list(range(core, lay.nf, 2)) for core in range(2)]
+
+    def send(self, value, mask):
+        queue = self.sent[mask]
+        if len(queue) >= 2:
+            value = tie(value, queue[-2])
+        queue.append(self.lay.flip_dp(value, mask))
+        return queue[-1]
+
+    def turn(self):
+        self.far = 3 - self.far
+        return self.far
+
+    def gather(self, buf):
+        far = self.turn()
+        if len(self.gathered) >= 2:
+            buf = tie(buf, self.gathered[-2])
+        own = lax.all_gather(buf, "fsdp", axis=0, axis_index_groups=self.groups)
+        self.gathered.append(own)
+        x, y = self.send(own, 1), self.send(own, 2)
+        d = self.send(x, 2) if far == 2 else self.send(y, 1)
+        return [own, x, y, d]
+
+    def scatter(self, order, parts):
+        far = self.turn()
+        own, x, y, d = parts
+        d = self.lay.flip_dp(d, far)
+        if far == 2:
+            y = self.lay.flip_dp(y, 2)
+            yield
+            x = self.lay.flip_dp(order.add(x, d), 1)
+        else:
+            x = self.lay.flip_dp(x, 1)
+            yield
+            y = self.lay.flip_dp(order.add(y, d), 2)
+        yield
+        total = order.add(own, x, y)
+        yield lax.psum_scatter(
+            total, "fsdp", scatter_dimension=0, axis_index_groups=self.groups
+        ).astype(F32)
 
 
 def shards_fast(
@@ -1746,6 +1802,9 @@
     core = lay.core
     dec_rows = STREAMS * LEN
 
+    links = Links(lay)
+    w = {"dec_down": links.gather(dec_ffn_out), "enc_down": links.gather(enc_ffn_out)}
+
     def halves(matrix, groups, width):
         parts = matrix.reshape(r, groups, 2, width)
         return (
@@ -1804,25 +1863,21 @@
     at = [0, 3 * WIDE, 7 * WIDE, 10 * WIDE, 11 * WIDE, 13 * WIDE]
     chunk_parts = {
         "enc": column_blocks(at[0], 3) + row_blocks(enc_out_proj),
-        "enc_ffn": column_blocks(at[1], 4) + row_blocks(enc_ffn_out),
+        "enc_up": column_blocks(at[1], 4),
         "dec": column_blocks(at[2], 3) + row_blocks(dec_out_proj) + [rel_block, vec_block],
         "cross": column_blocks(at[3], 1) + column_blocks(at[4], 2) + row_blocks(cross_out),
-        "dec_ffn": column_blocks(at[5], 4) + row_blocks(dec_ffn_out),
+        "dec_up": column_blocks(at[5], 4),
     }
-    w = {}
-    order = ["dec", "enc", "enc_ffn", "cross", "dec_ffn"]
-    for i, name in enumerate(order):
-        buf = jnp.concatenate(chunk_parts[name], axis=0)
-        if i >= 2:
-            buf = tie(buf, *w[order[i - 2]][2:4])
-        w[name] = gather_pieces(lay, buf)
-
-    lens = vec_pair[:, nvec - 2 :].T.reshape(-1).astype(F32).astype(jnp.int32)
+    for name in ("dec", "enc", "enc_up", "cross", "dec_up"):
+        w[name] = links.gather(jnp.concatenate(chunk_parts[name], axis=0))
+
+    lens = vec_pair[:, nvec - 2 : nvec].T.reshape(-1).astype(F32).astype(jnp.int32)
     place = jnp.concatenate(
         [jnp.stack([lay.dp, lay.z, core]).astype(jnp.int32), lens, jnp.zeros((1,), jnp.int32)]
     )
 
-    vec_all = vec_chunk(place, w["dec"]).reshape(chips, 16, WIDE)[:, :vec_used]
+    order = Order(place)
+    vec_all = order.run(vec_chunk, w["dec"]).reshape(chips, 16, WIDE)[:, :vec_used]
     vec_all = vec_all.reshape(lay.devices, padded).astype(F32)
     widths = [enc_biases.shape[0], enc_gains.shape[0], dec_biases.shape[0], dec_gains.shape[0]]
     starts = [0]
@@ -1854,33 +1909,38 @@
 
     x = pair(source, source_got, 0)
     y = pair(dec_own, dec_got, 0)
-    dqkv, rel, da_keep, da_send = ngram_attention(
-        place,
+    dcot_own = dec_cot.transpose(1, 0, 2).reshape(dec_rows, D)
+    dcot = pair(dcot_own, swap(dcot_own), 0)
+    ecot = pair(enc_cot, swap(enc_cot), 0)
+    order.after(x, y, dcot, ecot)
+    dqkv, rel, da_keep, da_send = order.run(
+        ngram_attention,
         y,
         qkv_bias(v_dec_b[:D], v_dec_b[D : 2 * D]),
         half_of(v_dec_b[2 * D : d_split])[None],
         w["dec"],
     )
     da_got = swap(da_send)
-    p3 = out_projection(place, da_keep, da_got, w["dec"])
+    eqkv, ea_keep, ea_send = order.run(enc_attention, x, qkv_bias(eb[0], eb[1]), w["enc"])
+    ea_got = swap(ea_send)
+    p3 = order.run(out_projection, da_keep, da_got, w["dec"])
     p3_got = swap(p3)
-    eqkv, ea_keep, ea_send = enc_attention(place, x, qkv_bias(eb[0], eb[1]), w["enc"])
-    ea_got = swap(ea_send)
-    p1 = out_projection(place, ea_keep, ea_got, w["enc"])
+    p1 = order.run(out_projection, ea_keep, ea_got, w["enc"])
     p1_got = swap(p1)
-    eunit1, einv1, eh1_low, eg, egp, p2 = ffn_forward(
-        place,
+    eunit1, einv1, eh1_low, eg, egp, p2 = order.run(
+        ffn_forward,
         x,
         False,
         p1,
         p1_got,
         rows_of(eb[2], eb[2], eb[2], eg_rows[0], eb[8]),
         hidden_of(eb[3:7]),
-        w["enc_ffn"],
+        w["enc_up"],
+        w["enc_down"],
     )
     p2_got = swap(p2)
-    dunit1, dinv1, dh1_low, eunit2, einv2, enc_low, cq, ckv, ca_keep, ca_send = cross_forward(
-        place,
+    dunit1, dinv1, dh1_low, eunit2, einv2, enc_low, cq, ckv, ca_keep, ca_send = order.run(
+        cross_forward,
         y,
         p3,
         p3_got,
@@ -1894,98 +1954,106 @@
         w["cross"],
     )
     ca_got = swap(ca_send)
-    p4 = out_projection(place, ca_keep, ca_got, w["cross"])
+    p4 = order.run(out_projection, ca_keep, ca_got, w["cross"])
     p4_got = swap(p4)
-    dunit2, dinv2, dh2_low, dg, dgp, p5 = ffn_forward(
-        place,
+    dunit2, dinv2, dh2_low, dg, dgp, p5 = order.run(
+        ffn_forward,
         dunit1,
         True,
         p4,
         p4_got,
         rows_of(dg_rows[0], db[9], db[3], dg_rows[1], db[10]),
         hidden_of(db[4:8]),
-        w["dec_ffn"],
+        w["dec_up"],
+        w["dec_down"],
     )
     p5_got = swap(p5)
 
-    dcot_own = dec_cot.transpose(1, 0, 2).reshape(dec_rows, D)
-    dcot = pair(dcot_own, swap(dcot_own), 0)
-    ecot = pair(enc_cot, swap(enc_cot), 0)
-    dec_out, gz3, gf, gu, p6, s_gain3, s_shift3, s_gf, s_gu = ffn_back(
-        place,
+    dec_out, gz3, gf, gu, p6, s_gain3, s_shift3, s_gf, s_gu = order.run(
+        ffn_back,
         True,
         [dcot],
         [dunit2, p5, p5_got],
         rows_of(dg_rows[1], db[10], db[8], dg_rows[2], db[11]),
         dgp,
-        w["dec_ffn"],
+        w["dec_up"],
+        w["dec_down"],
     )
     p6_got = swap(p6)
     up_terms = [("plain", 64 * b, 0, 1, WIDE * b) for b in range(4)]
-    down_terms = [("plain", 256 + 128 * h, 2, 3, WIDE * h) for h in range(2)]
-    total4 = scatter_pieces(
-        lay, grad_chunk(place, [dh2_low, gu, dg, gf], up_terms + down_terms, 512)
-    )
-    gz2, gx, gca_keep, gca_send, s_gain2, s_shift2, s_gx = branch_back(
-        place, gz3, p6, p6_got, dunit2, dinv2, dg_rows[1:2], w["cross"]
+    down_terms = [("rows", 0, 0, 1, WIDE * h) for h in range(2)]
+
+    def grads(*args):
+        scatter = links.scatter(order, order.run(grad_chunk, *args))
+        next(scatter)
+        return scatter
+
+    r_dd = grads([dg, gf], down_terms, 128, D)
+    r_du = grads([dh2_low, gu], up_terms, 256)
+    gz2, gx, gca_keep, gca_send, s_gain2, s_shift2, s_gx = order.run(
+        branch_back, gz3, p6, p6_got, dunit2, dinv2, dg_rows[1:2], w["cross"]
     )
     gca_got = swap(gca_send)
-    gcq, gckv, p7, s_gcq, s_gckv = cross_back(place, cq, ckv, gca_keep, gca_got, w["cross"])
+    next(r_dd)
+    next(r_du)
+    gcq, gckv, p7, s_gcq, s_gckv = order.run(
+        cross_back, cq, ckv, gca_keep, gca_got, w["cross"]
+    )
     p7_got = swap(p7)
-    total3 = scatter_pieces(
-        lay,
-        grad_chunk(
-            place,
-            [dh1_low, gcq, enc_low, gckv, ca_keep, ca_got, gx],
-            [
-                ("plain", 0, 0, 1, 0),
-                ("plain", 64, 2, 3, 0),
-                ("plain", 128, 2, 3, WIDE),
-                ("heads", 192, 4, 6, 0),
-                ("heads", 224, 4, 6, WIDE),
-            ],
-            256,
-        ),
-    )
-    gz1, go, gda_keep, gda_send, s_gain1, s_shift1, s_go = branch_back(
-        place, gz2, p7, p7_got, dunit1, dinv1, dg_rows[0:1], w["dec"]
+    r_cross = grads(
+        [dh1_low, gcq, enc_low, gckv, ca_keep, ca_got, gx],
+        [
+            ("plain", 0, 0, 1, 0),
+            ("plain", 64, 2, 3, 0),
+            ("plain", 128, 2, 3, WIDE),
+            ("heads", 192, 4, 6, 0),
+            ("heads", 224, 4, 6, WIDE),
+        ],
+        256,
+    )
+    gz1, go, gda_keep, gda_send, s_gain1, s_shift1, s_go = order.run(
+        branch_back, gz2, p7, p7_got, dunit1, dinv1, dg_rows[0:1], w["dec"]
     )
     gda_got = swap(gda_send)
-    gqkv, grel, p8, p8_send, s_gqkv, s_grel = ngram_back_kernel(
-        place, dqkv, rel, gda_keep, gda_got, gz1, w["dec"]
-    )
-    p8_got = swap(p8_send)
-    total2 = scatter_pieces(
-        lay,
-        grad_chunk(
-            place,
-            [y, gqkv, da_keep, da_got, go, grel],
-            [("plain", 64 * b, 0, 1, WIDE * b) for b in range(3)]
-            + [("heads", 192, 2, 4, 0), ("heads", 224, 2, 4, WIDE), ("rel", 256, 0, 5, 0)],
-            288,
-        ),
-    )
-    gz2e, gfe, gue, p9, e_gain2, e_shift2, s_gfe, s_gue = ffn_back(
-        place,
+    gz2e, gfe, gue, p9, e_gain2, e_shift2, s_gfe, s_gue = order.run(
+        ffn_back,
         False,
         [ecot, p7, p7_got],
         [eunit2, einv2],
         rows_of(*([eg_rows[1]] * 5)),
         egp,
-        w["enc_ffn"],
+        w["enc_up"],
+        w["enc_down"],
     )
     p9_got = swap(p9)
-    total1 = scatter_pieces(
-        lay, grad_chunk(place, [eh1_low, gue, eg, gfe], up_terms + down_terms, 512)
-    )
-    gz1e, goe, gea_keep, gea_send, e_gain1, e_shift1, s_goe = branch_back(
-        place, gz2e, p9, p9_got, eunit1, einv1, eg_rows[0:1], w["enc"]
+    total_dd = next(r_dd)
+    next(r_cross)
+    total_du = next(r_du)
+    r_ed = grads([eg, gfe], down_terms, 128, D)
+    r_eu = grads([eh1_low, gue], up_terms, 256)
+    gz1e, goe, gea_keep, gea_send, e_gain1, e_shift1, s_goe = order.run(
+        branch_back, gz2e, p9, p9_got, eunit1, einv1, eg_rows[0:1], w["enc"]
     )
     gea_got = swap(gea_send)
-    geqkv, p10, p10_send, s_geqkv = enc_attention_back(
-        place, eqkv, gea_keep, gea_got, gz1e, w["enc"]
+    gqkv, grel, p8, p8_send, s_gqkv, s_grel = order.run(
+        ngram_back_kernel, dqkv, rel, gda_keep, gda_got, gz1, w["dec"]
+    )
+    p8_got = swap(p8_send)
+    next(r_ed)
+    next(r_eu)
+    total_cross = next(r_cross)
+    geqkv, p10, p10_send, s_geqkv = order.run(
+        enc_attention_back, eqkv, gea_keep, gea_got, gz1e, w["enc"]
     )
     p10_got = swap(p10_send)
+    r_dec = grads(
+        [y, gqkv, da_keep, da_got, go, grel],
+        [("plain", 64 * b, 0, 1, WIDE * b) for b in range(3)]
+        + [("heads", 192, 2, 4, 0), ("heads", 224, 2, 4, WIDE), ("rel", 256, 0, 5, 0)],
+        288,
+    )
+    total_ed = next(r_ed)
+    total_eu = next(r_eu)
 
     def widen(vector):
         zeros = jnp.zeros_like(vector)
@@ -2035,16 +2103,16 @@
     vec_grads = jnp.pad(vec_grads, ((0, 0), (0, padded - vec_width)))
     vec_grads = vec_grads.reshape(chips, vec_used, WIDE)
     vec_grads = jnp.pad(vec_grads, ((0, 0), (0, 16 - vec_used), (0, 0))).reshape(chips * 16, WIDE)
-    total0 = scatter_pieces(
-        lay,
-        grad_chunk(
-            place,
-            [x, geqkv, ea_keep, ea_got, goe, vec_grads],
-            [("plain", 64 * b, 0, 1, WIDE * b) for b in range(3)]
-            + [("heads", 192, 2, 4, 0), ("heads", 224, 2, 4, WIDE), ("whole", 256, 5, 5, 0)],
-            272,
-        ),
-    )
+    r_enc = grads(
+        [x, geqkv, ea_keep, ea_got, goe, vec_grads],
+        [("plain", 64 * b, 0, 1, WIDE * b) for b in range(3)]
+        + [("heads", 192, 2, 4, 0), ("heads", 224, 2, 4, WIDE), ("whole", 256, 5, 5, 0)],
+        272,
+    )
+    next(r_dec)
+    next(r_enc)
+    total2 = next(r_dec)
+    total0 = next(r_enc)
 
     def split_rows(total, sizes):
         at = 0
@@ -2075,18 +2143,18 @@
     vec_sum = t0[3][:vec_used].reshape(2, padded)
     vec_sum = pick(vec_sum[0], vec_sum[1]) + swap(pick(vec_sum[1], vec_sum[0]))
     o_vec = [vec_sum[starts[i] : starts[i + 1]] for i in range(4)]
-    t1 = split_rows(total1, [8 * r, f, f])
-    o_enc_up, o_enc_down = up_rows(own_rows_of(t1[0], 4)), side(t1[1], t1[2])
+    o_enc_up = up_rows(own_rows_of(total_eu, 4))
+    o_enc_down = total_ed
     t2 = split_rows(total2, [6 * r, r, r, r])
     o_dec_in, o_dec_out = in_rows(own_rows_of(t2[0], 3)), side(t2[1], t2[2])
     relp = t2[3].reshape(r, 2, REL_HALF)
     o_rel = pair(pick(relp[:, 0], relp[:, 1]), swap(pick(relp[:, 1], relp[:, 0])), 1)
-    t3 = split_rows(total3, [2 * r, 4 * r, r, r])
+    t3 = split_rows(total_cross, [2 * r, 4 * r, r, r])
     o_cross_q = in_rows(own_rows_of(t3[0], 1))
     o_cross_kv = in_rows(own_rows_of(t3[1], 2))
     o_cross_out = side(t3[2], t3[3])
-    t4 = split_rows(total4, [8 * r, f, f])
-    o_dec_up, o_dec_down = up_rows(own_rows_of(t4[0], 4)), side(t4[1], t4[2])
+    o_dec_up = up_rows(own_rows_of(total_du, 4))
+    o_dec_down = total_dd
 
     return (
         pick(enc_low[:LEN], enc_low[LEN:]),

time: 963 us -> 820 us (0.85); the launches traced: 945 us -> 812 us
  starting transfers between devices: 185 us -> 52.7 us
  between operations: 4.54 us -> 17.6 us
  waiting for transfers between devices: 370 us -> 360 us
    ppermute x30 -> x0, waiting for transfers between devices: 157 us -> none  [shift_z(): lax.ppermute(value, 'fsdp', [(i, (i + 2 * step) % self.nf) for i in range...]
    ppermute x30 -> x0, starting transfers between devices: 120 us -> none  [shift_z(): lax.ppermute(value, 'fsdp', [(i, (i + 2 * step) % self.nf) for i in range...]
    ppermute x60 -> x42, waiting for transfers between devices: 202 us -> 280 us  [flip_dp(): return lax.ppermute(value, 'dp', [(i, i ^ mask) for i in range(self.ndp)])]
    all_gather x0 -> x7, waiting for transfers between devices: none -> 55.5 us  [gather(): own = lax.all_gather(buf, 'fsdp', axis=0, axis_index_groups=self.groups)]
    another operation x30 -> x20, other arithmetic: 17.6 us -> 0.4 us
    ppermute x60 -> x42, starting transfers between devices: 59.9 us -> 46.8 us  [flip_dp(): return lax.ppermute(value, 'dp', [(i, i ^ mask) for i in range(self.ndp)])]
    reduce_scatter x0 -> x7, waiting for transfers between devices: none -> 12.3 us  [scatter(): lax.psum_scatter(total, 'fsdp', scatter_dimension=0, axis_index_groups=se...]
    select_n x26 -> x34, other arithmetic: 14.2 us -> 26 us  [pick(): return jnp.where(self.core == 0, first, second)]
  transfers between devices with their start and end apart: 120 -> 86, of which waited for: 45 -> 34; matrix products, arithmetic and copies ran while one was open for 12% -> 13% of each run, Pallas kernels for 20% -> 25%
where the time goes in v3:
time: 820 us; the launch traced here: 812 us
  waiting for transfers between devices  360 us (44%)
  Pallas kernels  257 us (31%)
  other arithmetic  73.5 us (9%)
  starting transfers between devices  52.7 us (6%)
  local copies, waits for them, and re-layouts  51.6 us (6%)
  between operations  17.6 us (2%)
    ppermute x42, waiting for transfers between devices, flip_dp(): return lax.ppermute(value, 'dp', [(i, i ^ mask) for i in range(self.ndp)])  280 us
    pallas_call x24, Pallas kernels, run(): pl.pallas_call(body, grid=(grid,), in_specs=[s for a, s in ins], out_spec...  257 us
    all_gather x7, waiting for transfers between devices, gather(): own = lax.all_gather(buf, 'fsdp', axis=0, axis_index_groups=self.groups)  55.5 us
    ppermute x42, starting transfers between devices, flip_dp(): return lax.ppermute(value, 'dp', [(i, i ^ mask) for i in range(self.ndp)])  46.8 us
    convert_element_type x14, other arithmetic, add_low(): return sum((v.astype(F32) for v in values)).astype(BF)  27.5 us
    select_n x34, other arithmetic, pick(): return jnp.where(self.core == 0, first, second)  26 us
  transfers between devices with their start and end apart: 86, of which 34 were waited for; matrix products, arithmetic and copies ran while one was open for 13% of the time, Pallas kernels for 25%

profile of v3, /device:TPU:0, one launch (start us, length us, event | category | flops | bytes accessed | tf_op | source)
XLA Modules:
  0.0 812.5 jit_solution(6403809140066788945)
XLA Ops:
  18.6 21.6 %all-gather.15.cloned.1.call-done = bf16[512,1024]{1,0:T(8,128)(2,1)} async-done(((bf16[128,1024]{1,0:T(8,128)(2,1)}), bf16[512,1024]{1,0:T(8,128)(2,1)}) %all-gather.15.cloned.1.call-update) | async-done | bytes 1048592 | tf_op jit(solution)/shard_map/all_gather | solution.py:1747
  43.5 25.8 %all-gather.19.cloned.1.call-done = bf16[512,1024]{1,0:T(8,128)(2,1)} async-done(((bf16[128,1024]{1,0:T(8,128)(2,1)}), bf16[512,1024]{1,0:T(8,128)(2,1)}) %all-gather.19.cloned.1.call-update) | async-done | bytes 1048592 | tf_op jit(solution)/shard_map/all_gather | solution.py:1747
  75.8 18.8 %collective-permute-done.5.refs_6_.refs_11_ = bf16[4,128,1024]{2,1,0:T(8,128)(2,1)} collective-permute-done((bf16[4,128,1024]{2,1,0:T(8,128)(2,1)}, bf16[4,128,1024]{2,1,0:T(8,128)(2,1)}, u32[]{:S(2)}, u32[]{:S(2)}) %collective-permute-start.5) | collective-permute-done | bytes 1048608 | tf_op jit(solution)/shard_map/ppermute | solution.py:143
  137.9 15.9 %collective-permute-done.15.refs_7_.refs_12_ = bf16[4,128,1024]{2,1,0:T(8,128)(2,1)} collective-permute-done((bf16[4,128,1024]{2,1,0:T(8,128)(2,1)S(1)}, bf16[4,128,1024]{2,1,0:T(8,128)(2,1)}, u32[]{:S(2)}, u32[]{:S(2)}) %collective-permute-start.15) | collective-permute-done | bytes 1048608 | tf_op jit(solution)/shard_map/ppermute | solution.py:143
  196.7 19.6 %collective-permute-done.21.refs_1_.refs_6_ = bf16[4,256,512]{2,1,0:T(8,128)(2,1)} collective-permute-done((bf16[4,256,512]{2,1,0:T(8,128)(2,1)}, bf16[4,256,512]{2,1,0:T(8,128)(2,1)}, u32[]{:S(2)}, u32[]{:S(2)}) %collective-permute-start.21) | collective-permute-done | bytes 1048608 | tf_op jit(solution)/shard_map/ppermute | solution.py:143
  219.0 18.9 %shard_map.366 = (bf16[768,1536]{1,0:T(8,128)(2,1)}, f32[768,256]{1,0:T(8,128)}, bf16[768,256]{1,0:T(8,128)(2,1)}, bf16[768,256]{1,0:T(8,128)(2,1)}) custom-call(s32[8]{0:T(128)} %concatenate.330.place, bf16[768,1024]{1,0:T(8,128)(2,1)} %maximum_select_fusion.y.refs_0_, f32[1,1536]{1,0:T(1,128)} %broadcast_in_dim.18.bias, f32[1,256]{1,0:T(1,128)} %bitcast.302, ...), custom_call_target="tpu_custom_call" | custom-call | bytes 57000000 | tf_op jit(solution)/shard_map/pallas_call | solution.py:743
  284.9 19.5 %collective-permute-done.28.refs_3_ = bf16[4,256,512]{2,1,0:T(8,128)(2,1)} collective-permute-done((bf16[4,256,512]{2,1,0:T(8,128)(2,1)S(1)}, bf16[4,256,512]{2,1,0:T(8,128)(2,1)}, u32[]{:S(2)}, u32[]{:S(2)}) %collective-permute-start.28) | collective-permute-done | bytes 1048608 | tf_op jit(solution)/shard_map/ppermute | solution.py:143
  304.4 14.8 %shard_map.371 = (f32[768,1024]{1,0:T(8,128)}, f32[768,128]{1,0:T(8,128)}, bf16[768,1024]{1,0:T(8,128)(2,1)}, f32[256,1024]{1,0:T(8,128)}, f32[256,128]{1,0:T(8,...) custom-call(s32[8]{0:T(128)} %concatenate.330.place, ...), custom_call_target="tpu_custom_call" | custom-call | bytes 45000000 | tf_op jit(solution)/shard_map/pallas_call | solution.py:743
  330.8 21.0 %collective-permute-done.31.refs_1_.refs_5_ = bf16[4,256,512]{2,1,0:T(8,128)(2,1)S(1)} collective-permute-done((bf16[4,256,512]{2,1,0:T(8,128)(2,1)S(1)}, bf16[4,256,512]{2,1,0:T(8,128)(2,1)S(1)}, u32[]{:S(2)}, u32[]{:S(2)}) %collective-permute-start.31) | collective-permute-done | bytes 1048608 | tf_op jit(solution)/shard_map/ppermute | solution.py:143
  351.8 22.0 %collective-permute-done.33.refs_3_.refs_7_ = bf16[4,256,512]{2,1,0:T(8,128)(2,1)} collective-permute-done((bf16[4,256,512]{2,1,0:T(8,128)(2,1)S(1)}, bf16[4,256,512]{2,1,0:T(8,128)(2,1)}, u32[]{:S(2)}, u32[]{:S(2)}) %collective-permute-start.33) | collective-permute-done | bytes 1048608 | tf_op jit(solution)/shard_map/ppermute | solution.py:143
  373.8 21.7 %shard_map.373 = (f32[768,1024]{1,0:T(8,128)}, f32[768,128]{1,0:T(8,128)}, bf16[768,1024]{1,0:T(8,128)(2,1)}, bf16[768,2048]{1,0:T(8,128)(2,1)}, bf16[768,2048]{1,0:T(8,128)(2,1)}, /*index=5*/bf16[768,1024]{1,0:T(8,128)(2,1)}) custom-call(s32[8]{0:T(128)} %concatenate.330.place, f32[768,1024]{1,0:T(8,128)} %get-tuple-element.222.base.unit, ...), custom_call_target="tpu_custom_call" | custom-call | bytes 60000000 | tf_op jit(solution)/shard_map/pallas_call | solution.py:743
  400.4 21.1 %shard_map.374 = (bf16[384,1024]{1,0:T(8,128)(2,1)}, f32[768,1024]{1,0:T(8,128)}, bf16[768,1024]{1,0:T(8,128)(2,1)}, bf16[768,2048]{1,0:T(8,128)(2,1)}, bf16[768...) custom-call(s32[8]{0:T(128)} %concatenate.330.place, ...), custom_call_target="tpu_custom_call" | custom-call | bytes 63000000 | tf_op jit(solution)/shard_map/pallas_call | solution.py:743
  467.2 14.1 %shard_map.378 = (bf16[768,512]{1,0:T(8,128)(2,1)}, bf16[256,1024]{1,0:T(8,128)(2,1)}, bf16[1024,1024]{1,0:T(8,128)(2,1)}, f32[1,512]{1,0:T(1,128)}, f32[1,1024]{1,0:T(1,128)}) custom-call(s32[8]{0:T(128)} %concatenate.330.place, bf16[768,512]{1,0:T(8,128)(2,1)} %get-tuple-element.256.q, bf16[256,1024]{1,0:T(8,128)(2,1)} %get-tuple-element.257.kv, ...), custom_call_target="tpu_custom_call" | custom-call | bytes 42000000 | tf_op jit(solution)/shard_map/pallas_call | solution.py:743
  495.6 10.9 %shard_map.380 = (f32[768,1024]{1,0:T(8,128)}, bf16[768,1024]{1,0:T(8,128)(2,1)}, bf16[768,256]{1,0:T(8,128)(2,1)}, bf16[768,256]{1,0:T(8,128)(2,1)}, f32[1,1024...) custom-call(s32[8]{0:T(128)} %concatenate.330.place, f32[768,1024]{1,0:T(8,128)} %get-tuple-element.250.resid, ...), custom_call_target="tpu_custom_call" | custom-call | bytes 30000000 | tf_op jit(solution)/shard_map/pallas_call | solution.py:743
  507.1 11.8 %shard_map.381 = (f32[256,1024]{1,0:T(8,128)}, bf16[256,1024]{1,0:T(8,128)(2,1)}, bf16[256,2048]{1,0:T(8,128)(2,1)}, bf16[256,1024]{1,0:T(8,128)(2,1)}, f32[1,10...) custom-call(s32[8]{0:T(128)} %concatenate.330.place, f32[5,1024]{1,0:T(8,128)} %stack.35.vecs, ...), custom_call_target="tpu_custom_call" | custom-call | bytes 36000000 | tf_op jit(solution)/shard_map/pallas_call | solution.py:743
  531.7 20.5 %collective-permute-done.44 = bf16[4,256,512]{2,1,0:T(8,128)(2,1)} collective-permute-done((bf16[4,256,512]{2,1,0:T(8,128)(2,1)S(1)}, bf16[4,256,512]{2,1,0:T(8,128)(2,1)}, u32[]{:S(2)}, u32[]{:S(2)}) %collective-permute-start.44) | collective-permute-done | bytes 1048608 | tf_op jit(solution)/shard_map/ppermute | solution.py:143
  578.0 28.7 %shard_map.385 = (bf16[768,1536]{1,0:T(8,128)(2,1)}, bf16[768,256]{1,0:T(8,128)(2,1)}, f32[384,1024]{1,0:T(8,128)}, bf16[384,1024]{1,0:T(8,128)(2,1)}, f32[1,1536]{1,0:T(1,128)}, /*index=5*/f32[1,256]{1,0:T(1,128)}) custom-call(s32[8]{0:T(128)} %concatenate.330.place, bf16[768,1536]{1,0:T(8,128)(2,1)} %get-tuple-element.195.qkv, ...), custom_call_target="tpu_custom_call" | custom-call | bytes 87000000 | tf_op jit(solution)/shard_map/pallas_call | solution.py:743
  626.9 12.8 %shard_map.386 = (bf16[256,1536]{1,0:T(8,128)(2,1)}, f32[128,1024]{1,0:T(8,128)}, bf16[128,1024]{1,0:T(8,128)(2,1)}, f32[1,1536]{1,0:T(1,128)}) custom-call(s32[8]{0:T(128)} %concatenate.330.place, bf16[256,1536]{1,0:T(8,128)(2,1)} %get-tuple-element.202.qkv, bf16[256,256]{1,0:T(8,128)(2,1)} %get-tuple-element.308.keep, bf16[256,256]{1,0:T(8,128)(2,1)} %copy-done.57, ...), custom_call_target="tpu_custom_call" | custom-call | bytes 39000000 | tf_op jit(solution)/shard_map/pallas_call | solution.py:743
  639.7 10.8 %shard_map.387 = (bf16[4,288,512]{2,1,0:T(8,128)(2,1)}, bf16[4,288,512]{2,1,0:T(8,128)(2,1)}, bf16[4,288,512]{2,1,0:T(8,128)(2,1)}, bf16[4,288,512]{2,1,0:T(8,128)(2,1)}) custom-call(s32[8]{0:T(128)} %concatenate.330.place, bf16[768,1024]{1,0:T(8,128)(2,1)} %maximum_select_fusion.y.refs_0_, bf16[768,1536]{1,0:T(8,128)(2,1)} %get-tuple-element.300.refs_1_, ...), custom_call_target="tpu_custom_call" | custom-call | bytes 30000000 | tf_op jit(solution)/shard_map/pallas_call | solution.py:743
  653.8 14.3 %collective-permute-done.57 = bf16[4,256,512]{2,1,0:T(8,128)(2,1)} collective-permute-done((bf16[4,256,512]{2,1,0:T(8,128)(2,1)}, bf16[4,256,512]{2,1,0:T(8,128)(2,1)}, u32[]{:S(2)}, u32[]{:S(2)}) %collective-permute-start.57) | collective-permute-done | bytes 1048608 | tf_op jit(solution)/shard_map/ppermute | solution.py:143
  685.6 15.6 %collective-permute-done.58 = bf16[4,288,512]{2,1,0:T(8,128)(2,1)S(1)} collective-permute-done((bf16[4,288,512]{2,1,0:T(8,128)(2,1)}, bf16[4,288,512]{2,1,0:T(8,128)(2,1)S(1)}, u32[]{:S(2)}, u32[]{:S(2)}) %collective-permute-start.58) | collective-permute-done | bytes 1179680 | tf_op jit(solution)/shard_map/ppermute | solution.py:143
  712.1 12.1 %collective-permute-done.60 = bf16[4,288,512]{2,1,0:T(8,128)(2,1)S(1)} collective-permute-done((bf16[4,288,512]{2,1,0:T(8,128)(2,1)}, bf16[4,288,512]{2,1,0:T(8,128)(2,1)S(1)}, u32[]{:S(2)}, u32[]{:S(2)}) %collective-permute-start.60) | collective-permute-done | bytes 1179680 | tf_op jit(solution)/shard_map/ppermute | solution.py:143
  752.1 16.1 %collective-permute-done.63 = bf16[4,272,512]{2,1,0:T(8,128)(2,1)} collective-permute-done((bf16[4,272,512]{2,1,0:T(8,128)(2,1)}, bf16[4,272,512]{2,1,0:T(8,128)(2,1)}, u32[]{:S(2)}, u32[]{:S(2)}) %collective-permute-start.63) | collective-permute-done | bytes 1114144 | tf_op jit(solution)/shard_map/ppermute | solution.py:143
  786.9 12.3 %reduce-scatter.8.cloned.1.call-done = bf16[1,272,512]{2,1,0:T(8,128)(2,1)} async-done(((bf16[4,272,512]{2,1,0:T(8,128)(2,1)}), bf16[1,272,512]{2,1,0:T(8,128)(2,1)}) %reduce-scatter.8.cloned.1.call-update) | async-done | bytes 278544 | tf_op jit(solution)/shard_map/reduce_scatter | solution.py:1767
  (638 shorter events, 374.1 us)
Async XLA Ops:
  7.9 61.4 %all-gather.19.cloned.1.call-start = ((), (), s32[]{:S(2)}) async-start(), calls=%async_computation.16 | async-start | bytes 1310720 | tf_op jit(solution)/shard_map/all_gather | solution.py:1747
  16.6 85.9 %all-gather.17.cloned.1.call-start = ((), (), s32[]{:S(2)}) async-start(), calls=%async_computation.15 | async-start | bytes 1556480 | tf_op jit(solution)/shard_map/all_gather | solution.py:1747
  40.3 113.5 %all-gather.21.cloned.1.call-start = ((), (), s32[]{:S(2)}) async-start(), calls=%async_computation.17 | async-start | bytes 1310720 | tf_op jit(solution)/shard_map/all_gather | solution.py:1747
  69.3 96.0 %all-gather.23.cloned.1.call-start = ((), (), s32[]{:S(2)}) async-start(), calls=%async_computation.18 | async-start | bytes 1310720 | tf_op jit(solution)/shard_map/all_gather | solution.py:1747
  72.4 103.5 %collective-permute-start.11 = (bf16[384,1024]{1,0:T(8,128)(2,1)}, bf16[384,1024]{1,0:T(8,128)(2,1)}, u32[]{:S(2)}, u32[]{:S(2)}) collective-permute-start(bf16[384,1024]{1,0:T(8,128)(2,1)} %bitcast.11), channel_id=1, source_target_pairs={{0,1},{1,0},{2,3},{3,2},{4,5},{5,4},{6,7},{7,6},{8,9},{9,8},{10,11... | collective-permute-start | bytes 2359304 | tf_op jit(solution)/shard_map/ppermute | solution.py:135
  72.4 49.1 %collective-permute-start.10 = (bf16[128,1024]{1,0:T(8,128)(2,1)}, bf16[128,1024]{1,0:T(8,128)(2,1)}, u32[]{:S(2)}, u32[]{:S(2)}) collective-permute-start(bf16[128,1024]{1,0:T(8,128)(2,1)} %param.22), channel_id=1, source_target_pairs={{0,1},{1,0},{2,3},{3,2},{4,5},{5,4},{6,7},{7,6},{8,9},{9,8},{10,11... | collective-permute-start | bytes 786440 | tf_op jit(solution)/shard_map/ppermute | solution.py:135
  73.0 46.5 %collective-permute-start.8 = (bf16[4,128,1024]{2,1,0:T(8,128)(2,1)}, bf16[4,128,1024]{2,1,0:T(8,128)(2,1)S(1)}, u32[]{:S(2)}, u32[]{:S(2)}) collective-permute-start(bf16[4,128,1024]{2,1,0:T(8,128)(2,1)} %bitcast.232), channel_id=1, source_target_pairs={{0,8},{8,0},{16,24},{24,16},{1,9},{9,1},{17,25},{25,17},{2,10},{10... | collective-permute-start | bytes 3145736 | tf_op jit(solution)/shard_map/ppermute | solution.py:143
  105.7 91.0 %all-gather.25.cloned.1.call-start = ((), (), s32[]{:S(2)}) async-start(), calls=%async_computation.19 | async-start | bytes 1310720 | tf_op jit(solution)/shard_map/all_gather | solution.py:1747
  105.7 48.1 %collective-permute-start.4 = (bf16[4,304,512]{2,1,0:T(8,128)(2,1)}, bf16[4,304,512]{2,1,0:T(8,128)(2,1)S(1)}, u32[]{:S(2)}, u32[]{:S(2)}) collective-permute-start(bf16[4,304,512]{2,1,0:T(8,128)(2,1)} %bitcast.211), channel_id=1, source_target_pairs={{0,8},{8,0},{16,24},{24,16},{1,9},{9,1},{17,25},{25,17},{2,10},{10... | collective-permute-start | bytes 3735560 | tf_op jit(solution)/shard_map/ppermute | solution.py:143
  156.8 121.8 %all-gather.27.cloned.1.call-start = ((), (), s32[]{:S(2)}) async-start(), calls=%async_computation.20 | async-start | bytes 1310720 | tf_op jit(solution)/shard_map/all_gather | solution.py:1747
  183.1 55.8 %collective-permute-start.22 = (bf16[4,256,512]{2,1,0:T(8,128)(2,1)}, bf16[4,256,512]{2,1,0:T(8,128)(2,1)}, u32[]{:S(2)}, u32[]{:S(2)}) collective-permute-start(bf16[4,256,512]{2,1,0:T(8,128)(2,1)} %bitcast.22.refs_0_.refs_5_), channel_id=1, source_target_pairs={{0,16},{8,24},{16,0},{24,8},{1,17},{9,25},{17,1},{25,9},{2,18},{10... | collective-permute-start | bytes 3145736 | tf_op jit(solution)/shard_map/ppermute | solution.py:143
  216.3 46.5 %collective-permute-start.26 = (bf16[4,256,512]{2,1,0:T(8,128)(2,1)}, bf16[4,256,512]{2,1,0:T(8,128)(2,1)S(1)}, u32[]{:S(2)}, u32[]{:S(2)}) collective-permute-start(bf16[4,256,512]{2,1,0:T(8,128)(2,1)} %bitcast.225), channel_id=1, source_target_pairs={{0,8},{8,0},{16,24},{24,16},{1,9},{9,1},{17,25},{25,17},{2,10},{10... | collective-permute-start | bytes 3145736 | tf_op jit(solution)/shard_map/ppermute | solution.py:143
  238.7 501.0 %reduce-scatter.18.cloned.1.call-start = ((), (), s32[]{:S(2)}) async-start(), calls=%async_computation.12 | async-start | bytes 1310720 | tf_op jit(solution)/shard_map/reduce_scatter | solution.py:1767
  325.7 48.2 %collective-permute-start.30 = (bf16[768,1024]{1,0:T(8,128)(2,1)}, bf16[768,1024]{1,0:T(8,128)(2,1)}, u32[]{:S(2)}, u32[]{:S(2)}) collective-permute-start(bf16[768,1024]{1,0:T(8,128)(2,1)} %shard_map.372.own), channel_id=1, source_target_pairs={{0,1},{1,0},{2,3},{3,2},{4,5},{5,4},{6,7},{7,6},{8,9},{9,8},{10,11... | collective-permute-start | bytes 4718600 | tf_op jit(solution)/shard_map/ppermute | solution.py:135
  327.3 46.5 %collective-permute-start.33 = (bf16[4,256,512]{2,1,0:T(8,128)(2,1)S(1)}, bf16[4,256,512]{2,1,0:T(8,128)(2,1)}, u32[]{:S(2)}, u32[]{:S(2)}) collective-permute-start(bf16[4,256,512]{2,1,0:T(8,128)(2,1)S(1)} %collective-permute-done.32.refs_2_.refs_6_), channel_id=1, source_target_pairs={{0,8},{8,0},{16,24},{24,16},{1,9},{9,1},{17,25},{25,17},{2,10},{10... | collective-permute-start | bytes 3145736 | tf_op jit(solution)/shard_map/ppermute | solution.py:143
  494.0 58.2 %collective-permute-start.44 = (bf16[4,256,512]{2,1,0:T(8,128)(2,1)S(1)}, bf16[4,256,512]{2,1,0:T(8,128)(2,1)}, u32[]{:S(2)}, u32[]{:S(2)}) collective-permute-start(bf16[4,256,512]{2,1,0:T(8,128)(2,1)S(1)} %add_convert_fusion.12), channel_id=1, source_target_pairs={{0,16},{8,24},{16,0},{24,8},{1,17},{9,25},{17,1},{25,9},{2,18},{10... | collective-permute-start | bytes 3145736 | tf_op jit(solution)/shard_map/ppermute | solution.py:143
  555.5 189.5 %reduce-scatter.20.cloned.1.call-start = ((), (), s32[]{:S(2)}) async-start(), calls=%async_computation.13 | async-start | bytes 1310720 | tf_op jit(solution)/shard_map/reduce_scatter | solution.py:1767
  556.3 192.9 %reduce-scatter.16.cloned.1.call-start = ((), (), s32[]{:S(2)}) async-start(), calls=%async_computation.11 | async-start | bytes 1310720 | tf_op jit(solution)/shard_map/reduce_scatter | solution.py:1767
  570.3 46.8 %collective-permute-start.50 = (bf16[4,256,512]{2,1,0:T(8,128)(2,1)}, bf16[4,256,512]{2,1,0:T(8,128)(2,1)}, u32[]{:S(2)}, u32[]{:S(2)}) collective-permute-start(bf16[4,256,512]{2,1,0:T(8,128)(2,1)} %get-tuple-element.306), channel_id=1, source_target_pairs={{0,16},{8,24},{16,0},{24,8},{1,17},{9,25},{17,1},{25,9},{2,18},{10... | collective-permute-start | bytes 3145736 | tf_op jit(solution)/shard_map/ppermute | solution.py:143
  620.1 154.4 %reduce-scatter.10.cloned.1.call-start = ((), (), s32[]{:S(2)}) async-start(), calls=%async_computation.8 | async-start | bytes 1310720 | tf_op jit(solution)/shard_map/reduce_scatter | solution.py:1767
  671.4 105.9 %reduce-scatter.12.cloned.1.call-start = ((), (), s32[]{:S(2)}) async-start(), calls=%async_computation.9 | async-start | bytes 1310720 | tf_op jit(solution)/shard_map/reduce_scatter | solution.py:1767
  676.0 105.4 %reduce-scatter.14.cloned.1.call-start = ((), (), s32[]{:S(2)}) async-start(), calls=%async_computation.10 | async-start | bytes 1474560 | tf_op jit(solution)/shard_map/reduce_scatter | solution.py:1767
  677.1 47.1 %collective-permute-start.60 = (bf16[4,288,512]{2,1,0:T(8,128)(2,1)}, bf16[4,288,512]{2,1,0:T(8,128)(2,1)S(1)}, u32[]{:S(2)}, u32[]{:S(2)}) collective-permute-start(bf16[4,288,512]{2,1,0:T(8,128)(2,1)} %get-tuple-element.355), channel_id=1, source_target_pairs={{0,8},{8,0},{16,24},{24,16},{1,9},{9,1},{17,25},{25,17},{2,10},{10... | collective-permute-start | bytes 3538952 | tf_op jit(solution)/shard_map/ppermute | solution.py:143
  735.8 63.4 %reduce-scatter.8.cloned.1.call-start = ((), (), s32[]{:S(2)}) async-start(), calls=%async_computation.7 | async-start | bytes 1392640 | tf_op jit(solution)/shard_map/reduce_scatter | solution.py:1767
  (165 other events, 3261.1 us)
Sparse Core Ops, SparseCore 0:
  9.6 30.6 all-gather.14
  41.8 27.4 all-gather.18
  71.4 31.0 all-gather.16
  104.5 26.9 all-gather.20
  133.6 27.4 all-gather.22
  163.0 27.4 all-gather.24
  238.8 26.0 all-gather.26
  555.6 26.9 reduce-scatter.17
  585.0 25.7 reduce-scatter.19
  620.2 26.0 reduce-scatter.15
  671.6 26.9 reduce-scatter.9
  700.7 25.7 reduce-scatter.11
  735.9 28.6 reduce-scatter.13
  772.4 26.7 reduce-scatter.7

commit v4 on v3

--- a/solution.py
+++ b/solution.py
@@ -733,9 +733,10 @@
     )
 
 
-BUDGET = 58 * 1024 * 1024
+BUDGET = 36 * 1024 * 1024
 PIECES = 4
-HBM_RATE = 3.0e6
+HBM_RATE = 1.0e6
+FLOP_RATE = 1.0e9
 
 
 def run(body, grid, ins, outs, scratch=(), us=5):
@@ -749,7 +750,7 @@
         scratch_shapes=list(scratch),
         compiler_params=pltpu.CompilerParams(vmem_limit_bytes=BUDGET),
         cost_estimate=pl.CostEstimate(
-            flops=0, bytes_accessed=int(us * HBM_RATE), transcendentals=0
+            flops=int(us * FLOP_RATE), bytes_accessed=int(us * HBM_RATE), transcendentals=0
         ),
     )(*arrays)
 
@@ -951,32 +952,56 @@
     each_tile(rows, LEN, step)
 
 
+def norm_forward(place, base, affine, own, other, vecs):
+    rows = base.shape[0]
+
+    def body(place, base, own, other, vecs, unit, inv, low):
+        aff = (vecs[0:1], vecs[1:2]) if affine else None
+        norm_tiles(LEN, base, aff, own, other, vecs[2:3], vecs[3:4], vecs[4:5], unit, inv, low)
+
+    def tiles(array):
+        return array, pl.BlockSpec((LEN, array.shape[1]), lambda t: (t, 0))
+
+    def out(width, dtype):
+        return jax.ShapeDtypeStruct((rows, width), dtype), pl.BlockSpec((LEN, width), lambda t: (t, 0))
+
+    return run(
+        body,
+        rows // LEN,
+        [small(place), tiles(base), tiles(own), tiles(other), full(vecs)],
+        [out(D, F32), out(128, F32), out(D, BF)],
+        us=4,
+    )
+
+
 ROOT_HALF = math.sqrt(0.5)
 ROOT_TWO_PI = math.sqrt(0.5 / math.pi)
+TAIL = (0.254829592, -0.284496736, 1.421413741, -1.453152027, 1.061405429)
 
 
 def gelu_pair(u):
-    phi = 0.5 + 0.5 * lax.erf(u * ROOT_HALF)
-    return u * phi, phi + u * (jnp.exp(-0.5 * u * u) * ROOT_TWO_PI)
-
-
-def ffn_forward(place, base, affine, own, other, vecs, hidden_bias, up_pieces, down_pieces):
-    rows = base.shape[0]
+    depth = 1.0 + (0.3275911 * ROOT_HALF) * jnp.abs(u)
+    t = pl.reciprocal(depth, approx=True)
+    t = t * (2.0 - depth * t)
+    bell = jnp.exp(-0.5 * u * u)
+    poly = TAIL[4]
+    for c in TAIL[3::-1]:
+        poly = poly * t + c
+    tail = (0.5 * t) * poly * bell
+    phi = jnp.where(u < 0.0, tail, 1.0 - tail)
+    return u * phi, phi + u * (bell * ROOT_TWO_PI)
+
+
+def ffn_forward(place, low, hidden_bias, up_pieces, down_pieces):
+    rows = low.shape[0]
     hidden = hidden_bias.shape[1]
     ups = hidden // WIDE
     tile = 256
 
-    def body(place, base, own, other, vecs, hb, *refs):
+    def body(place, low, hb, *refs):
         wu, wd = refs[:PIECES], refs[PIECES : 2 * PIECES]
-        unit, inv, low, g, gp, part, scr_u, scr_d, acts = refs[2 * PIECES :]
+        g, gp, part, scr_u, scr_d, acts = refs[2 * PIECES :]
         t = pl.program_id(0)
-
-        @pl.when(t == 0)
-        def _():
-            aff = (vecs[0:1], vecs[1:2]) if affine else None
-            norm_tiles(
-                rows, base, aff, own, other, vecs[2:3], vecs[3:4], vecs[4:5], unit, inv, low
-            )
 
         @pl.when(t < ups)
         def _():
@@ -1003,19 +1028,16 @@
     return run(
         body,
         ups + 2,
-        [small(place), full(base), full(own), full(other), full(vecs), in_cols(hidden_bias, up)]
+        [small(place), full(low), in_cols(hidden_bias, up)]
         + blocks(up_pieces, 64, up)
         + wide_blocks(down_pieces, down),
         [
-            out_full((rows, D), F32),
-            out_full((rows, 128), F32),
-            out_full((rows, D), BF),
             out_cols(rows, hidden, BF, up),
             out_cols(rows, hidden, BF, up),
             out_cols(rows, D, BF, down),
         ],
         [weight_scratch(64), weight_scratch(128), pltpu.VMEM((rows, hidden), BF)],
-        us=20 if rows > 256 else 11,
+        us=14 if rows > 256 else 8,
     )
 
 
@@ -1237,61 +1259,99 @@
     return inverse * (scaled - one - unit * two)
 
 
-def ffn_back(place, final, total_ins, unit_ins, vecs, gp, up_pieces, down_pieces):
-    rows, hidden = gp.shape
-    ups = hidden // WIDE
+def norm_backward(place, final, total_ins, unit_ins, vecs):
+    rows = total_ins[0].shape[0]
     n_total, n_unit = len(total_ins), len(unit_ins)
-    mine = rows // 2
-
-    def body(place, vecs, gp, *refs):
-        at = 0
-
-        def take_refs(n):
-            nonlocal at
-            at += n
-            return refs[at - n : at]
-
-        tot, uni = take_refs(n_total), take_refs(n_unit)
-        wu, wd = take_refs(PIECES), take_refs(PIECES)
-        outs = take_refs(1) if final else ()
-        gz, gf, gu, part, s_gain, s_shift, s_gf, s_gu = take_refs(8)
-        scr_u, scr_d, all_u, scr_all_u, acc = refs[at:]
+    steps = rows // LEN
+    mine = steps // 2
+
+    def body(place, vecs, *refs):
+        tot, uni = refs[:n_total], refs[n_total : n_total + n_unit]
+        *outs, gz, gf, s_gain, s_shift, s_gf, acc = refs[n_total + n_unit :]
         t = pl.program_id(0)
 
         @pl.when(t == 0)
         def _():
             acc[...] = jnp.zeros_like(acc)
 
-            def step(r):
-                here = pl.ds(r, LEN)
-                if final:
-                    v = uni[0][here] * vecs[0:1] + vecs[1:2]
-                    v = v + (uni[1][here].astype(F32) + uni[2][here].astype(F32)) + vecs[2:3]
-                    unit, inverse = stats(v)
-
-                    @pl.when((r >= mine) == (place[2] == 1))
-                    def _():
-                        to = pl.ds(pl.multiple_of(r - mine * place[2], LEN), LEN)
-                        outs[0][to] = (unit * vecs[3:4] + vecs[4:5]).astype(BF)
-
-                else:
-                    unit, inverse = uni[0][here], uni[1][here, 0:1]
-                total = tot[0][here].astype(F32)
-                if n_total > 1:
-                    there = pl.ds(r + tot[1].shape[0] - rows, LEN)
-                    total = total + (tot[1][there].astype(F32) + tot[2][there].astype(F32))
-                acc[0:8] += fold(total * unit)
-                acc[8:16] += fold(total)
-                back = norm_back_tile(total, unit, inverse, vecs[3:4])
-                gz[here] = back
-                low = back.astype(BF)
-                gf[here] = low
-                acc[16:24] += fold(low.astype(F32))
-
-            each_tile(rows, LEN, step)
+        if final:
+            v = uni[0][...] * vecs[0:1] + vecs[1:2]
+            v = v + (uni[1][...].astype(F32) + uni[2][...].astype(F32)) + vecs[2:3]
+            unit, inverse = stats(v)
+
+            @pl.when((t >= mine) == (place[2] == 1))
+            def _():
+                outs[0][...] = (unit * vecs[3:4] + vecs[4:5]).astype(BF)
+
+        else:
+            unit, inverse = uni[0][...], uni[1][:, 0:1]
+        total = tot[0][...].astype(F32)
+        if n_total > 1:
+            total = total + (tot[1][...].astype(F32) + tot[2][...].astype(F32))
+        acc[0:8] += fold(total * unit)
+        acc[8:16] += fold(total)
+        back = norm_back_tile(total, unit, inverse, vecs[3:4])
+        gz[...] = back
+        low = back.astype(BF)
+        gf[...] = low
+        acc[16:24] += fold(low.astype(F32))
+
+        @pl.when(t == steps - 1)
+        def _():
             s_gain[...] = jnp.sum(acc[0:8], axis=0, keepdims=True)
             s_shift[...] = jnp.sum(acc[8:16], axis=0, keepdims=True)
             s_gf[...] = jnp.sum(acc[16:24], axis=0, keepdims=True)
+
+    def tiles(array):
+        skip = (array.shape[0] - rows) // LEN
+        return array, pl.BlockSpec((LEN, array.shape[1]), lambda t: (t + skip, 0))
+
+    def out(dtype):
+        return jax.ShapeDtypeStruct((rows, D), dtype), pl.BlockSpec((LEN, D), lambda t: (t, 0))
+
+    def own_tile(t, place):
+        return (jnp.clip(t - mine * place[2], 0, mine - 1), 0)
+
+    outs = [out(F32), out(BF)] + [out_full((1, D), F32)] * 3
+    specs = [s for a, s in outs]
+    shapes = [a for a, s in outs]
+    ins = [full(vecs)] + [tiles(a) for a in total_ins + unit_ins]
+
+    def with_place(spec):
+        index = spec.index_map
+        return pl.BlockSpec(
+            spec.block_shape, lambda t, place: index(t), pipeline_mode=spec.pipeline_mode
+        )
+
+    specs = [with_place(s) for s in specs]
+    if final:
+        shapes = [jax.ShapeDtypeStruct((rows // 2, D), BF)] + shapes
+        specs = [pl.BlockSpec((LEN, D), own_tile)] + specs
+    return pl.pallas_call(
+        body,
+        grid_spec=pltpu.PrefetchScalarGridSpec(
+            num_scalar_prefetch=1,
+            grid=(steps,),
+            in_specs=[with_place(s) for a, s in ins],
+            out_specs=specs,
+            scratch_shapes=[pltpu.VMEM((24, D), F32)],
+        ),
+        out_shape=shapes,
+        compiler_params=pltpu.CompilerParams(vmem_limit_bytes=BUDGET),
+        cost_estimate=pl.CostEstimate(
+            flops=int(5 * FLOP_RATE), bytes_accessed=int(5 * HBM_RATE), transcendentals=0
+        ),
+    )(place, *[a for a, s in ins])
+
+
+def ffn_back(place, gf, gp, up_pieces, down_pieces):
+    rows, hidden = gp.shape
+    ups = hidden // WIDE
+
+    def body(place, gf, gp, *refs):
+        wu, wd = refs[:PIECES], refs[PIECES : 2 * PIECES]
+        gu, part, s_gu, scr_u, scr_d, all_u, scr_all_u = refs[2 * PIECES :]
+        t = pl.program_id(0)
 
         @pl.when(t < 2)
         def _():
@@ -1316,34 +1376,24 @@
 
     up = lambda t: jnp.maximum(t - 2, 0)
     down = lambda t: jnp.minimum(t, 1)
-    outs = [out_full((mine, D), BF)] if final else []
-    outs += [
-        out_full((rows, D), F32),
-        out_full((rows, D), BF),
-        out_cols(rows, hidden, BF, up),
-        out_full((rows, D), BF),
-        out_full((1, D), F32),
-        out_full((1, D), F32),
-        out_full((1, D), F32),
-        out_cols(1, hidden, F32, up),
-    ]
     return run(
         body,
         ups + 2,
-        [small(place), full(vecs), in_cols(gp, up)]
-        + [full(a) for a in total_ins]
-        + [full(a) for a in unit_ins]
+        [small(place), full(gf), in_cols(gp, up)]
         + blocks(up_pieces, 64, up)
         + wide_blocks(down_pieces, down),
-        outs,
+        [
+            out_cols(rows, hidden, BF, up),
+            out_full((rows, D), BF),
+            out_cols(1, hidden, F32, up),
+        ],
         [
             weight_scratch(64),
             pltpu.VMEM((2, 4, 4, 128, WIDE), BF),
             pltpu.VMEM((rows, hidden), BF),
             pltpu.VMEM((D, hidden), BF),
-            pltpu.VMEM((24, D), F32),
         ],
-        us=21 if rows > 256 else 12,
+        us=14 if rows > 256 else 8,
     )
 
 
@@ -1713,10 +1763,16 @@
         self.last = out[0] if isinstance(out, (list, tuple)) else out
         return out
 
-    def add(self, first, *others):
+    def matmul(self, left, right):
+        if self.last is not None:
+            right = tie(right, self.last)
+        self.last = dot_g(left, right).astype(BF)
+        return self.last
+
+    def add(self, first, *others, dtype=BF):
         if self.last is not None:
             first = tie(first, self.last)
-        self.last = add_low(first, *others)
+        self.last = sum((v.astype(F32) for v in others), first.astype(F32)).astype(dtype)
         return self.last
 
 
@@ -1724,46 +1780,66 @@
 
     def __init__(self, lay):
         self.lay = lay
-        self.sent = {1: [], 2: []}
         self.gathered = []
+        self.first = []
+        self.second = []
         self.far = 2
         self.groups = [list(range(core, lay.nf, 2)) for core in range(2)]
-
-    def send(self, value, mask):
-        queue = self.sent[mask]
-        if len(queue) >= 2:
-            value = tie(value, queue[-2])
-        queue.append(self.lay.flip_dp(value, mask))
-        return queue[-1]
 
     def turn(self):
         self.far = 3 - self.far
         return self.far
 
-    def gather(self, buf):
-        far = self.turn()
+    def gather(self, buf, direct=False):
+        far = 3 if direct else self.turn()
         if len(self.gathered) >= 2:
             buf = tie(buf, self.gathered[-2])
         own = lax.all_gather(buf, "fsdp", axis=0, axis_index_groups=self.groups)
         self.gathered.append(own)
-        x, y = self.send(own, 1), self.send(own, 2)
-        d = self.send(x, 2) if far == 2 else self.send(y, 1)
+        ready = own
+        if self.first:
+            ready = tie(ready, *self.first[-1])
+        if len(self.second) >= 3:
+            ready = tie(ready, self.second[-3])
+        x, y = self.lay.flip_dp(ready, 1), self.lay.flip_dp(ready, 2)
+        self.first.append((x, y))
+        if direct:
+            d = self.lay.flip_dp(ready, 3)
+        else:
+            d = self.lay.flip_dp(x, 2) if far == 2 else self.lay.flip_dp(y, 1)
+        self.second.append(d)
         return [own, x, y, d]
 
-    def scatter(self, order, parts):
-        far = self.turn()
+    def scatter_whole(self, value):
+        lay = self.lay
+        groups = [
+            [dp * lay.nf + fs for dp in range(lay.ndp) for fs in range(core, lay.nf, 2)]
+            for core in range(2)
+        ]
+        return lax.psum_scatter(
+            value, ("dp", "fsdp"), scatter_dimension=0, tiled=True, axis_index_groups=groups
+        ).astype(F32)
+
+    def scatter(self, order, parts, direct=False):
         own, x, y, d = parts
-        d = self.lay.flip_dp(d, far)
-        if far == 2:
-            y = self.lay.flip_dp(y, 2)
+        if direct:
+            moved = [self.lay.flip_dp(part, i + 1) for i, part in enumerate((x, y, d))]
             yield
-            x = self.lay.flip_dp(order.add(x, d), 1)
+            yield
+            total = order.add(own, *moved)
         else:
-            x = self.lay.flip_dp(x, 1)
+            far = self.turn()
+            d = self.lay.flip_dp(d, far)
+            if far == 2:
+                y = self.lay.flip_dp(y, 2)
+                yield
+                x = self.lay.flip_dp(order.add(x, d), 1)
+            else:
+                x = self.lay.flip_dp(x, 1)
+                yield
+                y = self.lay.flip_dp(order.add(y, d), 2)
             yield
-            y = self.lay.flip_dp(order.add(y, d), 2)
-        yield
-        total = order.add(own, x, y)
+            total = order.add(own, x, y)
         yield lax.psum_scatter(
             total, "fsdp", scatter_dimension=0, axis_index_groups=self.groups
         ).astype(F32)
@@ -1913,6 +1989,7 @@
     dcot = pair(dcot_own, swap(dcot_own), 0)
     ecot = pair(enc_cot, swap(enc_cot), 0)
     order.after(x, y, dcot, ecot)
+    order.after(links.gathered[5], *links.first[3], links.second[1])
     dqkv, rel, da_keep, da_send = order.run(
         ngram_attention,
         y,
@@ -1921,24 +1998,28 @@
         w["dec"],
     )
     da_got = swap(da_send)
+    order.after(links.gathered[6], *links.first[4])
     eqkv, ea_keep, ea_send = order.run(enc_attention, x, qkv_bias(eb[0], eb[1]), w["enc"])
     ea_got = swap(ea_send)
+    order.after(*links.first[5])
     p3 = order.run(out_projection, da_keep, da_got, w["dec"])
     p3_got = swap(p3)
     p1 = order.run(out_projection, ea_keep, ea_got, w["enc"])
     p1_got = swap(p1)
-    eunit1, einv1, eh1_low, eg, egp, p2 = order.run(
-        ffn_forward,
+    eunit1, einv1, eh1_low = order.run(
+        norm_forward,
         x,
         False,
         p1,
         p1_got,
         rows_of(eb[2], eb[2], eb[2], eg_rows[0], eb[8]),
-        hidden_of(eb[3:7]),
-        w["enc_up"],
-        w["enc_down"],
+    )
+    order.after(links.second[5], *links.first[6])
+    eg, egp, p2 = order.run(
+        ffn_forward, eh1_low, hidden_of(eb[3:7]), w["enc_up"], w["enc_down"]
     )
     p2_got = swap(p2)
+    order.after(links.second[6])
     dunit1, dinv1, dh1_low, eunit2, einv2, enc_low, cq, ckv, ca_keep, ca_send = order.run(
         cross_forward,
         y,
@@ -1956,39 +2037,37 @@
     ca_got = swap(ca_send)
     p4 = order.run(out_projection, ca_keep, ca_got, w["cross"])
     p4_got = swap(p4)
-    dunit2, dinv2, dh2_low, dg, dgp, p5 = order.run(
-        ffn_forward,
+    dunit2, dinv2, dh2_low = order.run(
+        norm_forward,
         dunit1,
         True,
         p4,
         p4_got,
         rows_of(dg_rows[0], db[9], db[3], dg_rows[1], db[10]),
-        hidden_of(db[4:8]),
-        w["dec_up"],
-        w["dec_down"],
+    )
+    dg, dgp, p5 = order.run(
+        ffn_forward, dh2_low, hidden_of(db[4:8]), w["dec_up"], w["dec_down"]
     )
     p5_got = swap(p5)
 
-    dec_out, gz3, gf, gu, p6, s_gain3, s_shift3, s_gf, s_gu = order.run(
-        ffn_back,
+    up_terms = [("plain", 64 * b, 0, 1, WIDE * b) for b in range(4)]
+    down_terms = [("rows", 0, 0, 1, WIDE * h) for h in range(2)]
+
+    def grads(*args):
+        scatter = links.scatter(order, order.run(grad_chunk, *args))
+        next(scatter)
+        return scatter
+
+    dec_out, gz3, gf, s_gain3, s_shift3, s_gf = order.run(
+        norm_backward,
         True,
         [dcot],
         [dunit2, p5, p5_got],
         rows_of(dg_rows[1], db[10], db[8], dg_rows[2], db[11]),
-        dgp,
-        w["dec_up"],
-        w["dec_down"],
-    )
+    )
+    r_dd = grads([dg, gf], down_terms, 128, D)
+    gu, p6, s_gu = order.run(ffn_back, gf, dgp, w["dec_up"], w["dec_down"])
     p6_got = swap(p6)
-    up_terms = [("plain", 64 * b, 0, 1, WIDE * b) for b in range(4)]
-    down_terms = [("rows", 0, 0, 1, WIDE * h) for h in range(2)]
-
-    def grads(*args):
-        scatter = links.scatter(order, order.run(grad_chunk, *args))
-        next(scatter)
-        return scatter
-
-    r_dd = grads([dg, gf], down_terms, 128, D)
     r_du = grads([dh2_low, gu], up_terms, 256)
     gz2, gx, gca_keep, gca_send, s_gain2, s_shift2, s_gx = order.run(
         branch_back, gz3, p6, p6_got, dunit2, dinv2, dg_rows[1:2], w["cross"]
@@ -2015,22 +2094,16 @@
         branch_back, gz2, p7, p7_got, dunit1, dinv1, dg_rows[0:1], w["dec"]
     )
     gda_got = swap(gda_send)
-    gz2e, gfe, gue, p9, e_gain2, e_shift2, s_gfe, s_gue = order.run(
-        ffn_back,
-        False,
-        [ecot, p7, p7_got],
-        [eunit2, einv2],
-        rows_of(*([eg_rows[1]] * 5)),
-        egp,
-        w["enc_up"],
-        w["enc_down"],
-    )
+    gz2e, gfe, e_gain2, e_shift2, s_gfe = order.run(
+        norm_backward, False, [ecot, p7, p7_got], [eunit2, einv2], rows_of(*([eg_rows[1]] * 5))
+    )
+    gue, p9, s_gue = order.run(ffn_back, gfe, egp, w["enc_up"], w["enc_down"])
     p9_got = swap(p9)
     total_dd = next(r_dd)
     next(r_cross)
-    total_du = next(r_du)
     r_ed = grads([eg, gfe], down_terms, 128, D)
     r_eu = grads([eh1_low, gue], up_terms, 256)
+    total_du = next(r_du)
     gz1e, goe, gea_keep, gea_send, e_gain1, e_shift1, s_goe = order.run(
         branch_back, gz2e, p9, p9_got, eunit1, einv1, eg_rows[0:1], w["enc"]
     )
@@ -2046,12 +2119,14 @@
         enc_attention_back, eqkv, gea_keep, gea_got, gz1e, w["enc"]
     )
     p10_got = swap(p10_send)
+    g_dec_in = order.add(p8, p8_got, dtype=F32)
     r_dec = grads(
         [y, gqkv, da_keep, da_got, go, grel],
         [("plain", 64 * b, 0, 1, WIDE * b) for b in range(3)]
         + [("heads", 192, 2, 4, 0), ("heads", 224, 2, 4, WIDE), ("rel", 256, 0, 5, 0)],
         288,
     )
+    g_source = order.add(p10, p10_got, dtype=F32)
     total_ed = next(r_ed)
     total_eu = next(r_eu)
 
@@ -2159,8 +2234,8 @@
     return (
         pick(enc_low[:LEN], enc_low[LEN:]),
         dec_out.reshape(STREAMS, LEN, D).transpose(1, 0, 2),
-        p10 + p10_got.astype(F32),
-        (p8 + p8_got.astype(F32)).reshape(STREAMS, LEN, D).transpose(1, 0, 2),
+        g_source,
+        g_dec_in.reshape(STREAMS, LEN, D).transpose(1, 0, 2),
         o_enc_in,
         o_enc_out,
         o_enc_up,

time: 820 us -> 815 us (level)
  Pallas kernels: 257 us -> 210 us
  local copies, waits for them, and re-layouts: 51.6 us -> 97.7 us
    pallas_call x24 -> x26, Pallas kernels: 257 us -> 199 us  [run(): pl.pallas_call(body, grid=(grid,), in_specs=[s for a, s in ins], out_spec...]
    unnamed x239 -> x367, local copies, waits for them, and re-layouts: 15 us -> 72.2 us
    ppermute x42, waiting for transfers between devices: 280 us -> 244 us  [flip_dp(): return lax.ppermute(value, 'dp', [(i, i ^ mask) for i in range(self.ndp)])]
    all_gather x7, waiting for transfers between devices: 55.5 us -> 87.1 us  [gather(): own = lax.all_gather(buf, 'fsdp', axis=0, axis_index_groups=self.groups)]
    pallas_call x0 -> x2, Pallas kernels: none -> 11 us  [norm_backward(): pl.pallas_call(body, grid_spec=pltpu.PrefetchScalarGridSpec(num_scalar_pr...]
    select_n x34, other arithmetic: 26 us -> 15.6 us  [pick(): return jnp.where(self.core == 0, first, second)]
  transfers between devices with their start and end apart: 86 -> 86, of which waited for: 34 -> 34; matrix products, arithmetic and copies ran while one was open for 13% -> 12% of each run, Pallas kernels for 25% -> 17%
where the time goes in v4:
time: 815 us; the launch traced here: 805 us
  waiting for transfers between devices  357 us (44%)
  Pallas kernels  210 us (26%)
  local copies, waits for them, and re-layouts  97.7 us (12%)
  other arithmetic  71.2 us (9%)
  starting transfers between devices  51.5 us (6%)
  between operations  18 us (2%)
    ppermute x42, waiting for transfers between devices, flip_dp(): return lax.ppermute(value, 'dp', [(i, i ^ mask) for i in range(self.ndp)])  244 us
    pallas_call x26, Pallas kernels, run(): pl.pallas_call(body, grid=(grid,), in_specs=[s for a, s in ins], out_spec...  199 us
    all_gather x7, waiting for transfers between devices, gather(): own = lax.all_gather(buf, 'fsdp', axis=0, axis_index_groups=self.groups)  87.1 us
    unnamed x367, local copies, waits for them, and re-layouts  72.2 us
    ppermute x42, starting transfers between devices, flip_dp(): return lax.ppermute(value, 'dp', [(i, i ^ mask) for i in range(self.ndp)])  45.3 us
    convert_element_type x14, other arithmetic, add(): sum((v.astype(F32) for v in others), first.astype(F32)).astype(dtype)  32.9 us
  transfers between devices with their start and end apart: 86, of which 34 were waited for; matrix products, arithmetic and copies ran while one was open for 12% of the time, Pallas kernels for 17%

profile of v4, /device:TPU:0, one launch (start us, length us, event | category | flops | bytes accessed | tf_op | source)
XLA Modules:
  0.0 804.7 jit_solution(2678925818831350581)
XLA Ops:
  17.5 22.8 %all-gather.15.cloned.1.call-done = bf16[512,1024]{1,0:T(8,128)(2,1)} async-done(((bf16[128,1024]{1,0:T(8,128)(2,1)}), bf16[512,1024]{1,0:T(8,128)(2,1)}) %all-gather.15.cloned.1.call-update) | async-done | bytes 1048592 | tf_op jit(solution)/shard_map/all_gather | solution.py:1797
  46.5 22.8 %all-gather.19.cloned.1.call-done = bf16[512,1024]{1,0:T(8,128)(2,1)} async-done(((bf16[128,1024]{1,0:T(8,128)(2,1)}), bf16[512,1024]{1,0:T(8,128)(2,1)}) %all-gather.19.cloned.1.call-update) | async-done | bytes 1048592 | tf_op jit(solution)/shard_map/all_gather | solution.py:1797
  77.6 24.9 %all-gather.17.cloned.1.call-done = bf16[1216,512]{1,0:T(8,128)(2,1)} async-done(((bf16[304,512]{1,0:T(8,128)(2,1)}), bf16[1216,512]{1,0:T(8,128)(2,1)}) %all-gather.17.cloned.1.call-update) | async-done | bytes 1245200 | tf_op jit(solution)/shard_map/all_gather | solution.py:1797
  115.0 16.5 %all-gather.21.cloned.1.call-done = bf16[1024,512]{1,0:T(8,128)(2,1)} async-done(((bf16[256,512]{1,0:T(8,128)(2,1)}), bf16[1024,512]{1,0:T(8,128)(2,1)}) %all-gather.21.cloned.1.call-update) | async-done | bytes 1048592 | tf_op jit(solution)/shard_map/all_gather | solution.py:1797
  138.1 20.8 %collective-permute-done.13.refs_7_ = bf16[4,128,1024]{2,1,0:T(8,128)(2,1)} collective-permute-done((bf16[4,128,1024]{2,1,0:T(8,128)(2,1)S(1)}, bf16[4,128,1024]{2,1,0:T(8,128)(2,1)}, u32[]{:S(2)}, u32[]{:S(2)}) %collective-permute-start.13) | collective-permute-done | bytes 1048608 | tf_op jit(solution)/shard_map/ppermute | solution.py:143
  172.5 34.3 %collective-permute-done.14.refs_1_ = bf16[4,256,512]{2,1,0:T(8,128)(2,1)} collective-permute-done((bf16[4,256,512]{2,1,0:T(8,128)(2,1)}, bf16[4,256,512]{2,1,0:T(8,128)(2,1)}, u32[]{:S(2)}, u32[]{:S(2)}) %collective-permute-start.14) | collective-permute-done | bytes 1048608 | tf_op jit(solution)/shard_map/ppermute | solution.py:143
  218.3 17.1 %shard_map.366 = (bf16[768,1536]{1,0:T(8,128)(2,1)S(1)}, f32[768,256]{1,0:T(8,128)S(1)}, bf16[768,256]{1,0:T(8,128)(2,1)S(1)}, bf16[768,256]{1,0:T(8,128)(2,1)}) custom-call(s32[8]{0:T(128)S(1)} %concatenate.330.place, bf16[768,1024]{1,0:T(8,128)(2,1)S(1)} %maximum_select_fusion.y.refs_0_, f32[1,1536]{1,0:T(1,128)S(1)} %broadcast_in_dim.18.bias, ...), custom_call_target="tpu_custom_call" | custom-call | flops 19000000512 | bytes 19000000 | tf_op jit(solution)/shard_map/pallas_call | solution.py:744
  239.8 17.4 %collective-permute-done.19.refs_3_ = bf16[4,256,512]{2,1,0:T(8,128)(2,1)} collective-permute-done((bf16[4,256,512]{2,1,0:T(8,128)(2,1)}, bf16[4,256,512]{2,1,0:T(8,128)(2,1)}, u32[]{:S(2)}, u32[]{:S(2)}) %collective-permute-start.19) | collective-permute-done | bytes 1048608 | tf_op jit(solution)/shard_map/ppermute | solution.py:143
  259.4 8.9 %shard_map.367 = (bf16[256,1536]{1,0:T(8,128)(2,1)S(1)}, bf16[256,256]{1,0:T(8,128)(2,1)S(1)}, bf16[256,256]{1,0:T(8,128)(2,1)S(1)}) custom-call(s32[8]{0:T(128)S(1)} %concatenate.330.place, bf16[256,1024]{1,0:T(8,128)(2,1)S(1)} %copy-done.19, f32[1,1536]{1,0:T(1,128)S(1)} %broadcast_in_dim.19.bias, bf16[4,256,512]{2,1,0:T(8,128)(2,1)S(1)} %bitcast.230, ...), custom_call_target="tpu_custom_call" | custom-call | flops 10000000000 | bytes 10000000 | tf_op jit(solution)/shard_map/pallas_call | solution.py:744
  290.7 26.9 %collective-permute-done.26.refs_1_ = bf16[4,256,512]{2,1,0:T(8,128)(2,1)} collective-permute-done((bf16[4,256,512]{2,1,0:T(8,128)(2,1)}, bf16[4,256,512]{2,1,0:T(8,128)(2,1)}, u32[]{:S(2)}, u32[]{:S(2)}) %collective-permute-start.26) | collective-permute-done | bytes 1048608 | tf_op jit(solution)/shard_map/ppermute | solution.py:143
  335.1 9.8 %collective-permute-done.29.refs_3_ = bf16[4,256,512]{2,1,0:T(8,128)(2,1)S(1)} collective-permute-done((bf16[4,256,512]{2,1,0:T(8,128)(2,1)}, bf16[4,256,512]{2,1,0:T(8,128)(2,1)S(1)}, u32[]{:S(2)}, u32[]{:S(2)}) %collective-permute-start.29) | collective-permute-done | bytes 1048608 | tf_op jit(solution)/shard_map/ppermute | solution.py:143
  344.9 11.3 %shard_map.372 = (f32[768,1024]{1,0:T(8,128)}, f32[768,128]{1,0:T(8,128)S(1)}, bf16[768,1024]{1,0:T(8,128)(2,1)S(1)}, f32[256,1024]{1,0:T(8,128)S(1)}, f32[256,1...) custom-call(s32[8]{0:T(128)S(1)} %concatenate.330.place, ...), custom_call_target="tpu_custom_call" | custom-call | flops 15000000512 | bytes 15000000 | tf_op jit(solution)/shard_map/pallas_call | solution.py:744
  373.6 19.0 %shard_map.375 = (bf16[768,2048]{1,0:T(8,128)(2,1)S(1)}, bf16[768,2048]{1,0:T(8,128)(2,1)S(1)}, bf16[768,1024]{1,0:T(8,128)(2,1)}) custom-call(s32[8]{0:T(128)S(1)} %concatenate.330.place, bf16[768,1024]{1,0:T(8,128)(2,1)S(1)} %get-tuple-element.230.low.refs_0_, f32[1,2048]{1,0:T(1,128)S(1)} %fusion.28.hb, bf16[4,256,512]{2,1,0:T(8,128)(2,1)} %bitcast.22.refs_0_, ...), custom_call_target="tpu_custom_call" | custom-call | flops 14000000000 | bytes 14000000 | tf_op jit(solution)/shard_map/pallas_call | solution.py:744
  419.4 10.6 %shard_map.378 = (bf16[768,2048]{1,0:T(8,128)(2,1)S(1)}, bf16[768,1024]{1,0:T(8,128)(2,1)S(1)}, f32[1,2048]{1,0:T(1,128)S(1)}) custom-call(s32[8]{0:T(128)S(1)} %concatenate.330.place, bf16[768,1024]{1,0:T(8,128)(2,1)S(1)} %copy-done.83, bf16[768,2048]{1,0:T(8,128)(2,1)S(1)} %copy-done.121, bf16[4,256,512]{2,1,0:T(8,128)(2,1)} %bitcast.22.refs_0_, ...), custom_call_target="tpu_custom_call" | custom-call | flops 14000000000 | bytes 14000000 | tf_op jit(solution)/shard_map/pallas_call | solution.py:744
  447.3 8.5 %collective-permute-done.36 = bf16[4,128,1024]{2,1,0:T(8,128)(2,1)S(1)} collective-permute-done((bf16[4,128,1024]{2,1,0:T(8,128)(2,1)S(1)}, bf16[4,128,1024]{2,1,0:T(8,128)(2,1)S(1)}, u32[]{:S(2)}, u32[]{:S(2)}) %collective-permute-start.36) | collective-permute-done | bytes 1048608 | tf_op jit(solution)/shard_map/ppermute | solution.py:143
  465.8 12.9 %shard_map.381 = (bf16[768,512]{1,0:T(8,128)(2,1)S(1)}, bf16[256,1024]{1,0:T(8,128)(2,1)S(1)}, bf16[1024,1024]{1,0:T(8,128)(2,1)}, f32[1,512]{1,0:T(1,128)S(1)}, f32[1,1024]{1,0:T(1,128)S(1)}) custom-call(s32[8]{0:T(128)S(1)} %concatenate.330.place, bf16[768,512]{1,0:T(8,128)(2,1)S(1)} %copy-done.145, bf16[256,1024]{1,0:T(8,128)(2,1)S(1)} %copy-done.147, ...), custom_call_target="tpu_custom_call" | custom-call | flops 14000000000 | bytes 14000000 | tf_op jit(solution)/shard_map/pallas_call | solution.py:744
  532.9 18.4 %collective-permute-done.42 = bf16[4,256,512]{2,1,0:T(8,128)(2,1)} collective-permute-done((bf16[4,256,512]{2,1,0:T(8,128)(2,1)}, bf16[4,256,512]{2,1,0:T(8,128)(2,1)}, u32[]{:S(2)}, u32[]{:S(2)}) %collective-permute-start.42) | collective-permute-done | bytes 1048608 | tf_op jit(solution)/shard_map/ppermute | solution.py:143
  584.8 24.8 %shard_map.389 = (bf16[768,1536]{1,0:T(8,128)(2,1)S(1)}, bf16[768,256]{1,0:T(8,128)(2,1)S(1)}, f32[384,1024]{1,0:T(8,128)S(1)}, bf16[384,1024]{1,0:T(8,128)(2,1)...) custom-call(s32[8]{0:T(128)S(1)} %concatenate.330.place, bf16[768,1536]{1,0:T(8,128)(2,1)S(1)} %copy-done.137, ...), custom_call_target="tpu_custom_call" | custom-call | flops 28999999488 | bytes 29000000 | tf_op jit(solution)/shard_map/pallas_call | solution.py:744
  609.7 10.3 %collective-permute-done.47 = bf16[4,128,1024]{2,1,0:T(8,128)(2,1)} collective-permute-done((bf16[4,128,1024]{2,1,0:T(8,128)(2,1)}, bf16[4,128,1024]{2,1,0:T(8,128)(2,1)}, u32[]{:S(2)}, u32[]{:S(2)}) %collective-permute-start.47) | collective-permute-done | bytes 1048608 | tf_op jit(solution)/shard_map/ppermute | solution.py:143
  635.7 11.0 %shard_map.390 = (bf16[256,1536]{1,0:T(8,128)(2,1)S(1)}, f32[128,1024]{1,0:T(8,128)S(1)}, bf16[128,1024]{1,0:T(8,128)(2,1)S(1)}, f32[1,1536]{1,0:T(1,128)S(1)}) custom-call(s32[8]{0:T(128)S(1)} %concatenate.330.place, bf16[256,1536]{1,0:T(8,128)(2,1)S(1)} %copy-done.135, bf16[256,256]{1,0:T(8,128)(2,1)S(1)} %copy-done.127, ...), custom_call_target="tpu_custom_call" | custom-call | flops 12999999488 | bytes 13000000 | tf_op jit(solution)/shard_map/pallas_call | solution.py:744
  682.4 20.7 %collective-permute-done.58 = bf16[4,288,512]{2,1,0:T(8,128)(2,1)} collective-permute-done((bf16[4,288,512]{2,1,0:T(8,128)(2,1)}, bf16[4,288,512]{2,1,0:T(8,128)(2,1)}, u32[]{:S(2)}, u32[]{:S(2)}) %collective-permute-start.58) | collective-permute-done | bytes 1179680 | tf_op jit(solution)/shard_map/ppermute | solution.py:143
  710.6 12.7 %collective-permute-done.60 = bf16[4,288,512]{2,1,0:T(8,128)(2,1)} collective-permute-done((bf16[4,288,512]{2,1,0:T(8,128)(2,1)}, bf16[4,288,512]{2,1,0:T(8,128)(2,1)}, u32[]{:S(2)}, u32[]{:S(2)}) %collective-permute-start.60) | collective-permute-done | bytes 1179680 | tf_op jit(solution)/shard_map/ppermute | solution.py:143
  743.8 16.8 %collective-permute-done.63 = bf16[4,272,512]{2,1,0:T(8,128)(2,1)} collective-permute-done((bf16[4,272,512]{2,1,0:T(8,128)(2,1)S(1)}, bf16[4,272,512]{2,1,0:T(8,128)(2,1)}, u32[]{:S(2)}, u32[]{:S(2)}) %collective-permute-start.63) | collective-permute-done | bytes 1114144 | tf_op jit(solution)/shard_map/ppermute | solution.py:143
  778.6 12.8 %reduce-scatter.8.cloned.1.call-done = bf16[1,272,512]{2,1,0:T(8,128)(2,1)} async-done(((bf16[4,272,512]{2,1,0:T(8,128)(2,1)}), bf16[1,272,512]{2,1,0:T(8,128)(2,1)}) %reduce-scatter.8.cloned.1.call-update) | async-done | bytes 278544 | tf_op jit(solution)/shard_map/reduce_scatter | solution.py:1843
  (770 shorter events, 374.5 us)
Async XLA Ops:
  7.9 61.4 %all-gather.19.cloned.1.call-start = ((), (), s32[]{:S(2)}) async-start(), calls=%async_computation.16 | async-start | bytes 1310720 | tf_op jit(solution)/shard_map/all_gather | solution.py:1797
  15.5 87.1 %all-gather.17.cloned.1.call-start = ((), (), s32[]{:S(2)}) async-start(), calls=%async_computation.15 | async-start | bytes 1556480 | tf_op jit(solution)/shard_map/all_gather | solution.py:1797
  40.3 91.3 %all-gather.21.cloned.1.call-start = ((), (), s32[]{:S(2)}) async-start(), calls=%async_computation.17 | async-start | bytes 1310720 | tf_op jit(solution)/shard_map/all_gather | solution.py:1797
  69.3 103.1 %all-gather.25.cloned.1.call-start = ((), (), s32[]{:S(2)}) async-start(), calls=%async_computation.19 | async-start | bytes 1310720 | tf_op jit(solution)/shard_map/all_gather | solution.py:1797
  102.6 113.1 %all-gather.23.cloned.1.call-start = ((), (), s32[]{:S(2)}) async-start(), calls=%async_computation.18 | async-start | bytes 1310720 | tf_op jit(solution)/shard_map/all_gather | solution.py:1797
  102.6 61.9 %collective-permute-start.10 = (bf16[384,1024]{1,0:T(8,128)(2,1)S(1)}, bf16[384,1024]{1,0:T(8,128)(2,1)}, u32[]{:S(2)}, u32[]{:S(2)}) collective-permute-start(bf16[384,1024]{1,0:T(8,128)(2,1)S(1)} %bitcast.252), channel_id=1, source_target_pairs={{0,1},{1,0},{2,3},{3,2},{4,5},{5,4},{6,7},{7,6},{8,9},{9,8},{10,11... | collective-permute-start | bytes 2359304 | tf_op jit(solution)/shard_map/ppermute | solution.py:135
  102.7 56.7 %collective-permute-start.9 = (bf16[128,1024]{1,0:T(8,128)(2,1)}, bf16[128,1024]{1,0:T(8,128)(2,1)}, u32[]{:S(2)}, u32[]{:S(2)}) collective-permute-start(bf16[128,1024]{1,0:T(8,128)(2,1)} %param.22), channel_id=1, source_target_pairs={{0,1},{1,0},{2,3},{3,2},{4,5},{5,4},{6,7},{7,6},{8,9},{9,8},{10,11... | collective-permute-start | bytes 786440 | tf_op jit(solution)/shard_map/ppermute | solution.py:135
  131.6 108.2 %all-gather.27.cloned.1.call-start = ((), (), s32[]{:S(2)}) async-start(), calls=%async_computation.20 | async-start | bytes 1310720 | tf_op jit(solution)/shard_map/all_gather | solution.py:1797
  136.3 74.0 %collective-permute-start.8 = (bf16[4,304,512]{2,1,0:T(8,128)(2,1)}, bf16[4,304,512]{2,1,0:T(8,128)(2,1)}, u32[]{:S(2)}, u32[]{:S(2)}) collective-permute-start(bf16[4,304,512]{2,1,0:T(8,128)(2,1)} %collective-permute-done.7.refs_2_.refs_6_), channel_id=1, source_target_pairs={{0,8},{8,0},{16,24},{24,16},{1,9},{9,1},{17,25},{25,17},{2,10},{10... | collective-permute-start | bytes 3735560 | tf_op jit(solution)/shard_map/ppermute | solution.py:143
  172.5 559.7 %reduce-scatter.18.cloned.1.call-start = ((), (), s32[]{:S(2)}) async-start(), calls=%async_computation.12 | async-start | bytes 1310720 | tf_op jit(solution)/shard_map/reduce_scatter | solution.py:1843
  269.3 55.3 %collective-permute-start.28 = (bf16[4,256,512]{2,1,0:T(8,128)(2,1)}, bf16[4,256,512]{2,1,0:T(8,128)(2,1)}, u32[]{:S(2)}, u32[]{:S(2)}) collective-permute-start(bf16[4,256,512]{2,1,0:T(8,128)(2,1)} %collective-permute-done.18.refs_2_), channel_id=1, source_target_pairs={{0,8},{8,0},{16,24},{24,16},{1,9},{9,1},{17,25},{25,17},{2,10},{10... | collective-permute-start | bytes 3145736 | tf_op jit(solution)/shard_map/ppermute | solution.py:143
  287.0 57.9 %collective-permute-start.30 = (bf16[768,1024]{1,0:T(8,128)(2,1)}, bf16[768,1024]{1,0:T(8,128)(2,1)S(1)}, u32[]{:S(2)}, u32[]{:S(2)}) collective-permute-start(bf16[768,1024]{1,0:T(8,128)(2,1)} %copy-done.25), channel_id=1, source_target_pairs={{0,1},{1,0},{2,3},{3,2},{4,5},{5,4},{6,7},{7,6},{8,9},{9,8},{10,11... | collective-permute-start | bytes 4718600 | tf_op jit(solution)/shard_map/ppermute | solution.py:135
  482.0 84.2 %collective-permute-start.43 = (bf16[4,256,512]{2,1,0:T(8,128)(2,1)}, bf16[4,256,512]{2,1,0:T(8,128)(2,1)}, u32[]{:S(2)}, u32[]{:S(2)}) collective-permute-start(bf16[4,256,512]{2,1,0:T(8,128)(2,1)} %get-tuple-element.287), channel_id=1, source_target_pairs={{0,8},{8,0},{16,24},{24,16},{1,9},{9,1},{17,25},{25,17},{2,10},{10... | collective-permute-start | bytes 3145736 | tf_op jit(solution)/shard_map/ppermute | solution.py:143
  484.0 82.2 %collective-permute-start.44 = (bf16[4,256,512]{2,1,0:T(8,128)(2,1)}, bf16[4,256,512]{2,1,0:T(8,128)(2,1)}, u32[]{:S(2)}, u32[]{:S(2)}) collective-permute-start(bf16[4,256,512]{2,1,0:T(8,128)(2,1)} %add_convert_fusion.12), channel_id=1, source_target_pairs={{0,16},{8,24},{16,0},{24,8},{1,17},{9,25},{17,1},{25,9},{2,18},{10... | collective-permute-start | bytes 3145736 | tf_op jit(solution)/shard_map/ppermute | solution.py:143
  499.0 52.4 %collective-permute-start.42 = (bf16[4,256,512]{2,1,0:T(8,128)(2,1)}, bf16[4,256,512]{2,1,0:T(8,128)(2,1)}, u32[]{:S(2)}, u32[]{:S(2)}) collective-permute-start(bf16[4,256,512]{2,1,0:T(8,128)(2,1)} %get-tuple-element.281), channel_id=1, source_target_pairs={{0,16},{8,24},{16,0},{24,8},{1,17},{9,25},{17,1},{25,9},{2,18},{10... | collective-permute-start | bytes 3145736 | tf_op jit(solution)/shard_map/ppermute | solution.py:143
  569.3 167.4 %reduce-scatter.20.cloned.1.call-start = ((), (), s32[]{:S(2)}) async-start(), calls=%async_computation.13 | async-start | bytes 1310720 | tf_op jit(solution)/shard_map/reduce_scatter | solution.py:1843
  569.5 55.1 %collective-permute-start.50 = (bf16[4,256,512]{2,1,0:T(8,128)(2,1)}, bf16[4,256,512]{2,1,0:T(8,128)(2,1)}, u32[]{:S(2)}, u32[]{:S(2)}) collective-permute-start(bf16[4,256,512]{2,1,0:T(8,128)(2,1)} %copy-done.61), channel_id=1, source_target_pairs={{0,16},{8,24},{16,0},{24,8},{1,17},{9,25},{17,1},{25,9},{2,18},{10... | collective-permute-start | bytes 3145736 | tf_op jit(solution)/shard_map/ppermute | solution.py:143
  571.1 54.1 %collective-permute-start.49 = (bf16[4,256,512]{2,1,0:T(8,128)(2,1)}, bf16[4,256,512]{2,1,0:T(8,128)(2,1)}, u32[]{:S(2)}, u32[]{:S(2)}) collective-permute-start(bf16[4,256,512]{2,1,0:T(8,128)(2,1)} %add_convert_fusion.10), channel_id=1, source_target_pairs={{0,8},{8,0},{16,24},{24,16},{1,9},{9,1},{17,25},{25,17},{2,10},{10... | collective-permute-start | bytes 3145736 | tf_op jit(solution)/shard_map/ppermute | solution.py:143
  573.9 166.9 %reduce-scatter.16.cloned.1.call-start = ((), (), s32[]{:S(2)}) async-start(), calls=%async_computation.11 | async-start | bytes 1310720 | tf_op jit(solution)/shard_map/reduce_scatter | solution.py:1843
  584.0 74.6 %collective-permute-start.54 = (bf16[4,128,1024]{2,1,0:T(8,128)(2,1)}, bf16[4,128,1024]{2,1,0:T(8,128)(2,1)}, u32[]{:S(2)}, u32[]{:S(2)}) collective-permute-start(bf16[4,128,1024]{2,1,0:T(8,128)(2,1)} %get-tuple-element.320), channel_id=1, source_target_pairs={{0,8},{8,0},{16,24},{24,16},{1,9},{9,1},{17,25},{25,17},{2,10},{10... | collective-permute-start | bytes 3145736 | tf_op jit(solution)/shard_map/ppermute | solution.py:143
  629.6 136.6 %reduce-scatter.10.cloned.1.call-start = ((), (), s32[]{:S(2)}) async-start(), calls=%async_computation.8 | async-start | bytes 1310720 | tf_op jit(solution)/shard_map/reduce_scatter | solution.py:1843
  670.9 98.1 %reduce-scatter.12.cloned.1.call-start = ((), (), s32[]{:S(2)}) async-start(), calls=%async_computation.9 | async-start | bytes 1310720 | tf_op jit(solution)/shard_map/reduce_scatter | solution.py:1843
  676.3 96.9 %reduce-scatter.14.cloned.1.call-start = ((), (), s32[]{:S(2)}) async-start(), calls=%async_computation.10 | async-start | bytes 1474560 | tf_op jit(solution)/shard_map/reduce_scatter | solution.py:1843
  731.8 59.6 %reduce-scatter.8.cloned.1.call-start = ((), (), s32[]{:S(2)}) async-start(), calls=%async_computation.7 | async-start | bytes 1392640 | tf_op jit(solution)/shard_map/reduce_scatter | solution.py:1843
  (229 other events, 2954.2 us)
Sparse Core Ops, SparseCore 0:
  9.6 30.6 all-gather.14
  41.8 27.4 all-gather.18
  71.4 31.0 all-gather.16
  104.5 26.9 all-gather.20
  133.5 27.4 all-gather.24
  163.0 27.4 all-gather.22
  192.6 27.4 all-gather.26
  569.4 26.2 reduce-scatter.17
  598.1 25.7 reduce-scatter.19
  629.7 25.2 reduce-scatter.15
  671.1 25.3 reduce-scatter.9
  698.6 25.7 reduce-scatter.11
  731.9 27.3 reduce-scatter.13
  764.2 27.2 reduce-scatter.7

commit v5 on v4

--- a/solution.py
+++ b/solution.py
@@ -733,7 +733,7 @@
     )
 
 
-BUDGET = 36 * 1024 * 1024
+BUDGET = 26 * 1024 * 1024
 PIECES = 4
 HBM_RATE = 1.0e6
 FLOP_RATE = 1.0e9
@@ -996,7 +996,7 @@
     rows = low.shape[0]
     hidden = hidden_bias.shape[1]
     ups = hidden // WIDE
-    tile = 256
+    tile = 128
 
     def body(place, low, hb, *refs):
         wu, wd = refs[:PIECES], refs[PIECES : 2 * PIECES]
@@ -1008,15 +1008,13 @@
             assemble(wu, scr_u, place)
             w = matrix_of(scr_u)
 
-            def step(r):
-                here = pl.ds(r, tile)
+            for r in range(0, rows, tile):
+                here = slice(r, r + tile)
                 a, b = gelu_pair(dot(low[here], w) + hb[...])
                 a = a.astype(BF)
                 g[here] = a
                 acts[here, pl.ds(t * WIDE, WIDE)] = a
                 gp[here] = b.astype(BF)
-
-            each_tile(rows, tile, step)
 
         @pl.when(t >= ups)
         def _():
@@ -1778,10 +1776,11 @@
 
 class Links:
 
-    def __init__(self, lay):
+    def __init__(self, lay, before):
         self.lay = lay
         self.gathered = []
         self.first = []
+        self.before = before
         self.second = []
         self.far = 2
         self.groups = [list(range(core, lay.nf, 2)) for core in range(2)]
@@ -1796,9 +1795,7 @@
             buf = tie(buf, self.gathered[-2])
         own = lax.all_gather(buf, "fsdp", axis=0, axis_index_groups=self.groups)
         self.gathered.append(own)
-        ready = own
-        if self.first:
-            ready = tie(ready, *self.first[-1])
+        ready = tie(own, *(self.first[-1] if self.first else self.before))
         if len(self.second) >= 3:
             ready = tie(ready, self.second[-3])
         x, y = self.lay.flip_dp(ready, 1), self.lay.flip_dp(ready, 2)
@@ -1878,9 +1875,6 @@
     core = lay.core
     dec_rows = STREAMS * LEN
 
-    links = Links(lay)
-    w = {"dec_down": links.gather(dec_ffn_out), "enc_down": links.gather(enc_ffn_out)}
-
     def halves(matrix, groups, width):
         parts = matrix.reshape(r, groups, 2, width)
         return (
@@ -1917,6 +1911,11 @@
     source_got = swap(source)
     dec_own = dec_in.transpose(1, 0, 2).reshape(dec_rows, D)
     dec_got = swap(dec_own)
+    dcot_own = dec_cot.transpose(1, 0, 2).reshape(dec_rows, D)
+    dcot_got = swap(dcot_own)
+    ecot_got = swap(enc_cot)
+    links = Links(lay, (theirs_got, vec_got, source_got, dec_got, dcot_got, ecot_got))
+    w = {"dec_down": links.gather(dec_ffn_out), "enc_down": links.gather(enc_ffn_out)}
 
     def column_blocks(start, count):
         return [
@@ -1985,9 +1984,8 @@
 
     x = pair(source, source_got, 0)
     y = pair(dec_own, dec_got, 0)
-    dcot_own = dec_cot.transpose(1, 0, 2).reshape(dec_rows, D)
-    dcot = pair(dcot_own, swap(dcot_own), 0)
-    ecot = pair(enc_cot, swap(enc_cot), 0)
+    dcot = pair(dcot_own, dcot_got, 0)
+    ecot = pair(enc_cot, ecot_got, 0)
     order.after(x, y, dcot, ecot)
     order.after(links.gathered[5], *links.first[3], links.second[1])
     dqkv, rel, da_keep, da_send = order.run(

time: 815 us -> 806 us (0.989)
    unnamed x367 -> x381, local copies, waits for them, and re-layouts: 72.2 us -> 71.9 us
  transfers between devices with their start and end apart: 86 -> 86, of which waited for: 34 -> 35; matrix products, arithmetic and copies ran while one was open for 12% -> 12% of each run, Pallas kernels for 17% -> 17%
where the time goes in v5:
time: 806 us; the launch traced here: 796 us
  waiting for transfers between devices  354 us (44%)
  Pallas kernels  205 us (25%)
  local copies, waits for them, and re-layouts  96.9 us (12%)
  other arithmetic  71.9 us (9%)
  starting transfers between devices  50.4 us (6%)
  between operations  18 us (2%)
    ppermute x42, waiting for transfers between devices, flip_dp(): return lax.ppermute(value, 'dp', [(i, i ^ mask) for i in range(self.ndp)])  246 us
    pallas_call x26, Pallas kernels, run(): pl.pallas_call(body, grid=(grid,), in_specs=[s for a, s in ins], out_spec...  194 us
    all_gather x7, waiting for transfers between devices, gather(): own = lax.all_gather(buf, 'fsdp', axis=0, axis_index_groups=self.groups)  80.6 us
    unnamed x381, local copies, waits for them, and re-layouts  71.9 us
    ppermute x42, starting transfers between devices, flip_dp(): return lax.ppermute(value, 'dp', [(i, i ^ mask) for i in range(self.ndp)])  44 us
    convert_element_type x14, other arithmetic, add(): sum((v.astype(F32) for v in others), first.astype(F32)).astype(dtype)  31.6 us
    select_n x34, other arithmetic, pick(): return jnp.where(self.core == 0, first, second)  18.2 us
  transfers between devices with their start and end apart: 86, of which 35 were waited for; matrix products, arithmetic and copies ran while one was open for 12% of the time, Pallas kernels for 17%

profile of v5, /device:TPU:0, one launch (start us, length us, event | category | flops | bytes accessed | tf_op | source)
XLA Modules:
  0.0 796.4 jit_solution(13447473346162969172)
XLA Ops:
  20.6 19.6 %all-gather.15.cloned.1.call-done = bf16[512,1024]{1,0:T(8,128)(2,1)} async-done(((bf16[128,1024]{1,0:T(8,128)(2,1)}), bf16[512,1024]{1,0:T(8,128)(2,1)}) %all-gather.15.cloned.1.call-update) | async-done | bytes 1048592 | tf_op jit(solution)/shard_map/all_gather | solution.py:1796
  51.0 18.3 %all-gather.19.cloned.1.call-done = bf16[512,1024]{1,0:T(8,128)(2,1)} async-done(((bf16[128,1024]{1,0:T(8,128)(2,1)}), bf16[512,1024]{1,0:T(8,128)(2,1)}) %all-gather.19.cloned.1.call-update) | async-done | bytes 1048592 | tf_op jit(solution)/shard_map/all_gather | solution.py:1796
  80.1 22.5 %all-gather.17.cloned.1.call-done = bf16[1216,512]{1,0:T(8,128)(2,1)} async-done(((bf16[304,512]{1,0:T(8,128)(2,1)}), bf16[1216,512]{1,0:T(8,128)(2,1)}) %all-gather.17.cloned.1.call-update) | async-done | bytes 1245200 | tf_op jit(solution)/shard_map/all_gather | solution.py:1796
  111.4 20.1 %all-gather.21.cloned.1.call-done = bf16[1024,512]{1,0:T(8,128)(2,1)} async-done(((bf16[256,512]{1,0:T(8,128)(2,1)}), bf16[1024,512]{1,0:T(8,128)(2,1)}) %all-gather.21.cloned.1.call-update) | async-done | bytes 1048592 | tf_op jit(solution)/shard_map/all_gather | solution.py:1796
  135.9 22.5 %collective-permute-done.13.refs_7_ = bf16[4,128,1024]{2,1,0:T(8,128)(2,1)} collective-permute-done((bf16[4,128,1024]{2,1,0:T(8,128)(2,1)S(1)}, bf16[4,128,1024]{2,1,0:T(8,128)(2,1)}, u32[]{:S(2)}, u32[]{:S(2)}) %collective-permute-start.13) | collective-permute-done | bytes 1048608 | tf_op jit(solution)/shard_map/ppermute | solution.py:143
  173.1 32.3 %collective-permute-done.14.refs_1_ = bf16[4,256,512]{2,1,0:T(8,128)(2,1)} collective-permute-done((bf16[4,256,512]{2,1,0:T(8,128)(2,1)}, bf16[4,256,512]{2,1,0:T(8,128)(2,1)}, u32[]{:S(2)}, u32[]{:S(2)}) %collective-permute-start.14) | collective-permute-done | bytes 1048608 | tf_op jit(solution)/shard_map/ppermute | solution.py:143
  216.9 17.1 %shard_map.366 = (bf16[768,1536]{1,0:T(8,128)(2,1)S(1)}, f32[768,256]{1,0:T(8,128)S(1)}, bf16[768,256]{1,0:T(8,128)(2,1)S(1)}, bf16[768,256]{1,0:T(8,128)(2,1)}) custom-call(s32[8]{0:T(128)S(1)} %concatenate.330.place, bf16[768,1024]{1,0:T(8,128)(2,1)S(1)} %maximum_select_fusion.y.refs_0_, f32[1,1536]{1,0:T(1,128)S(1)} %broadcast_in_dim.18.bias, ...), custom_call_target="tpu_custom_call" | custom-call | flops 19000000512 | bytes 19000000 | tf_op jit(solution)/shard_map/pallas_call | solution.py:744
  238.3 17.4 %collective-permute-done.19.refs_3_ = bf16[4,256,512]{2,1,0:T(8,128)(2,1)} collective-permute-done((bf16[4,256,512]{2,1,0:T(8,128)(2,1)}, bf16[4,256,512]{2,1,0:T(8,128)(2,1)}, u32[]{:S(2)}, u32[]{:S(2)}) %collective-permute-start.19) | collective-permute-done | bytes 1048608 | tf_op jit(solution)/shard_map/ppermute | solution.py:143
  258.0 8.9 %shard_map.367 = (bf16[256,1536]{1,0:T(8,128)(2,1)S(1)}, bf16[256,256]{1,0:T(8,128)(2,1)S(1)}, bf16[256,256]{1,0:T(8,128)(2,1)S(1)}) custom-call(s32[8]{0:T(128)S(1)} %concatenate.330.place, bf16[256,1024]{1,0:T(8,128)(2,1)S(1)} %copy-done.19, f32[1,1536]{1,0:T(1,128)S(1)} %broadcast_in_dim.19.bias, bf16[4,256,512]{2,1,0:T(8,128)(2,1)S(1)} %bitcast.230, ...), custom_call_target="tpu_custom_call" | custom-call | flops 10000000000 | bytes 10000000 | tf_op jit(solution)/shard_map/pallas_call | solution.py:744
  288.4 27.8 %collective-permute-done.26.refs_1_ = bf16[4,256,512]{2,1,0:T(8,128)(2,1)} collective-permute-done((bf16[4,256,512]{2,1,0:T(8,128)(2,1)}, bf16[4,256,512]{2,1,0:T(8,128)(2,1)}, u32[]{:S(2)}, u32[]{:S(2)}) %collective-permute-start.26) | collective-permute-done | bytes 1048608 | tf_op jit(solution)/shard_map/ppermute | solution.py:143
  331.7 9.5 %collective-permute-done.29.refs_3_ = bf16[4,256,512]{2,1,0:T(8,128)(2,1)S(1)} collective-permute-done((bf16[4,256,512]{2,1,0:T(8,128)(2,1)}, bf16[4,256,512]{2,1,0:T(8,128)(2,1)S(1)}, u32[]{:S(2)}, u32[]{:S(2)}) %collective-permute-start.29) | collective-permute-done | bytes 1048608 | tf_op jit(solution)/shard_map/ppermute | solution.py:143
  341.3 9.6 %shard_map.372 = (f32[768,1024]{1,0:T(8,128)S(1)}, f32[768,128]{1,0:T(8,128)S(1)}, bf16[768,1024]{1,0:T(8,128)(2,1)S(1)}, f32[256,1024]{1,0:T(8,128)S(1)}, f32[2...) custom-call(s32[8]{0:T(128)S(1)} %concatenate.330.place, ...), custom_call_target="tpu_custom_call" | custom-call | flops 15000000512 | bytes 15000000 | tf_op jit(solution)/shard_map/pallas_call | solution.py:744
  369.4 17.0 %shard_map.375 = (bf16[768,2048]{1,0:T(8,128)(2,1)S(1)}, bf16[768,2048]{1,0:T(8,128)(2,1)S(1)}, bf16[768,1024]{1,0:T(8,128)(2,1)}) custom-call(s32[8]{0:T(128)S(1)} %concatenate.330.place, bf16[768,1024]{1,0:T(8,128)(2,1)S(1)} %get-tuple-element.232.low.refs_0_, f32[1,2048]{1,0:T(1,128)S(1)} %fusion.28.hb, bf16[4,256,512]{2,1,0:T(8,128)(2,1)} %bitcast.22.refs_0_, ...), custom_call_target="tpu_custom_call" | custom-call | flops 14000000000 | bytes 14000000 | tf_op jit(solution)/shard_map/pallas_call | solution.py:744
  409.9 10.8 %shard_map.378 = (bf16[768,2048]{1,0:T(8,128)(2,1)S(1)}, bf16[768,1024]{1,0:T(8,128)(2,1)S(1)}, f32[1,2048]{1,0:T(1,128)S(1)}) custom-call(s32[8]{0:T(128)S(1)} %concatenate.330.place, bf16[768,1024]{1,0:T(8,128)(2,1)S(1)} %get-tuple-element.238.refs_1_.gf, bf16[768,2048]{1,0:T(8,128)(2,1)S(1)} %copy-done.122, bf16[4,256,512]{2,1,0:T(8,128)(2,1)} %bitcast.22.refs_0_, ...), custom_call_target="tpu_custom_call" | custom-call | flops 14000000000 | bytes 14000000 | tf_op jit(solution)/shard_map/pallas_call | solution.py:744
  434.9 11.4 %collective-permute-done.36 = bf16[4,128,1024]{2,1,0:T(8,128)(2,1)S(1)} collective-permute-done((bf16[4,128,1024]{2,1,0:T(8,128)(2,1)S(1)}, bf16[4,128,1024]{2,1,0:T(8,128)(2,1)S(1)}, u32[]{:S(2)}, u32[]{:S(2)}) %collective-permute-start.36) | collective-permute-done | bytes 1048608 | tf_op jit(solution)/shard_map/ppermute | solution.py:143
  454.9 12.9 %shard_map.381 = (bf16[768,512]{1,0:T(8,128)(2,1)S(1)}, bf16[256,1024]{1,0:T(8,128)(2,1)S(1)}, bf16[1024,1024]{1,0:T(8,128)(2,1)}, f32[1,512]{1,0:T(1,128)S(1)}, f32[1,1024]{1,0:T(1,128)S(1)}) custom-call(s32[8]{0:T(128)S(1)} %concatenate.330.place, bf16[768,512]{1,0:T(8,128)(2,1)S(1)} %copy-done.146, bf16[256,1024]{1,0:T(8,128)(2,1)S(1)} %copy-done.148, ...), custom_call_target="tpu_custom_call" | custom-call | flops 14000000000 | bytes 14000000 | tf_op jit(solution)/shard_map/pallas_call | solution.py:744
  520.7 19.8 %collective-permute-done.42 = bf16[4,256,512]{2,1,0:T(8,128)(2,1)} collective-permute-done((bf16[4,256,512]{2,1,0:T(8,128)(2,1)}, bf16[4,256,512]{2,1,0:T(8,128)(2,1)}, u32[]{:S(2)}, u32[]{:S(2)}) %collective-permute-start.42) | collective-permute-done | bytes 1048608 | tf_op jit(solution)/shard_map/ppermute | solution.py:143
  573.4 24.8 %shard_map.389 = (bf16[768,1536]{1,0:T(8,128)(2,1)S(1)}, bf16[768,256]{1,0:T(8,128)(2,1)S(1)}, f32[384,1024]{1,0:T(8,128)S(1)}, bf16[384,1024]{1,0:T(8,128)(2,1)...) custom-call(s32[8]{0:T(128)S(1)} %concatenate.330.place, bf16[768,1536]{1,0:T(8,128)(2,1)S(1)} %copy-done.138, ...), custom_call_target="tpu_custom_call" | custom-call | flops 28999999488 | bytes 29000000 | tf_op jit(solution)/shard_map/pallas_call | solution.py:744
  598.3 10.6 %collective-permute-done.47 = bf16[4,128,1024]{2,1,0:T(8,128)(2,1)} collective-permute-done((bf16[4,128,1024]{2,1,0:T(8,128)(2,1)}, bf16[4,128,1024]{2,1,0:T(8,128)(2,1)}, u32[]{:S(2)}, u32[]{:S(2)}) %collective-permute-start.47) | collective-permute-done | bytes 1048608 | tf_op jit(solution)/shard_map/ppermute | solution.py:143
  624.1 11.0 %shard_map.390 = (bf16[256,1536]{1,0:T(8,128)(2,1)S(1)}, f32[128,1024]{1,0:T(8,128)S(1)}, bf16[128,1024]{1,0:T(8,128)(2,1)S(1)}, f32[1,1536]{1,0:T(1,128)S(1)}) custom-call(s32[8]{0:T(128)S(1)} %concatenate.330.place, bf16[256,1536]{1,0:T(8,128)(2,1)S(1)} %copy-done.136, bf16[256,256]{1,0:T(8,128)(2,1)S(1)} %copy-done.128, ...), custom_call_target="tpu_custom_call" | custom-call | flops 12999999488 | bytes 13000000 | tf_op jit(solution)/shard_map/pallas_call | solution.py:744
  671.2 20.8 %collective-permute-done.58 = bf16[4,288,512]{2,1,0:T(8,128)(2,1)} collective-permute-done((bf16[4,288,512]{2,1,0:T(8,128)(2,1)}, bf16[4,288,512]{2,1,0:T(8,128)(2,1)}, u32[]{:S(2)}, u32[]{:S(2)}) %collective-permute-start.58) | collective-permute-done | bytes 1179680 | tf_op jit(solution)/shard_map/ppermute | solution.py:143
  699.6 12.7 %collective-permute-done.60 = bf16[4,288,512]{2,1,0:T(8,128)(2,1)} collective-permute-done((bf16[4,288,512]{2,1,0:T(8,128)(2,1)}, bf16[4,288,512]{2,1,0:T(8,128)(2,1)}, u32[]{:S(2)}, u32[]{:S(2)}) %collective-permute-start.60) | collective-permute-done | bytes 1179680 | tf_op jit(solution)/shard_map/ppermute | solution.py:143
  732.2 17.2 %collective-permute-done.63 = bf16[4,272,512]{2,1,0:T(8,128)(2,1)} collective-permute-done((bf16[4,272,512]{2,1,0:T(8,128)(2,1)S(1)}, bf16[4,272,512]{2,1,0:T(8,128)(2,1)}, u32[]{:S(2)}, u32[]{:S(2)}) %collective-permute-start.63) | collective-permute-done | bytes 1114144 | tf_op jit(solution)/shard_map/ppermute | solution.py:143
  767.5 15.6 %reduce-scatter.8.cloned.1.call-done = bf16[1,272,512]{2,1,0:T(8,128)(2,1)} async-done(((bf16[4,272,512]{2,1,0:T(8,128)(2,1)}), bf16[1,272,512]{2,1,0:T(8,128)(2,1)}) %reduce-scatter.8.cloned.1.call-update) | async-done | bytes 278544 | tf_op jit(solution)/shard_map/reduce_scatter | solution.py:1840
  (784 shorter events, 368.1 us)
Async XLA Ops:
  7.9 61.4 %all-gather.19.cloned.1.call-start = ((), (), s32[]{:S(2)}) async-start(), calls=%async_computation.16 | async-start | bytes 1310720 | tf_op jit(solution)/shard_map/all_gather | solution.py:1796
  18.6 83.9 %all-gather.17.cloned.1.call-start = ((), (), s32[]{:S(2)}) async-start(), calls=%async_computation.15 | async-start | bytes 1556480 | tf_op jit(solution)/shard_map/all_gather | solution.py:1796
  40.2 91.3 %all-gather.21.cloned.1.call-start = ((), (), s32[]{:S(2)}) async-start(), calls=%async_computation.17 | async-start | bytes 1310720 | tf_op jit(solution)/shard_map/all_gather | solution.py:1796
  69.3 103.7 %all-gather.25.cloned.1.call-start = ((), (), s32[]{:S(2)}) async-start(), calls=%async_computation.19 | async-start | bytes 1310720 | tf_op jit(solution)/shard_map/all_gather | solution.py:1796
  102.6 111.7 %all-gather.23.cloned.1.call-start = ((), (), s32[]{:S(2)}) async-start(), calls=%async_computation.18 | async-start | bytes 1310720 | tf_op jit(solution)/shard_map/all_gather | solution.py:1796
  107.6 50.8 %collective-permute-start.13 = (bf16[4,128,1024]{2,1,0:T(8,128)(2,1)S(1)}, bf16[4,128,1024]{2,1,0:T(8,128)(2,1)}, u32[]{:S(2)}, u32[]{:S(2)}) collective-permute-start(bf16[4,128,1024]{2,1,0:T(8,128)(2,1)S(1)} %collective-permute-done.7.refs_6_), channel_id=1, source_target_pairs={{0,8},{8,0},{16,24},{24,16},{1,9},{9,1},{17,25},{25,17},{2,10},{10... | collective-permute-start | bytes 3145736 | tf_op jit(solution)/shard_map/ppermute | solution.py:143
  131.6 106.7 %all-gather.27.cloned.1.call-start = ((), (), s32[]{:S(2)}) async-start(), calls=%async_computation.20 | async-start | bytes 1310720 | tf_op jit(solution)/shard_map/all_gather | solution.py:1796
  132.6 76.3 %collective-permute-start.12 = (bf16[4,304,512]{2,1,0:T(8,128)(2,1)}, bf16[4,304,512]{2,1,0:T(8,128)(2,1)}, u32[]{:S(2)}, u32[]{:S(2)}) collective-permute-start(bf16[4,304,512]{2,1,0:T(8,128)(2,1)} %collective-permute-done.11.refs_2_.refs_6_), channel_id=1, source_target_pairs={{0,8},{8,0},{16,24},{24,16},{1,9},{9,1},{17,25},{25,17},{2,10},{10... | collective-permute-start | bytes 3735560 | tf_op jit(solution)/shard_map/ppermute | solution.py:143
  134.4 71.0 %collective-permute-start.16 = (bf16[4,128,1024]{2,1,0:T(8,128)(2,1)}, bf16[4,128,1024]{2,1,0:T(8,128)(2,1)}, u32[]{:S(2)}, u32[]{:S(2)}) collective-permute-start(bf16[4,128,1024]{2,1,0:T(8,128)(2,1)} %collective-permute-done.8.refs_5_), channel_id=1, source_target_pairs={{0,16},{8,24},{16,0},{24,8},{1,17},{9,25},{17,1},{25,9},{2,18},{10... | collective-permute-start | bytes 3145736 | tf_op jit(solution)/shard_map/ppermute | solution.py:143
  173.0 548.0 %reduce-scatter.18.cloned.1.call-start = ((), (), s32[]{:S(2)}) async-start(), calls=%async_computation.12 | async-start | bytes 1310720 | tf_op jit(solution)/shard_map/reduce_scatter | solution.py:1840
  267.9 53.5 %collective-permute-start.28 = (bf16[4,256,512]{2,1,0:T(8,128)(2,1)}, bf16[4,256,512]{2,1,0:T(8,128)(2,1)}, u32[]{:S(2)}, u32[]{:S(2)}) collective-permute-start(bf16[4,256,512]{2,1,0:T(8,128)(2,1)} %collective-permute-done.18.refs_2_), channel_id=1, source_target_pairs={{0,8},{8,0},{16,24},{24,16},{1,9},{9,1},{17,25},{25,17},{2,10},{10... | collective-permute-start | bytes 3145736 | tf_op jit(solution)/shard_map/ppermute | solution.py:143
  284.7 56.6 %collective-permute-start.30 = (bf16[768,1024]{1,0:T(8,128)(2,1)}, bf16[768,1024]{1,0:T(8,128)(2,1)S(1)}, u32[]{:S(2)}, u32[]{:S(2)}) collective-permute-start(bf16[768,1024]{1,0:T(8,128)(2,1)} %copy-done.25), channel_id=1, source_target_pairs={{0,1},{1,0},{2,3},{3,2},{4,5},{5,4},{6,7},{7,6},{8,9},{9,8},{10,11... | collective-permute-start | bytes 4718600 | tf_op jit(solution)/shard_map/ppermute | solution.py:135
  471.1 84.0 %collective-permute-start.43 = (bf16[4,256,512]{2,1,0:T(8,128)(2,1)}, bf16[4,256,512]{2,1,0:T(8,128)(2,1)}, u32[]{:S(2)}, u32[]{:S(2)}) collective-permute-start(bf16[4,256,512]{2,1,0:T(8,128)(2,1)} %get-tuple-element.289), channel_id=1, source_target_pairs={{0,8},{8,0},{16,24},{24,16},{1,9},{9,1},{17,25},{25,17},{2,10},{10... | collective-permute-start | bytes 3145736 | tf_op jit(solution)/shard_map/ppermute | solution.py:143
  473.1 82.0 %collective-permute-start.44 = (bf16[4,256,512]{2,1,0:T(8,128)(2,1)}, bf16[4,256,512]{2,1,0:T(8,128)(2,1)}, u32[]{:S(2)}, u32[]{:S(2)}) collective-permute-start(bf16[4,256,512]{2,1,0:T(8,128)(2,1)} %add_convert_fusion.12), channel_id=1, source_target_pairs={{0,16},{8,24},{16,0},{24,8},{1,17},{9,25},{17,1},{25,9},{2,18},{10... | collective-permute-start | bytes 3145736 | tf_op jit(solution)/shard_map/ppermute | solution.py:143
  488.0 52.4 %collective-permute-start.42 = (bf16[4,256,512]{2,1,0:T(8,128)(2,1)}, bf16[4,256,512]{2,1,0:T(8,128)(2,1)}, u32[]{:S(2)}, u32[]{:S(2)}) collective-permute-start(bf16[4,256,512]{2,1,0:T(8,128)(2,1)} %get-tuple-element.283), channel_id=1, source_target_pairs={{0,16},{8,24},{16,0},{24,8},{1,17},{9,25},{17,1},{25,9},{2,18},{10... | collective-permute-start | bytes 3145736 | tf_op jit(solution)/shard_map/ppermute | solution.py:143
  558.1 166.9 %reduce-scatter.20.cloned.1.call-start = ((), (), s32[]{:S(2)}) async-start(), calls=%async_computation.13 | async-start | bytes 1310720 | tf_op jit(solution)/shard_map/reduce_scatter | solution.py:1840
  558.4 55.0 %collective-permute-start.50 = (bf16[4,256,512]{2,1,0:T(8,128)(2,1)}, bf16[4,256,512]{2,1,0:T(8,128)(2,1)}, u32[]{:S(2)}, u32[]{:S(2)}) collective-permute-start(bf16[4,256,512]{2,1,0:T(8,128)(2,1)} %copy-done.61), channel_id=1, source_target_pairs={{0,16},{8,24},{16,0},{24,8},{1,17},{9,25},{17,1},{25,9},{2,18},{10... | collective-permute-start | bytes 3145736 | tf_op jit(solution)/shard_map/ppermute | solution.py:143
  559.9 54.0 %collective-permute-start.49 = (bf16[4,256,512]{2,1,0:T(8,128)(2,1)}, bf16[4,256,512]{2,1,0:T(8,128)(2,1)}, u32[]{:S(2)}, u32[]{:S(2)}) collective-permute-start(bf16[4,256,512]{2,1,0:T(8,128)(2,1)} %add_convert_fusion.10), channel_id=1, source_target_pairs={{0,8},{8,0},{16,24},{24,16},{1,9},{9,1},{17,25},{25,17},{2,10},{10... | collective-permute-start | bytes 3145736 | tf_op jit(solution)/shard_map/ppermute | solution.py:143
  562.8 166.4 %reduce-scatter.16.cloned.1.call-start = ((), (), s32[]{:S(2)}) async-start(), calls=%async_computation.11 | async-start | bytes 1310720 | tf_op jit(solution)/shard_map/reduce_scatter | solution.py:1840
  572.5 74.5 %collective-permute-start.54 = (bf16[4,128,1024]{2,1,0:T(8,128)(2,1)}, bf16[4,128,1024]{2,1,0:T(8,128)(2,1)}, u32[]{:S(2)}, u32[]{:S(2)}) collective-permute-start(bf16[4,128,1024]{2,1,0:T(8,128)(2,1)} %get-tuple-element.322), channel_id=1, source_target_pairs={{0,8},{8,0},{16,24},{24,16},{1,9},{9,1},{17,25},{25,17},{2,10},{10... | collective-permute-start | bytes 3145736 | tf_op jit(solution)/shard_map/ppermute | solution.py:143
  618.4 136.7 %reduce-scatter.10.cloned.1.call-start = ((), (), s32[]{:S(2)}) async-start(), calls=%async_computation.8 | async-start | bytes 1310720 | tf_op jit(solution)/shard_map/reduce_scatter | solution.py:1840
  659.8 98.1 %reduce-scatter.12.cloned.1.call-start = ((), (), s32[]{:S(2)}) async-start(), calls=%async_computation.9 | async-start | bytes 1310720 | tf_op jit(solution)/shard_map/reduce_scatter | solution.py:1840
  665.2 96.9 %reduce-scatter.14.cloned.1.call-start = ((), (), s32[]{:S(2)}) async-start(), calls=%async_computation.10 | async-start | bytes 1474560 | tf_op jit(solution)/shard_map/reduce_scatter | solution.py:1840
  720.7 62.4 %reduce-scatter.8.cloned.1.call-start = ((), (), s32[]{:S(2)}) async-start(), calls=%async_computation.7 | async-start | bytes 1392640 | tf_op jit(solution)/shard_map/reduce_scatter | solution.py:1840
  (236 other events, 2845.3 us)
Sparse Core Ops, SparseCore 0:
  9.6 30.5 all-gather.14
  41.8 27.4 all-gather.18
  71.4 31.0 all-gather.16
  104.5 26.9 all-gather.20
  133.5 27.4 all-gather.24
  163.0 27.4 all-gather.22
  192.6 27.4 all-gather.26
  558.3 28.9 reduce-scatter.17
  589.7 25.8 reduce-scatter.19
  618.5 28.0 reduce-scatter.15
  659.9 28.1 reduce-scatter.9
  690.2 25.7 reduce-scatter.11
  720.8 30.0 reduce-scatter.13
  753.2 29.7 reduce-scatter.7

commit v6 on v5

--- a/solution.py
+++ b/solution.py
@@ -2097,10 +2097,10 @@
     )
     gue, p9, s_gue = order.run(ffn_back, gfe, egp, w["enc_up"], w["enc_down"])
     p9_got = swap(p9)
+    r_ed = grads([eg, gfe], down_terms, 128, D)
+    r_eu = grads([eh1_low, gue], up_terms, 256)
     total_dd = next(r_dd)
     next(r_cross)
-    r_ed = grads([eg, gfe], down_terms, 128, D)
-    r_eu = grads([eh1_low, gue], up_terms, 256)
     total_du = next(r_du)
     gz1e, goe, gea_keep, gea_send, e_gain1, e_shift1, s_goe = order.run(
         branch_back, gz2e, p9, p9_got, eunit1, einv1, eg_rows[0:1], w["enc"]

time: 806 us -> 794 us (0.985)
  waiting for transfers between devices: 354 us -> 342 us
    ppermute x42, waiting for transfers between devices: 246 us -> 234 us  [flip_dp(): return lax.ppermute(value, 'dp', [(i, i ^ mask) for i in range(self.ndp)])]
    unnamed x381 -> x373, local copies, waits for them, and re-layouts: 71.9 us -> 71.9 us
  transfers between devices with their start and end apart: 86 -> 86, of which waited for: 35 -> 34; matrix products, arithmetic and copies ran while one was open for 12% -> 13% of each run, Pallas kernels for 17% -> 17%
where the time goes in v6:
time: 794 us; the launch traced here: 784 us
  waiting for transfers between devices  342 us (43%)
  Pallas kernels  205 us (26%)
  local copies, waits for them, and re-layouts  96.9 us (12%)
  other arithmetic  72 us (9%)
  starting transfers between devices  50.4 us (6%)
  between operations  18 us (2%)
    ppermute x42, waiting for transfers between devices, flip_dp(): return lax.ppermute(value, 'dp', [(i, i ^ mask) for i in range(self.ndp)])  234 us
    pallas_call x26, Pallas kernels, run(): pl.pallas_call(body, grid=(grid,), in_specs=[s for a, s in ins], out_spec...  194 us
    all_gather x7, waiting for transfers between devices, gather(): own = lax.all_gather(buf, 'fsdp', axis=0, axis_index_groups=self.groups)  80.6 us
    unnamed x373, local copies, waits for them, and re-layouts  71.9 us
    ppermute x42, starting transfers between devices, flip_dp(): return lax.ppermute(value, 'dp', [(i, i ^ mask) for i in range(self.ndp)])  44 us
    convert_element_type x14, other arithmetic, add(): sum((v.astype(F32) for v in others), first.astype(F32)).astype(dtype)  31.7 us
    select_n x34, other arithmetic, pick(): return jnp.where(self.core == 0, first, second)  18.2 us
  transfers between devices with their start and end apart: 86, of which 34 were waited for; matrix products, arithmetic and copies ran while one was open for 13% of the time, Pallas kernels for 17%

profile of v6, /device:TPU:0, one launch (start us, length us, event | category | flops | bytes accessed | tf_op | source)
XLA Modules:
  0.0 784.2 jit_solution(4011420247462275268)
XLA Ops:
  20.6 19.6 %all-gather.15.cloned.1.call-done = bf16[512,1024]{1,0:T(8,128)(2,1)} async-done(((bf16[128,1024]{1,0:T(8,128)(2,1)}), bf16[512,1024]{1,0:T(8,128)(2,1)}) %all-gather.15.cloned.1.call-update) | async-done | bytes 1048592 | tf_op jit(solution)/shard_map/all_gather | solution.py:1796
  51.0 18.3 %all-gather.19.cloned.1.call-done = bf16[512,1024]{1,0:T(8,128)(2,1)} async-done(((bf16[128,1024]{1,0:T(8,128)(2,1)}), bf16[512,1024]{1,0:T(8,128)(2,1)}) %all-gather.19.cloned.1.call-update) | async-done | bytes 1048592 | tf_op jit(solution)/shard_map/all_gather | solution.py:1796
  80.1 22.5 %all-gather.17.cloned.1.call-done = bf16[1216,512]{1,0:T(8,128)(2,1)} async-done(((bf16[304,512]{1,0:T(8,128)(2,1)}), bf16[1216,512]{1,0:T(8,128)(2,1)}) %all-gather.17.cloned.1.call-update) | async-done | bytes 1245200 | tf_op jit(solution)/shard_map/all_gather | solution.py:1796
  111.4 20.1 %all-gather.21.cloned.1.call-done = bf16[1024,512]{1,0:T(8,128)(2,1)} async-done(((bf16[256,512]{1,0:T(8,128)(2,1)}), bf16[1024,512]{1,0:T(8,128)(2,1)}) %all-gather.21.cloned.1.call-update) | async-done | bytes 1048592 | tf_op jit(solution)/shard_map/all_gather | solution.py:1796
  135.9 22.5 %collective-permute-done.13.refs_7_ = bf16[4,128,1024]{2,1,0:T(8,128)(2,1)} collective-permute-done((bf16[4,128,1024]{2,1,0:T(8,128)(2,1)S(1)}, bf16[4,128,1024]{2,1,0:T(8,128)(2,1)}, u32[]{:S(2)}, u32[]{:S(2)}) %collective-permute-start.13) | collective-permute-done | bytes 1048608 | tf_op jit(solution)/shard_map/ppermute | solution.py:143
  173.1 32.3 %collective-permute-done.14.refs_1_ = bf16[4,256,512]{2,1,0:T(8,128)(2,1)} collective-permute-done((bf16[4,256,512]{2,1,0:T(8,128)(2,1)}, bf16[4,256,512]{2,1,0:T(8,128)(2,1)}, u32[]{:S(2)}, u32[]{:S(2)}) %collective-permute-start.14) | collective-permute-done | bytes 1048608 | tf_op jit(solution)/shard_map/ppermute | solution.py:143
  216.9 17.1 %shard_map.366 = (bf16[768,1536]{1,0:T(8,128)(2,1)S(1)}, f32[768,256]{1,0:T(8,128)S(1)}, bf16[768,256]{1,0:T(8,128)(2,1)S(1)}, bf16[768,256]{1,0:T(8,128)(2,1)}) custom-call(s32[8]{0:T(128)S(1)} %concatenate.330.place, bf16[768,1024]{1,0:T(8,128)(2,1)S(1)} %maximum_select_fusion.y.refs_0_, f32[1,1536]{1,0:T(1,128)S(1)} %broadcast_in_dim.18.bias, ...), custom_call_target="tpu_custom_call" | custom-call | flops 19000000512 | bytes 19000000 | tf_op jit(solution)/shard_map/pallas_call | solution.py:744
  238.3 17.5 %collective-permute-done.19.refs_3_ = bf16[4,256,512]{2,1,0:T(8,128)(2,1)} collective-permute-done((bf16[4,256,512]{2,1,0:T(8,128)(2,1)}, bf16[4,256,512]{2,1,0:T(8,128)(2,1)}, u32[]{:S(2)}, u32[]{:S(2)}) %collective-permute-start.19) | collective-permute-done | bytes 1048608 | tf_op jit(solution)/shard_map/ppermute | solution.py:143
  258.0 8.9 %shard_map.367 = (bf16[256,1536]{1,0:T(8,128)(2,1)S(1)}, bf16[256,256]{1,0:T(8,128)(2,1)S(1)}, bf16[256,256]{1,0:T(8,128)(2,1)S(1)}) custom-call(s32[8]{0:T(128)S(1)} %concatenate.330.place, bf16[256,1024]{1,0:T(8,128)(2,1)S(1)} %copy-done.19, f32[1,1536]{1,0:T(1,128)S(1)} %broadcast_in_dim.19.bias, bf16[4,256,512]{2,1,0:T(8,128)(2,1)S(1)} %bitcast.230, ...), custom_call_target="tpu_custom_call" | custom-call | flops 10000000000 | bytes 10000000 | tf_op jit(solution)/shard_map/pallas_call | solution.py:744
  288.4 27.9 %collective-permute-done.26.refs_1_ = bf16[4,256,512]{2,1,0:T(8,128)(2,1)} collective-permute-done((bf16[4,256,512]{2,1,0:T(8,128)(2,1)}, bf16[4,256,512]{2,1,0:T(8,128)(2,1)}, u32[]{:S(2)}, u32[]{:S(2)}) %collective-permute-start.26) | collective-permute-done | bytes 1048608 | tf_op jit(solution)/shard_map/ppermute | solution.py:143
  331.7 9.5 %collective-permute-done.29.refs_3_ = bf16[4,256,512]{2,1,0:T(8,128)(2,1)S(1)} collective-permute-done((bf16[4,256,512]{2,1,0:T(8,128)(2,1)}, bf16[4,256,512]{2,1,0:T(8,128)(2,1)S(1)}, u32[]{:S(2)}, u32[]{:S(2)}) %collective-permute-start.29) | collective-permute-done | bytes 1048608 | tf_op jit(solution)/shard_map/ppermute | solution.py:143
  341.3 9.6 %shard_map.372 = (f32[768,1024]{1,0:T(8,128)S(1)}, f32[768,128]{1,0:T(8,128)S(1)}, bf16[768,1024]{1,0:T(8,128)(2,1)S(1)}, f32[256,1024]{1,0:T(8,128)S(1)}, f32[2...) custom-call(s32[8]{0:T(128)S(1)} %concatenate.330.place, ...), custom_call_target="tpu_custom_call" | custom-call | flops 15000000512 | bytes 15000000 | tf_op jit(solution)/shard_map/pallas_call | solution.py:744
  369.4 17.0 %shard_map.375 = (bf16[768,2048]{1,0:T(8,128)(2,1)S(1)}, bf16[768,2048]{1,0:T(8,128)(2,1)S(1)}, bf16[768,1024]{1,0:T(8,128)(2,1)}) custom-call(s32[8]{0:T(128)S(1)} %concatenate.330.place, bf16[768,1024]{1,0:T(8,128)(2,1)S(1)} %get-tuple-element.232.low.refs_0_, f32[1,2048]{1,0:T(1,128)S(1)} %fusion.28.hb, bf16[4,256,512]{2,1,0:T(8,128)(2,1)} %bitcast.22.refs_0_, ...), custom_call_target="tpu_custom_call" | custom-call | flops 14000000000 | bytes 14000000 | tf_op jit(solution)/shard_map/pallas_call | solution.py:744
  409.9 10.8 %shard_map.378 = (bf16[768,2048]{1,0:T(8,128)(2,1)S(1)}, bf16[768,1024]{1,0:T(8,128)(2,1)S(1)}, f32[1,2048]{1,0:T(1,128)S(1)}) custom-call(s32[8]{0:T(128)S(1)} %concatenate.330.place, bf16[768,1024]{1,0:T(8,128)(2,1)S(1)} %get-tuple-element.238.refs_1_.gf, bf16[768,2048]{1,0:T(8,128)(2,1)S(1)} %copy-done.118, bf16[4,256,512]{2,1,0:T(8,128)(2,1)} %bitcast.22.refs_0_, ...), custom_call_target="tpu_custom_call" | custom-call | flops 14000000000 | bytes 14000000 | tf_op jit(solution)/shard_map/pallas_call | solution.py:744
  434.9 11.4 %collective-permute-done.36 = bf16[4,128,1024]{2,1,0:T(8,128)(2,1)S(1)} collective-permute-done((bf16[4,128,1024]{2,1,0:T(8,128)(2,1)S(1)}, bf16[4,128,1024]{2,1,0:T(8,128)(2,1)S(1)}, u32[]{:S(2)}, u32[]{:S(2)}) %collective-permute-start.36) | collective-permute-done | bytes 1048608 | tf_op jit(solution)/shard_map/ppermute | solution.py:143
  454.9 12.9 %shard_map.381 = (bf16[768,512]{1,0:T(8,128)(2,1)S(1)}, bf16[256,1024]{1,0:T(8,128)(2,1)S(1)}, bf16[1024,1024]{1,0:T(8,128)(2,1)}, f32[1,512]{1,0:T(1,128)S(1)}, f32[1,1024]{1,0:T(1,128)S(1)}) custom-call(s32[8]{0:T(128)S(1)} %concatenate.330.place, bf16[768,512]{1,0:T(8,128)(2,1)S(1)} %copy-done.142, bf16[256,1024]{1,0:T(8,128)(2,1)S(1)} %copy-done.144, ...), custom_call_target="tpu_custom_call" | custom-call | flops 14000000000 | bytes 14000000 | tf_op jit(solution)/shard_map/pallas_call | solution.py:744
  524.6 15.8 %collective-permute-done.42 = bf16[4,256,512]{2,1,0:T(8,128)(2,1)} collective-permute-done((bf16[4,256,512]{2,1,0:T(8,128)(2,1)}, bf16[4,256,512]{2,1,0:T(8,128)(2,1)}, u32[]{:S(2)}, u32[]{:S(2)}) %collective-permute-start.42) | collective-permute-done | bytes 1048608 | tf_op jit(solution)/shard_map/ppermute | solution.py:143
  561.2 24.8 %shard_map.389 = (bf16[768,1536]{1,0:T(8,128)(2,1)S(1)}, bf16[768,256]{1,0:T(8,128)(2,1)S(1)}, f32[384,1024]{1,0:T(8,128)S(1)}, bf16[384,1024]{1,0:T(8,128)(2,1)...) custom-call(s32[8]{0:T(128)S(1)} %concatenate.330.place, bf16[768,1536]{1,0:T(8,128)(2,1)S(1)} %copy-done.134, ...), custom_call_target="tpu_custom_call" | custom-call | flops 28999999488 | bytes 29000000 | tf_op jit(solution)/shard_map/pallas_call | solution.py:744
  586.1 10.6 %collective-permute-done.47 = bf16[4,128,1024]{2,1,0:T(8,128)(2,1)} collective-permute-done((bf16[4,128,1024]{2,1,0:T(8,128)(2,1)}, bf16[4,128,1024]{2,1,0:T(8,128)(2,1)}, u32[]{:S(2)}, u32[]{:S(2)}) %collective-permute-start.47) | collective-permute-done | bytes 1048608 | tf_op jit(solution)/shard_map/ppermute | solution.py:143
  611.9 11.0 %shard_map.390 = (bf16[256,1536]{1,0:T(8,128)(2,1)S(1)}, f32[128,1024]{1,0:T(8,128)S(1)}, bf16[128,1024]{1,0:T(8,128)(2,1)S(1)}, f32[1,1536]{1,0:T(1,128)S(1)}) custom-call(s32[8]{0:T(128)S(1)} %concatenate.330.place, bf16[256,1536]{1,0:T(8,128)(2,1)S(1)} %copy-done.132, bf16[256,256]{1,0:T(8,128)(2,1)S(1)} %copy-done.124, ...), custom_call_target="tpu_custom_call" | custom-call | flops 12999999488 | bytes 13000000 | tf_op jit(solution)/shard_map/pallas_call | solution.py:744
  659.0 20.8 %collective-permute-done.58 = bf16[4,288,512]{2,1,0:T(8,128)(2,1)} collective-permute-done((bf16[4,288,512]{2,1,0:T(8,128)(2,1)}, bf16[4,288,512]{2,1,0:T(8,128)(2,1)}, u32[]{:S(2)}, u32[]{:S(2)}) %collective-permute-start.58) | collective-permute-done | bytes 1179680 | tf_op jit(solution)/shard_map/ppermute | solution.py:143
  687.4 12.7 %collective-permute-done.60 = bf16[4,288,512]{2,1,0:T(8,128)(2,1)} collective-permute-done((bf16[4,288,512]{2,1,0:T(8,128)(2,1)}, bf16[4,288,512]{2,1,0:T(8,128)(2,1)}, u32[]{:S(2)}, u32[]{:S(2)}) %collective-permute-start.60) | collective-permute-done | bytes 1179680 | tf_op jit(solution)/shard_map/ppermute | solution.py:143
  720.0 17.2 %collective-permute-done.63 = bf16[4,272,512]{2,1,0:T(8,128)(2,1)} collective-permute-done((bf16[4,272,512]{2,1,0:T(8,128)(2,1)S(1)}, bf16[4,272,512]{2,1,0:T(8,128)(2,1)}, u32[]{:S(2)}, u32[]{:S(2)}) %collective-permute-start.63) | collective-permute-done | bytes 1114144 | tf_op jit(solution)/shard_map/ppermute | solution.py:143
  755.4 15.5 %reduce-scatter.8.cloned.1.call-done = bf16[1,272,512]{2,1,0:T(8,128)(2,1)} async-done(((bf16[4,272,512]{2,1,0:T(8,128)(2,1)}), bf16[1,272,512]{2,1,0:T(8,128)(2,1)}) %reduce-scatter.8.cloned.1.call-update) | async-done | bytes 278544 | tf_op jit(solution)/shard_map/reduce_scatter | solution.py:1840
  (776 shorter events, 359.9 us)
Async XLA Ops:
  7.9 61.4 %all-gather.19.cloned.1.call-start = ((), (), s32[]{:S(2)}) async-start(), calls=%async_computation.16 | async-start | bytes 1310720 | tf_op jit(solution)/shard_map/all_gather | solution.py:1796
  18.6 83.9 %all-gather.17.cloned.1.call-start = ((), (), s32[]{:S(2)}) async-start(), calls=%async_computation.15 | async-start | bytes 1556480 | tf_op jit(solution)/shard_map/all_gather | solution.py:1796
  40.2 91.3 %all-gather.21.cloned.1.call-start = ((), (), s32[]{:S(2)}) async-start(), calls=%async_computation.17 | async-start | bytes 1310720 | tf_op jit(solution)/shard_map/all_gather | solution.py:1796
  69.3 103.7 %all-gather.25.cloned.1.call-start = ((), (), s32[]{:S(2)}) async-start(), calls=%async_computation.19 | async-start | bytes 1310720 | tf_op jit(solution)/shard_map/all_gather | solution.py:1796
  102.6 111.7 %all-gather.23.cloned.1.call-start = ((), (), s32[]{:S(2)}) async-start(), calls=%async_computation.18 | async-start | bytes 1310720 | tf_op jit(solution)/shard_map/all_gather | solution.py:1796
  131.6 106.7 %all-gather.27.cloned.1.call-start = ((), (), s32[]{:S(2)}) async-start(), calls=%async_computation.20 | async-start | bytes 1310720 | tf_op jit(solution)/shard_map/all_gather | solution.py:1796
  132.6 76.3 %collective-permute-start.12 = (bf16[4,304,512]{2,1,0:T(8,128)(2,1)}, bf16[4,304,512]{2,1,0:T(8,128)(2,1)}, u32[]{:S(2)}, u32[]{:S(2)}) collective-permute-start(bf16[4,304,512]{2,1,0:T(8,128)(2,1)} %collective-permute-done.11.refs_2_.refs_6_), channel_id=1, source_target_pairs={{0,8},{8,0},{16,24},{24,16},{1,9},{9,1},{17,25},{25,17},{2,10},{10... | collective-permute-start | bytes 3735560 | tf_op jit(solution)/shard_map/ppermute | solution.py:143
  134.4 71.0 %collective-permute-start.16 = (bf16[4,128,1024]{2,1,0:T(8,128)(2,1)}, bf16[4,128,1024]{2,1,0:T(8,128)(2,1)}, u32[]{:S(2)}, u32[]{:S(2)}) collective-permute-start(bf16[4,128,1024]{2,1,0:T(8,128)(2,1)} %collective-permute-done.8.refs_5_), channel_id=1, source_target_pairs={{0,16},{8,24},{16,0},{24,8},{1,17},{9,25},{17,1},{25,9},{2,18},{10... | collective-permute-start | bytes 3145736 | tf_op jit(solution)/shard_map/ppermute | solution.py:143
  173.0 535.8 %reduce-scatter.18.cloned.1.call-start = ((), (), s32[]{:S(2)}) async-start(), calls=%async_computation.12 | async-start | bytes 1310720 | tf_op jit(solution)/shard_map/reduce_scatter | solution.py:1840
  267.9 53.5 %collective-permute-start.28 = (bf16[4,256,512]{2,1,0:T(8,128)(2,1)}, bf16[4,256,512]{2,1,0:T(8,128)(2,1)}, u32[]{:S(2)}, u32[]{:S(2)}) collective-permute-start(bf16[4,256,512]{2,1,0:T(8,128)(2,1)} %collective-permute-done.18.refs_2_), channel_id=1, source_target_pairs={{0,8},{8,0},{16,24},{24,16},{1,9},{9,1},{17,25},{25,17},{2,10},{10... | collective-permute-start | bytes 3145736 | tf_op jit(solution)/shard_map/ppermute | solution.py:143
  284.7 56.6 %collective-permute-start.30 = (bf16[768,1024]{1,0:T(8,128)(2,1)}, bf16[768,1024]{1,0:T(8,128)(2,1)S(1)}, u32[]{:S(2)}, u32[]{:S(2)}) collective-permute-start(bf16[768,1024]{1,0:T(8,128)(2,1)} %copy-done.25), channel_id=1, source_target_pairs={{0,1},{1,0},{2,3},{3,2},{4,5},{5,4},{6,7},{7,6},{8,9},{9,8},{10,11... | collective-permute-start | bytes 4718600 | tf_op jit(solution)/shard_map/ppermute | solution.py:135
  469.6 53.4 %collective-permute-start.41 = (bf16[4,128,1024]{2,1,0:T(8,128)(2,1)}, bf16[4,128,1024]{2,1,0:T(8,128)(2,1)S(1)}, u32[]{:S(2)}, u32[]{:S(2)}) collective-permute-start(bf16[4,128,1024]{2,1,0:T(8,128)(2,1)} %get-tuple-element.285), channel_id=1, source_target_pairs={{0,16},{8,24},{16,0},{24,8},{1,17},{9,25},{17,1},{25,9},{2,18},{10... | collective-permute-start | bytes 3145736 | tf_op jit(solution)/shard_map/ppermute | solution.py:143
  471.1 71.9 %collective-permute-start.43 = (bf16[4,256,512]{2,1,0:T(8,128)(2,1)}, bf16[4,256,512]{2,1,0:T(8,128)(2,1)}, u32[]{:S(2)}, u32[]{:S(2)}) collective-permute-start(bf16[4,256,512]{2,1,0:T(8,128)(2,1)} %get-tuple-element.289), channel_id=1, source_target_pairs={{0,8},{8,0},{16,24},{24,16},{1,9},{9,1},{17,25},{25,17},{2,10},{10... | collective-permute-start | bytes 3145736 | tf_op jit(solution)/shard_map/ppermute | solution.py:143
  473.1 69.9 %collective-permute-start.44 = (bf16[4,256,512]{2,1,0:T(8,128)(2,1)}, bf16[4,256,512]{2,1,0:T(8,128)(2,1)}, u32[]{:S(2)}, u32[]{:S(2)}) collective-permute-start(bf16[4,256,512]{2,1,0:T(8,128)(2,1)} %add_convert_fusion.12), channel_id=1, source_target_pairs={{0,16},{8,24},{16,0},{24,8},{1,17},{9,25},{17,1},{25,9},{2,18},{10... | collective-permute-start | bytes 3145736 | tf_op jit(solution)/shard_map/ppermute | solution.py:143
  488.1 52.4 %collective-permute-start.42 = (bf16[4,256,512]{2,1,0:T(8,128)(2,1)}, bf16[4,256,512]{2,1,0:T(8,128)(2,1)}, u32[]{:S(2)}, u32[]{:S(2)}) collective-permute-start(bf16[4,256,512]{2,1,0:T(8,128)(2,1)} %get-tuple-element.287), channel_id=1, source_target_pairs={{0,16},{8,24},{16,0},{24,8},{1,17},{9,25},{17,1},{25,9},{2,18},{10... | collective-permute-start | bytes 3145736 | tf_op jit(solution)/shard_map/ppermute | solution.py:143
  546.0 166.9 %reduce-scatter.20.cloned.1.call-start = ((), (), s32[]{:S(2)}) async-start(), calls=%async_computation.13 | async-start | bytes 1310720 | tf_op jit(solution)/shard_map/reduce_scatter | solution.py:1840
  546.2 55.0 %collective-permute-start.50 = (bf16[4,256,512]{2,1,0:T(8,128)(2,1)}, bf16[4,256,512]{2,1,0:T(8,128)(2,1)}, u32[]{:S(2)}, u32[]{:S(2)}) collective-permute-start(bf16[4,256,512]{2,1,0:T(8,128)(2,1)} %copy-done.61), channel_id=1, source_target_pairs={{0,16},{8,24},{16,0},{24,8},{1,17},{9,25},{17,1},{25,9},{2,18},{10... | collective-permute-start | bytes 3145736 | tf_op jit(solution)/shard_map/ppermute | solution.py:143
  547.7 54.0 %collective-permute-start.49 = (bf16[4,256,512]{2,1,0:T(8,128)(2,1)}, bf16[4,256,512]{2,1,0:T(8,128)(2,1)}, u32[]{:S(2)}, u32[]{:S(2)}) collective-permute-start(bf16[4,256,512]{2,1,0:T(8,128)(2,1)} %add_convert_fusion.10), channel_id=1, source_target_pairs={{0,8},{8,0},{16,24},{24,16},{1,9},{9,1},{17,25},{25,17},{2,10},{10... | collective-permute-start | bytes 3145736 | tf_op jit(solution)/shard_map/ppermute | solution.py:143
  550.6 166.4 %reduce-scatter.16.cloned.1.call-start = ((), (), s32[]{:S(2)}) async-start(), calls=%async_computation.11 | async-start | bytes 1310720 | tf_op jit(solution)/shard_map/reduce_scatter | solution.py:1840
  560.3 74.6 %collective-permute-start.54 = (bf16[4,128,1024]{2,1,0:T(8,128)(2,1)}, bf16[4,128,1024]{2,1,0:T(8,128)(2,1)}, u32[]{:S(2)}, u32[]{:S(2)}) collective-permute-start(bf16[4,128,1024]{2,1,0:T(8,128)(2,1)} %get-tuple-element.322), channel_id=1, source_target_pairs={{0,8},{8,0},{16,24},{24,16},{1,9},{9,1},{17,25},{25,17},{2,10},{10... | collective-permute-start | bytes 3145736 | tf_op jit(solution)/shard_map/ppermute | solution.py:143
  606.3 136.7 %reduce-scatter.10.cloned.1.call-start = ((), (), s32[]{:S(2)}) async-start(), calls=%async_computation.8 | async-start | bytes 1310720 | tf_op jit(solution)/shard_map/reduce_scatter | solution.py:1840
  647.6 98.1 %reduce-scatter.12.cloned.1.call-start = ((), (), s32[]{:S(2)}) async-start(), calls=%async_computation.9 | async-start | bytes 1310720 | tf_op jit(solution)/shard_map/reduce_scatter | solution.py:1840
  653.0 97.0 %reduce-scatter.14.cloned.1.call-start = ((), (), s32[]{:S(2)}) async-start(), calls=%async_computation.10 | async-start | bytes 1474560 | tf_op jit(solution)/shard_map/reduce_scatter | solution.py:1840
  708.5 62.4 %reduce-scatter.8.cloned.1.call-start = ((), (), s32[]{:S(2)}) async-start(), calls=%async_computation.7 | async-start | bytes 1392640 | tf_op jit(solution)/shard_map/reduce_scatter | solution.py:1840
  (232 other events, 2808.3 us)
Sparse Core Ops, SparseCore 0:
  9.6 30.5 all-gather.14
  41.8 27.4 all-gather.18
  71.4 31.0 all-gather.16
  104.5 26.9 all-gather.20
  133.5 27.4 all-gather.24
  163.0 27.4 all-gather.22
  192.6 27.4 all-gather.26
  546.1 28.9 reduce-scatter.17
  577.5 25.7 reduce-scatter.19
  606.4 28.0 reduce-scatter.15
  647.8 28.0 reduce-scatter.9
  678.0 25.7 reduce-scatter.11
  708.6 30.0 reduce-scatter.13
  741.0 29.8 reduce-scatter.7

commit v7 on v6

--- a/solution.py
+++ b/solution.py
@@ -2071,12 +2071,12 @@
         branch_back, gz3, p6, p6_got, dunit2, dinv2, dg_rows[1:2], w["cross"]
     )
     gca_got = swap(gca_send)
+    gcq, gckv, p7, s_gcq, s_gckv = order.run(
+        cross_back, cq, ckv, gca_keep, gca_got, w["cross"]
+    )
+    p7_got = swap(p7)
     next(r_dd)
     next(r_du)
-    gcq, gckv, p7, s_gcq, s_gckv = order.run(
-        cross_back, cq, ckv, gca_keep, gca_got, w["cross"]
-    )
-    p7_got = swap(p7)
     r_cross = grads(
         [dh1_low, gcq, enc_low, gckv, ca_keep, ca_got, gx],
         [

time: 794 us -> 784 us (0.987)
  waiting for transfers between devices: 342 us -> 327 us
    ppermute x42, waiting for transfers between devices: 234 us -> 220 us  [flip_dp(): return lax.ppermute(value, 'dp', [(i, i ^ mask) for i in range(self.ndp)])]
    unnamed x373 -> x381, local copies, waits for them, and re-layouts: 71.9 us -> 72.1 us
  transfers between devices with their start and end apart: 86 -> 86, of which waited for: 34 -> 33; matrix products, arithmetic and copies ran while one was open for 13% -> 13% of each run, Pallas kernels for 17% -> 18%
where the time goes in v7:
time: 784 us; the launch traced here: 774 us
  waiting for transfers between devices  327 us (42%)
  Pallas kernels  205 us (26%)
  local copies, waits for them, and re-layouts  97.1 us (12%)
  other arithmetic  73.5 us (9%)
  starting transfers between devices  53.7 us (7%)
  between operations  18.1 us (2%)
    ppermute x42, waiting for transfers between devices, flip_dp(): return lax.ppermute(value, 'dp', [(i, i ^ mask) for i in range(self.ndp)])  220 us
    pallas_call x26, Pallas kernels, run(): pl.pallas_call(body, grid=(grid,), in_specs=[s for a, s in ins], out_spec...  194 us
    all_gather x7, waiting for transfers between devices, gather(): own = lax.all_gather(buf, 'fsdp', axis=0, axis_index_groups=self.groups)  80.6 us
    unnamed x381, local copies, waits for them, and re-layouts  72.1 us
    ppermute x42, starting transfers between devices, flip_dp(): return lax.ppermute(value, 'dp', [(i, i ^ mask) for i in range(self.ndp)])  46.7 us
    convert_element_type x14, other arithmetic, add(): sum((v.astype(F32) for v in others), first.astype(F32)).astype(dtype)  33.2 us
    select_n x34, other arithmetic, pick(): return jnp.where(self.core == 0, first, second)  18.2 us
  transfers between devices with their start and end apart: 86, of which 33 were waited for; matrix products, arithmetic and copies ran while one was open for 13% of the time, Pallas kernels for 18%

profile of v7, /device:TPU:0, one launch (start us, length us, event | category | flops | bytes accessed | tf_op | source)
XLA Modules:
  0.0 774.0 jit_solution(18330511425053006646)
XLA Ops:
  20.6 19.6 %all-gather.15.cloned.1.call-done = bf16[512,1024]{1,0:T(8,128)(2,1)} async-done(((bf16[128,1024]{1,0:T(8,128)(2,1)}), bf16[512,1024]{1,0:T(8,128)(2,1)}) %all-gather.15.cloned.1.call-update) | async-done | bytes 1048592 | tf_op jit(solution)/shard_map/all_gather | solution.py:1796
  51.0 18.3 %all-gather.19.cloned.1.call-done = bf16[512,1024]{1,0:T(8,128)(2,1)} async-done(((bf16[128,1024]{1,0:T(8,128)(2,1)}), bf16[512,1024]{1,0:T(8,128)(2,1)}) %all-gather.19.cloned.1.call-update) | async-done | bytes 1048592 | tf_op jit(solution)/shard_map/all_gather | solution.py:1796
  80.1 22.4 %all-gather.17.cloned.1.call-done = bf16[1216,512]{1,0:T(8,128)(2,1)} async-done(((bf16[304,512]{1,0:T(8,128)(2,1)}), bf16[1216,512]{1,0:T(8,128)(2,1)}) %all-gather.17.cloned.1.call-update) | async-done | bytes 1245200 | tf_op jit(solution)/shard_map/all_gather | solution.py:1796
  111.4 20.2 %all-gather.21.cloned.1.call-done = bf16[1024,512]{1,0:T(8,128)(2,1)} async-done(((bf16[256,512]{1,0:T(8,128)(2,1)}), bf16[1024,512]{1,0:T(8,128)(2,1)}) %all-gather.21.cloned.1.call-update) | async-done | bytes 1048592 | tf_op jit(solution)/shard_map/all_gather | solution.py:1796
  135.8 22.5 %collective-permute-done.13.refs_7_ = bf16[4,128,1024]{2,1,0:T(8,128)(2,1)} collective-permute-done((bf16[4,128,1024]{2,1,0:T(8,128)(2,1)S(1)}, bf16[4,128,1024]{2,1,0:T(8,128)(2,1)}, u32[]{:S(2)}, u32[]{:S(2)}) %collective-permute-start.13) | collective-permute-done | bytes 1048608 | tf_op jit(solution)/shard_map/ppermute | solution.py:143
  173.0 32.3 %collective-permute-done.14.refs_1_ = bf16[4,256,512]{2,1,0:T(8,128)(2,1)} collective-permute-done((bf16[4,256,512]{2,1,0:T(8,128)(2,1)}, bf16[4,256,512]{2,1,0:T(8,128)(2,1)}, u32[]{:S(2)}, u32[]{:S(2)}) %collective-permute-start.14) | collective-permute-done | bytes 1048608 | tf_op jit(solution)/shard_map/ppermute | solution.py:143
  216.8 17.1 %shard_map.366 = (bf16[768,1536]{1,0:T(8,128)(2,1)S(1)}, f32[768,256]{1,0:T(8,128)S(1)}, bf16[768,256]{1,0:T(8,128)(2,1)S(1)}, bf16[768,256]{1,0:T(8,128)(2,1)}) custom-call(s32[8]{0:T(128)S(1)} %concatenate.330.place, bf16[768,1024]{1,0:T(8,128)(2,1)S(1)} %maximum_select_fusion.y.refs_0_, f32[1,1536]{1,0:T(1,128)S(1)} %broadcast_in_dim.18.bias, ...), custom_call_target="tpu_custom_call" | custom-call | flops 19000000512 | bytes 19000000 | tf_op jit(solution)/shard_map/pallas_call | solution.py:744
  238.3 17.4 %collective-permute-done.19.refs_3_ = bf16[4,256,512]{2,1,0:T(8,128)(2,1)} collective-permute-done((bf16[4,256,512]{2,1,0:T(8,128)(2,1)}, bf16[4,256,512]{2,1,0:T(8,128)(2,1)}, u32[]{:S(2)}, u32[]{:S(2)}) %collective-permute-start.19) | collective-permute-done | bytes 1048608 | tf_op jit(solution)/shard_map/ppermute | solution.py:143
  258.0 8.9 %shard_map.367 = (bf16[256,1536]{1,0:T(8,128)(2,1)S(1)}, bf16[256,256]{1,0:T(8,128)(2,1)S(1)}, bf16[256,256]{1,0:T(8,128)(2,1)S(1)}) custom-call(s32[8]{0:T(128)S(1)} %concatenate.330.place, bf16[256,1024]{1,0:T(8,128)(2,1)S(1)} %copy-done.21, f32[1,1536]{1,0:T(1,128)S(1)} %broadcast_in_dim.19.bias, bf16[4,256,512]{2,1,0:T(8,128)(2,1)S(1)} %bitcast.230, ...), custom_call_target="tpu_custom_call" | custom-call | flops 10000000000 | bytes 10000000 | tf_op jit(solution)/shard_map/pallas_call | solution.py:744
  288.3 27.9 %collective-permute-done.26.refs_1_ = bf16[4,256,512]{2,1,0:T(8,128)(2,1)} collective-permute-done((bf16[4,256,512]{2,1,0:T(8,128)(2,1)}, bf16[4,256,512]{2,1,0:T(8,128)(2,1)}, u32[]{:S(2)}, u32[]{:S(2)}) %collective-permute-start.26) | collective-permute-done | bytes 1048608 | tf_op jit(solution)/shard_map/ppermute | solution.py:143
  321.4 8.3 %shard_map.371 = (bf16[256,2048]{1,0:T(8,128)(2,1)S(1)}, bf16[256,2048]{1,0:T(8,128)(2,1)S(1)}, bf16[256,1024]{1,0:T(8,128)(2,1)S(1)}) custom-call(s32[8]{0:T(128)S(1)} %concatenate.330.place, bf16[256,1024]{1,0:T(8,128)(2,1)S(1)} %get-tuple-element.220.low.refs_0_, f32[1,2048]{1,0:T(1,128)S(1)} %fusion.27.hb, bf16[4,256,512]{2,1,0:T(8,128)(2,1)S(1)} %bitcast.244, ...), custom_call_target="tpu_custom_call" | custom-call | flops 8000000000 | bytes 8000000 | tf_op jit(solution)/shard_map/pallas_call | solution.py:744
  331.7 9.5 %collective-permute-done.29.refs_3_ = bf16[4,256,512]{2,1,0:T(8,128)(2,1)S(1)} collective-permute-done((bf16[4,256,512]{2,1,0:T(8,128)(2,1)}, bf16[4,256,512]{2,1,0:T(8,128)(2,1)S(1)}, u32[]{:S(2)}, u32[]{:S(2)}) %collective-permute-start.29) | collective-permute-done | bytes 1048608 | tf_op jit(solution)/shard_map/ppermute | solution.py:143
  341.2 9.6 %shard_map.372 = (f32[768,1024]{1,0:T(8,128)S(1)}, f32[768,128]{1,0:T(8,128)S(1)}, bf16[768,1024]{1,0:T(8,128)(2,1)S(1)}, f32[256,1024]{1,0:T(8,128)S(1)}, f32[2...) custom-call(s32[8]{0:T(128)S(1)} %concatenate.330.place, ...), custom_call_target="tpu_custom_call" | custom-call | flops 15000000512 | bytes 15000000 | tf_op jit(solution)/shard_map/pallas_call | solution.py:744
  369.5 17.0 %shard_map.375 = (bf16[768,2048]{1,0:T(8,128)(2,1)S(1)}, bf16[768,2048]{1,0:T(8,128)(2,1)S(1)}, bf16[768,1024]{1,0:T(8,128)(2,1)}) custom-call(s32[8]{0:T(128)S(1)} %concatenate.330.place, bf16[768,1024]{1,0:T(8,128)(2,1)S(1)} %get-tuple-element.232.low.refs_0_, f32[1,2048]{1,0:T(1,128)S(1)} %fusion.28.hb, bf16[4,256,512]{2,1,0:T(8,128)(2,1)} %bitcast.22.refs_0_, ...), custom_call_target="tpu_custom_call" | custom-call | flops 14000000000 | bytes 14000000 | tf_op jit(solution)/shard_map/pallas_call | solution.py:744
  411.1 10.7 %shard_map.378 = (bf16[768,2048]{1,0:T(8,128)(2,1)S(1)}, bf16[768,1024]{1,0:T(8,128)(2,1)S(1)}, f32[1,2048]{1,0:T(1,128)S(1)}) custom-call(s32[8]{0:T(128)S(1)} %concatenate.330.place, bf16[768,1024]{1,0:T(8,128)(2,1)S(1)} %get-tuple-element.238.refs_1_.gf, bf16[768,2048]{1,0:T(8,128)(2,1)S(1)} %copy-done.122, bf16[4,256,512]{2,1,0:T(8,128)(2,1)} %bitcast.22.refs_0_, ...), custom_call_target="tpu_custom_call" | custom-call | flops 14000000000 | bytes 14000000 | tf_op jit(solution)/shard_map/pallas_call | solution.py:744
  441.5 12.9 %shard_map.381 = (bf16[768,512]{1,0:T(8,128)(2,1)S(1)}, bf16[256,1024]{1,0:T(8,128)(2,1)S(1)}, bf16[1024,1024]{1,0:T(8,128)(2,1)}, f32[1,512]{1,0:T(1,128)S(1)}, f32[1,1024]{1,0:T(1,128)S(1)}) custom-call(s32[8]{0:T(128)S(1)} %concatenate.330.place, bf16[768,512]{1,0:T(8,128)(2,1)S(1)} %copy-done.146, bf16[256,1024]{1,0:T(8,128)(2,1)S(1)} %copy-done.148, ...), custom_call_target="tpu_custom_call" | custom-call | flops 14000000000 | bytes 14000000 | tf_op jit(solution)/shard_map/pallas_call | solution.py:744
  517.2 15.6 %collective-permute-done.42 = bf16[4,256,512]{2,1,0:T(8,128)(2,1)} collective-permute-done((bf16[4,256,512]{2,1,0:T(8,128)(2,1)}, bf16[4,256,512]{2,1,0:T(8,128)(2,1)}, u32[]{:S(2)}, u32[]{:S(2)}) %collective-permute-start.42) | collective-permute-done | bytes 1048608 | tf_op jit(solution)/shard_map/ppermute | solution.py:143
  553.7 24.8 %shard_map.389 = (bf16[768,1536]{1,0:T(8,128)(2,1)S(1)}, bf16[768,256]{1,0:T(8,128)(2,1)S(1)}, f32[384,1024]{1,0:T(8,128)S(1)}, bf16[384,1024]{1,0:T(8,128)(2,1)...) custom-call(s32[8]{0:T(128)S(1)} %concatenate.330.place, bf16[768,1536]{1,0:T(8,128)(2,1)S(1)} %copy-done.138, ...), custom_call_target="tpu_custom_call" | custom-call | flops 28999999488 | bytes 29000000 | tf_op jit(solution)/shard_map/pallas_call | solution.py:744
  578.6 9.6 %collective-permute-done.47 = bf16[4,128,1024]{2,1,0:T(8,128)(2,1)} collective-permute-done((bf16[4,128,1024]{2,1,0:T(8,128)(2,1)}, bf16[4,128,1024]{2,1,0:T(8,128)(2,1)}, u32[]{:S(2)}, u32[]{:S(2)}) %collective-permute-start.47) | collective-permute-done | bytes 1048608 | tf_op jit(solution)/shard_map/ppermute | solution.py:143
  603.3 11.0 %shard_map.390 = (bf16[256,1536]{1,0:T(8,128)(2,1)S(1)}, f32[128,1024]{1,0:T(8,128)S(1)}, bf16[128,1024]{1,0:T(8,128)(2,1)S(1)}, f32[1,1536]{1,0:T(1,128)S(1)}) custom-call(s32[8]{0:T(128)S(1)} %concatenate.330.place, bf16[256,1536]{1,0:T(8,128)(2,1)S(1)} %copy-done.136, bf16[256,256]{1,0:T(8,128)(2,1)S(1)} %copy-done.128, ...), custom_call_target="tpu_custom_call" | custom-call | flops 12999999488 | bytes 13000000 | tf_op jit(solution)/shard_map/pallas_call | solution.py:744
  650.6 19.9 %collective-permute-done.58 = bf16[4,288,512]{2,1,0:T(8,128)(2,1)} collective-permute-done((bf16[4,288,512]{2,1,0:T(8,128)(2,1)}, bf16[4,288,512]{2,1,0:T(8,128)(2,1)}, u32[]{:S(2)}, u32[]{:S(2)}) %collective-permute-start.58) | collective-permute-done | bytes 1179680 | tf_op jit(solution)/shard_map/ppermute | solution.py:143
  678.0 11.8 %collective-permute-done.60 = bf16[4,288,512]{2,1,0:T(8,128)(2,1)} collective-permute-done((bf16[4,288,512]{2,1,0:T(8,128)(2,1)}, bf16[4,288,512]{2,1,0:T(8,128)(2,1)}, u32[]{:S(2)}, u32[]{:S(2)}) %collective-permute-start.60) | collective-permute-done | bytes 1179680 | tf_op jit(solution)/shard_map/ppermute | solution.py:143
  710.7 16.3 %collective-permute-done.63 = bf16[4,272,512]{2,1,0:T(8,128)(2,1)} collective-permute-done((bf16[4,272,512]{2,1,0:T(8,128)(2,1)S(1)}, bf16[4,272,512]{2,1,0:T(8,128)(2,1)}, u32[]{:S(2)}, u32[]{:S(2)}) %collective-permute-start.63) | collective-permute-done | bytes 1114144 | tf_op jit(solution)/shard_map/ppermute | solution.py:143
  746.1 14.6 %reduce-scatter.8.cloned.1.call-done = bf16[1,272,512]{2,1,0:T(8,128)(2,1)} async-done(((bf16[4,272,512]{2,1,0:T(8,128)(2,1)}), bf16[1,272,512]{2,1,0:T(8,128)(2,1)}) %reduce-scatter.8.cloned.1.call-update) | async-done | bytes 278544 | tf_op jit(solution)/shard_map/reduce_scatter | solution.py:1840
  (784 shorter events, 357.5 us)
Async XLA Ops:
  7.9 61.4 %all-gather.19.cloned.1.call-start = ((), (), s32[]{:S(2)}) async-start(), calls=%async_computation.16 | async-start | bytes 1310720 | tf_op jit(solution)/shard_map/all_gather | solution.py:1796
  18.6 83.9 %all-gather.17.cloned.1.call-start = ((), (), s32[]{:S(2)}) async-start(), calls=%async_computation.15 | async-start | bytes 1556480 | tf_op jit(solution)/shard_map/all_gather | solution.py:1796
  40.2 91.3 %all-gather.21.cloned.1.call-start = ((), (), s32[]{:S(2)}) async-start(), calls=%async_computation.17 | async-start | bytes 1310720 | tf_op jit(solution)/shard_map/all_gather | solution.py:1796
  69.3 103.6 %all-gather.25.cloned.1.call-start = ((), (), s32[]{:S(2)}) async-start(), calls=%async_computation.19 | async-start | bytes 1310720 | tf_op jit(solution)/shard_map/all_gather | solution.py:1796
  102.6 111.7 %all-gather.23.cloned.1.call-start = ((), (), s32[]{:S(2)}) async-start(), calls=%async_computation.18 | async-start | bytes 1310720 | tf_op jit(solution)/shard_map/all_gather | solution.py:1796
  131.6 106.7 %all-gather.27.cloned.1.call-start = ((), (), s32[]{:S(2)}) async-start(), calls=%async_computation.20 | async-start | bytes 1310720 | tf_op jit(solution)/shard_map/all_gather | solution.py:1796
  132.5 76.3 %collective-permute-start.12 = (bf16[4,304,512]{2,1,0:T(8,128)(2,1)}, bf16[4,304,512]{2,1,0:T(8,128)(2,1)}, u32[]{:S(2)}, u32[]{:S(2)}) collective-permute-start(bf16[4,304,512]{2,1,0:T(8,128)(2,1)} %collective-permute-done.11.refs_2_.refs_6_), channel_id=1, source_target_pairs={{0,8},{8,0},{16,24},{24,16},{1,9},{9,1},{17,25},{25,17},{2,10},{10... | collective-permute-start | bytes 3735560 | tf_op jit(solution)/shard_map/ppermute | solution.py:143
  134.3 71.0 %collective-permute-start.16 = (bf16[4,128,1024]{2,1,0:T(8,128)(2,1)}, bf16[4,128,1024]{2,1,0:T(8,128)(2,1)}, u32[]{:S(2)}, u32[]{:S(2)}) collective-permute-start(bf16[4,128,1024]{2,1,0:T(8,128)(2,1)} %collective-permute-done.8.refs_5_), channel_id=1, source_target_pairs={{0,16},{8,24},{16,0},{24,8},{1,17},{9,25},{17,1},{25,9},{2,18},{10... | collective-permute-start | bytes 3145736 | tf_op jit(solution)/shard_map/ppermute | solution.py:143
  173.0 525.6 %reduce-scatter.18.cloned.1.call-start = ((), (), s32[]{:S(2)}) async-start(), calls=%async_computation.12 | async-start | bytes 1310720 | tf_op jit(solution)/shard_map/reduce_scatter | solution.py:1840
  267.8 53.5 %collective-permute-start.28 = (bf16[4,256,512]{2,1,0:T(8,128)(2,1)}, bf16[4,256,512]{2,1,0:T(8,128)(2,1)}, u32[]{:S(2)}, u32[]{:S(2)}) collective-permute-start(bf16[4,256,512]{2,1,0:T(8,128)(2,1)} %collective-permute-done.18.refs_2_), channel_id=1, source_target_pairs={{0,8},{8,0},{16,24},{24,16},{1,9},{9,1},{17,25},{25,17},{2,10},{10... | collective-permute-start | bytes 3145736 | tf_op jit(solution)/shard_map/ppermute | solution.py:143
  284.6 56.6 %collective-permute-start.30 = (bf16[768,1024]{1,0:T(8,128)(2,1)}, bf16[768,1024]{1,0:T(8,128)(2,1)S(1)}, u32[]{:S(2)}, u32[]{:S(2)}) collective-permute-start(bf16[768,1024]{1,0:T(8,128)(2,1)} %copy-done.27), channel_id=1, source_target_pairs={{0,1},{1,0},{2,3},{3,2},{4,5},{5,4},{6,7},{7,6},{8,9},{9,8},{10,11... | collective-permute-start | bytes 4718600 | tf_op jit(solution)/shard_map/ppermute | solution.py:135
  456.3 59.2 %collective-permute-start.41 = (bf16[4,128,1024]{2,1,0:T(8,128)(2,1)}, bf16[4,128,1024]{2,1,0:T(8,128)(2,1)S(1)}, u32[]{:S(2)}, u32[]{:S(2)}) collective-permute-start(bf16[4,128,1024]{2,1,0:T(8,128)(2,1)} %copy-done.64), channel_id=1, source_target_pairs={{0,16},{8,24},{16,0},{24,8},{1,17},{9,25},{17,1},{25,9},{2,18},{10... | collective-permute-start | bytes 3145736 | tf_op jit(solution)/shard_map/ppermute | solution.py:143
  457.7 77.7 %collective-permute-start.43 = (bf16[4,256,512]{2,1,0:T(8,128)(2,1)}, bf16[4,256,512]{2,1,0:T(8,128)(2,1)}, u32[]{:S(2)}, u32[]{:S(2)}) collective-permute-start(bf16[4,256,512]{2,1,0:T(8,128)(2,1)} %copy-done.65), channel_id=1, source_target_pairs={{0,8},{8,0},{16,24},{24,16},{1,9},{9,1},{17,25},{25,17},{2,10},{10... | collective-permute-start | bytes 3145736 | tf_op jit(solution)/shard_map/ppermute | solution.py:143
  471.7 63.7 %collective-permute-start.44 = (bf16[4,256,512]{2,1,0:T(8,128)(2,1)}, bf16[4,256,512]{2,1,0:T(8,128)(2,1)}, u32[]{:S(2)}, u32[]{:S(2)}) collective-permute-start(bf16[4,256,512]{2,1,0:T(8,128)(2,1)} %add_convert_fusion.12), channel_id=1, source_target_pairs={{0,16},{8,24},{16,0},{24,8},{1,17},{9,25},{17,1},{25,9},{2,18},{10... | collective-permute-start | bytes 3145736 | tf_op jit(solution)/shard_map/ppermute | solution.py:143
  480.7 52.1 %collective-permute-start.42 = (bf16[4,256,512]{2,1,0:T(8,128)(2,1)}, bf16[4,256,512]{2,1,0:T(8,128)(2,1)}, u32[]{:S(2)}, u32[]{:S(2)}) collective-permute-start(bf16[4,256,512]{2,1,0:T(8,128)(2,1)} %get-tuple-element.287), channel_id=1, source_target_pairs={{0,16},{8,24},{16,0},{24,8},{1,17},{9,25},{17,1},{25,9},{2,18},{10... | collective-permute-start | bytes 3145736 | tf_op jit(solution)/shard_map/ppermute | solution.py:143
  538.4 165.2 %reduce-scatter.20.cloned.1.call-start = ((), (), s32[]{:S(2)}) async-start(), calls=%async_computation.13 | async-start | bytes 1310720 | tf_op jit(solution)/shard_map/reduce_scatter | solution.py:1840
  538.6 55.0 %collective-permute-start.50 = (bf16[4,256,512]{2,1,0:T(8,128)(2,1)}, bf16[4,256,512]{2,1,0:T(8,128)(2,1)}, u32[]{:S(2)}, u32[]{:S(2)}) collective-permute-start(bf16[4,256,512]{2,1,0:T(8,128)(2,1)} %copy-done.63), channel_id=1, source_target_pairs={{0,16},{8,24},{16,0},{24,8},{1,17},{9,25},{17,1},{25,9},{2,18},{10... | collective-permute-start | bytes 3145736 | tf_op jit(solution)/shard_map/ppermute | solution.py:143
  539.3 54.9 %collective-permute-start.49 = (bf16[4,256,512]{2,1,0:T(8,128)(2,1)}, bf16[4,256,512]{2,1,0:T(8,128)(2,1)}, u32[]{:S(2)}, u32[]{:S(2)}) collective-permute-start(bf16[4,256,512]{2,1,0:T(8,128)(2,1)} %add_convert_fusion.10), channel_id=1, source_target_pairs={{0,8},{8,0},{16,24},{24,16},{1,9},{9,1},{17,25},{25,17},{2,10},{10... | collective-permute-start | bytes 3145736 | tf_op jit(solution)/shard_map/ppermute | solution.py:143
  542.1 165.6 %reduce-scatter.16.cloned.1.call-start = ((), (), s32[]{:S(2)}) async-start(), calls=%async_computation.11 | async-start | bytes 1310720 | tf_op jit(solution)/shard_map/reduce_scatter | solution.py:1840
  552.7 73.6 %collective-permute-start.54 = (bf16[4,128,1024]{2,1,0:T(8,128)(2,1)}, bf16[4,128,1024]{2,1,0:T(8,128)(2,1)}, u32[]{:S(2)}, u32[]{:S(2)}) collective-permute-start(bf16[4,128,1024]{2,1,0:T(8,128)(2,1)} %get-tuple-element.322), channel_id=1, source_target_pairs={{0,8},{8,0},{16,24},{24,16},{1,9},{9,1},{17,25},{25,17},{2,10},{10... | collective-permute-start | bytes 3145736 | tf_op jit(solution)/shard_map/ppermute | solution.py:143
  597.7 135.9 %reduce-scatter.10.cloned.1.call-start = ((), (), s32[]{:S(2)}) async-start(), calls=%async_computation.8 | async-start | bytes 1310720 | tf_op jit(solution)/shard_map/reduce_scatter | solution.py:1840
  638.3 98.2 %reduce-scatter.12.cloned.1.call-start = ((), (), s32[]{:S(2)}) async-start(), calls=%async_computation.9 | async-start | bytes 1310720 | tf_op jit(solution)/shard_map/reduce_scatter | solution.py:1840
  643.6 97.0 %reduce-scatter.14.cloned.1.call-start = ((), (), s32[]{:S(2)}) async-start(), calls=%async_computation.10 | async-start | bytes 1474560 | tf_op jit(solution)/shard_map/reduce_scatter | solution.py:1840
  698.3 62.4 %reduce-scatter.8.cloned.1.call-start = ((), (), s32[]{:S(2)}) async-start(), calls=%async_computation.7 | async-start | bytes 1392640 | tf_op jit(solution)/shard_map/reduce_scatter | solution.py:1840
  (236 other events, 2785.4 us)
Sparse Core Ops, SparseCore 0:
  9.6 30.5 all-gather.14
  41.8 27.4 all-gather.18
  71.4 31.0 all-gather.16
  104.5 26.9 all-gather.20
  133.5 27.4 all-gather.24
  163.0 27.4 all-gather.22
  192.6 27.4 all-gather.26
  538.5 28.0 reduce-scatter.17
  569.0 25.7 reduce-scatter.19
  597.8 28.9 reduce-scatter.15
  638.4 29.0 reduce-scatter.9
  669.6 25.7 reduce-scatter.11
  698.4 30.9 reduce-scatter.13
  731.7 28.9 reduce-scatter.7
